TPU v7x, 32 devices: a whole 2x2x4 slice. The times are simulated.
32 devices in a mesh: heads: 4 (over y, x), ctx: 8 (over z, core).
Axes of the slice: x: 2, y: 2, z: 4, core: 2. Of those that a mesh axis runs over, the one named last changes fastest.
Arguments:
- queries: bfloat16 [3072, 8192], P('ctx', 'heads'), may hold values from -20 to 20
- keys: bfloat16 [3072, 1024], P('ctx', 'heads'), may hold values from -20 to 20
- values: bfloat16 [3072, 1024], P('ctx', 'heads'), may hold values from -6 to 6
- positions: int32 [3072], P('ctx'), may hold values from 0 to 4607, as said below
Outputs:
- attended: bfloat16 [3072, 8192], P(('ctx', 'heads'))
Inputs may be any that keep to these rules, and one draw needn't show every extreme that they name: `positions`: positions start at 0 at the first token and rise by 1 or 2 from each token to the next; exactly 1536 of these steps rise by 2.
All inputs are finite; a program needn't handle non-finite values.
Results may differ from a plain program's by a relative error of at most 0.0092.
Values may be sent and summed in bfloat16 or wider, within the bound.
No kernel may reach another device: no remote copies, remote signals or barrier semaphores. Data moves between devices by JAX's collectives and lax.ppermute only.
A program may use at most 64 MiB of HBM per device.

v0:
```python
import math

import jax
import jax.numpy as jnp
from jax import lax
from jax.sharding import PartitionSpec as P

HD = 128


NEG_FILL = -1e30


def rotary_tables(positions, head_dim):
    step_index = jnp.arange(head_dim // 2, dtype=jnp.float32)
    base_freq = jnp.power(jnp.float32(500000.0), -(2.0 * step_index / head_dim))
    wavelen = 2.0 * math.pi / base_freq
    blend_factor = (8192.0 / wavelen - 1.0) / 3.0
    middle = (1.0 - blend_factor) * base_freq / 8.0 + blend_factor * base_freq
    inv_freq = jnp.where(
        wavelen < 2048.0, base_freq, jnp.where(wavelen > 8192.0, base_freq / 8.0, middle)
    )
    angles = positions.astype(jnp.float32)[:, None] * inv_freq[None, :]
    return (jnp.cos(angles), jnp.sin(angles))


def rotate(head_data, cosine, sine_table):
    halfway = head_data.shape[-1] // 2
    first_part = head_data[..., :halfway]
    second = head_data[..., halfway:]
    cos_rows = cosine[:, None, :]
    sin_rows = sine_table[:, None, :]
    return jnp.concatenate(
        [first_part * cos_rows - second * sin_rows, second * cos_rows + first_part * sin_rows],
        axis=-1,
    )


def attend_piece(
    carry_now, queries_part, query_rows, keys_part, values_part, key_start, scale_value
):
    rows_count = queries_part.shape[0]
    keys_count = keys_part.shape[0]

    def update(state_now):
        prev_max, prev_sum, prev_acc = state_now
        scores = (
            jnp.einsum(
                "qhgd,khd->hgqk", queries_part, keys_part, preferred_element_type=jnp.float32
            )
            * scale_value
        )
        query_index = jnp.broadcast_to(query_rows[:, None], (rows_count, keys_count))
        key_index = key_start + lax.broadcasted_iota(jnp.int32, (rows_count, keys_count), 1)
        allowed = key_index <= query_index
        scores = jnp.where(allowed, scores, NEG_FILL)
        new_max = jnp.maximum(prev_max, jnp.max(scores, axis=-1))
        weights = jnp.where(allowed, jnp.exp(scores - new_max[..., None]), 0.0)
        factor = jnp.exp(prev_max - new_max)
        new_sum = prev_sum * factor + jnp.sum(weights, axis=-1)
        mixed_values = jnp.einsum(
            "hgqk,khd->hgqd",
            weights.astype(jnp.bfloat16),
            values_part,
            preferred_element_type=jnp.float32,
        )
        return (new_max, new_sum, prev_acc * factor[..., None] + mixed_values)

    return lax.cond(
        key_start <= jnp.max(query_rows), update, lambda state_now: state_now, carry_now
    )


def local(queries, keys, values, positions):
    tok_rows = queries.shape[0]
    kv_local = keys.shape[1] // HD
    group_size = queries.shape[1] // (kv_local * HD)
    halfway = tok_rows // 2
    ctx_rank = lax.axis_index("ctx")
    scale_value = 1.0 / math.sqrt(HD)
    cosine, sine_table = rotary_tables(positions, HD)
    rot_queries = rotate(
        queries.astype(jnp.float32).reshape(tok_rows, kv_local * group_size, HD), cosine, sine_table
    )
    rot_queries = rot_queries.astype(jnp.bfloat16).reshape(tok_rows, kv_local, group_size, HD)
    rot_keys = rotate(
        keys.astype(jnp.float32).reshape(tok_rows, kv_local, HD), cosine, sine_table
    ).astype(jnp.bfloat16)
    flat_keys = rot_keys.reshape(tok_rows, kv_local * HD)
    half_iota = jnp.arange(halfway, dtype=jnp.int32)
    first_queries = rot_queries[:halfway]
    second_queries = rot_queries[halfway:]
    first_rows = ctx_rank * tok_rows + half_iota
    second_rows = ctx_rank * tok_rows + halfway + half_iota

    def fresh_state():
        return (
            jnp.full((kv_local, group_size, halfway), NEG_FILL, jnp.float32),
            jnp.zeros((kv_local, group_size, halfway), jnp.float32),
            jnp.zeros((kv_local, group_size, halfway, HD), jnp.float32),
        )

    pieces = (
        lax.all_gather(flat_keys, "ctx", axis=0, tiled=True),
        lax.all_gather(values, "ctx", axis=0, tiled=True),
    )
    piece_rows = pieces[0].shape[0]
    block_rows = math.gcd(piece_rows, 512)

    def one_block(block_index, inner_carry):
        offset = block_index * block_rows
        key_block = lax.dynamic_slice_in_dim(pieces[0], offset, block_rows, 0).reshape(
            block_rows, kv_local, HD
        )
        value_block = lax.dynamic_slice_in_dim(pieces[1], offset, block_rows, 0).reshape(
            block_rows, kv_local, HD
        )
        first_state = attend_piece(
            inner_carry[0], first_queries, first_rows, key_block, value_block, offset, scale_value
        )
        second_state = attend_piece(
            inner_carry[1], second_queries, second_rows, key_block, value_block, offset, scale_value
        )
        return (first_state, second_state)

    states = lax.fori_loop(0, piece_rows // block_rows, one_block, (fresh_state(), fresh_state()))

    def finish(state_now):
        run_acc = state_now[2] / state_now[1][..., None]
        return (
            jnp.transpose(run_acc, (2, 0, 1, 3))
            .reshape(halfway, kv_local * group_size * HD)
            .astype(jnp.bfloat16)
        )

    first_out = finish(states[0])
    second_out = finish(states[1])
    combined = jnp.concatenate([first_out, second_out], axis=0)
    return lax.all_to_all(combined, "heads", split_axis=0, concat_axis=1, tiled=True)


def solution(mesh):
    return jax.shard_map(
        local,
        mesh=mesh,
        in_specs=(P("ctx", "heads"), P("ctx", "heads"), P("ctx", "heads"), P("ctx")),
        out_specs=P(("ctx", "heads"), None),
        check_vma=False,
    )
```

profile of v0, /device:TPU:25, one launch (start us, length us, event | category | flops | bytes accessed | tf_op | source)
XLA Modules:
  0.0 193.7 jit_solution(5453217863897771846)
XLA Ops:
  6.6 1.2 copy.60
  9.7 1.8 copy.40
  14.5 2.0 %add_convert_fusion = (bf16[384,16,64]{2,0,1:T(8,128)(2,1)S(1)}, bf16[384,16,64]{2,0,1:T(8,128)(2,1)S(1)}) fusion(f32[384,16,64]{2,1,0:T(8,128)S(1)} %get-tuple-element.511, f32[384,16,64]{2,1,0:T(8,128)S(1)} %get-tuple-element.510, f32[384,64]{1,0:T(8,128)S(1)} %copy.44, f32[384,64]{1,0:T(8,128)S(1)} %copy.42), kind=kLoop, calls=%fused_computation.43 | loop fusion | flops 3145728 | bytes 4915200 | tf_op jit(solution)/shard_map/convert.3
  17.4 17.2 %all-gather.3.cloned.1.call-done = bf16[3072,256]{0,1:T(8,128)(2,1)} async-done(((bf16[384,256]{0,1:T(8,128)(2,1)}), bf16[3072,256]{0,1:T(8,128)(2,1)}) %all-gather.3.cloned.1.call-update) | async-done | bytes 1572880 | tf_op jit(solution)/shard_map/all_gather | solution.py:104
  34.7 26.0 %all-gather.5.cloned.1.call-done = bf16[3072,256]{0,1:T(8,128)(2,1)} async-done(((bf16[384,256]{0,1:T(8,128)(2,1)}), bf16[3072,256]{0,1:T(8,128)(2,1)}) %all-gather.5.cloned.1.call-update) | async-done | bytes 1572880 | tf_op jit(solution)/shard_map/all_gather | solution.py:105
  60.7 1.3 broadcast.127
  62.0 1.3 broadcast.127.clone
  63.3 101.2 %while.25 = (s32[]{:T(128)}, f32[2,8,192]{2,1,0:T(8,128)S(1)}, f32[2,8,192]{2,1,0:T(8,128)S(1)}, f32[2,8,192,128]{3,2,1,0:T(8,128)}, f32[2,8,192]{2,1,0:T(8,128)...) while((s32[]{:T(128)}, f32[2,8,192]{2,1,0:T(8,128)S(1)}, ...), condition=%wide.region_11.12_spmd.clone, body=%wide.region_2.11_spmd.clone.sunk | while | flops 1653290368 | bytes 74070656 | solution.py:126
  65.1 7.2 %conditional.6 = ((f32[2,8,192]{2,1,0:T(8,128)S(1)}, f32[2,8,192]{2,1,0:T(8,128)S(1)}, f32[2,8,192,128]{3,2,1,0:T(8,128)})) conditional(s32[]{:T(128)} %convert_element_type.77, (f32[2,8,192]{2,1,0:T(8,128)S(1)}, f32[2,8,192]{2,1,0:T(8,128)S(1)}, f32[2,8,192,128]{3,2,1,0:T(8,128)}) %tuple.76, (s32[]{:T(128)}, s32[]{:T(128)}, ...), branch_computations={%region_3.3_spmd, %region_4.6_spmd} | conditional | flops 826645184 | bytes 36510048 | solution.py:69
  65.2 1.3 fusion.4
  66.6 2.1 %fusion.6 = f32[2,8,192]{2,1,0:T(8,128)S(1)} fusion(f32[2,512,192,8]{1,2,3,0:T(8,128)S(1)} %get-tuple-element.501, f32[2,8,192]{2,1,0:T(8,128)S(1)} %max.4, pred[192,512]{1,0:T(8,128)(4,1)S(1)} %broadcast_compare_fusion), kind=kLoop, calls=%fused_computation.6 | loop fusion | flops 7861248 | bytes 6414336 | tf_op jit(solution)/shard_map/while/body/eval_jaxpr/cond/branch_1_fun/reduce_sum | solution.py:60
  68.7 2.5 %multiply_add_fusion = f32[2,8,192,128]{3,2,1,0:T(8,128)S(1)} fusion(f32[2,8,192,128]{3,2,1,0:T(8,128)S(1)} %copy-done, f32[2,512,192,8]{1,2,3,0:T(8,128)S(1)} %get-tuple-element.501, f32[2,8,192]{2,1,0:T(8,128)S(1)} %max.4, pred[192,512]{1,0:T(8,128)(4,1)S(1)} %broadcast_compare_fusion, f32[2,8,192]{2,1,0:T(8,128)S(1)} %get-tuple-element.497, ...), kind=kOutput, calls=%fused_computation.9 | convolution fusion | flops 411303936 | bytes 9822208 | tf_op jit(solution)/shard_map/while/body/eval_jaxpr/cond/branch_1_fun/hgqk,khd->hgqd/dot_general | solution.py:61
  73.0 7.2 %conditional.7 = ((f32[2,8,192]{2,1,0:T(8,128)S(1)}, f32[2,8,192]{2,1,0:T(8,128)S(1)}, f32[2,8,192,128]{3,2,1,0:T(8,128)})) conditional(s32[]{:T(128)} %convert_element_type.78, (f32[2,8,192]{2,1,0:T(8,128)S(1)}, f32[2,8,192]{2,1,0:T(8,128)S(1)}, f32[2,8,192,128]{3,2,1,0:T(8,128)}) %tuple.78, (s32[]{:T(128)}, s32[]{:T(128)}, ...), branch_computations={%region_7.7_spmd, %region_8.10_spmd} | conditional | flops 826645184 | bytes 36510048 | solution.py:69
  73.1 1.3 fusion.18
  74.5 2.1 %fusion.20 = f32[2,8,192]{2,1,0:T(8,128)S(1)} fusion(f32[2,512,192,8]{1,2,3,0:T(8,128)S(1)} %get-tuple-element.503, f32[2,8,192]{2,1,0:T(8,128)S(1)} %max.5, pred[192,512]{1,0:T(8,128)(4,1)S(1)} %broadcast_compare_fusion.1), kind=kLoop, calls=%fused_computation.25 | loop fusion | flops 7861248 | bytes 6414336 | tf_op jit(solution)/shard_map/while/body/eval_jaxpr/cond/branch_1_fun/reduce_sum | solution.py:60
  76.6 2.5 %multiply_add_fusion.2 = f32[2,8,192,128]{3,2,1,0:T(8,128)S(1)} fusion(f32[2,8,192,128]{3,2,1,0:T(8,128)S(1)} %copy-done.3, f32[2,512,192,8]{1,2,3,0:T(8,128)S(1)} %get-tuple-element.503, f32[2,8,192]{2,1,0:T(8,128)S(1)} %max.5, pred[192,512]{1,0:T(8,128)(4,1)S(1)} %broadcast_compare_fusion.1, f32[2,8,192]{2,1,0:T(8,128)S(1)} %get-tuple-element.499, ...), kind=kOutput, calls=%fused_computation.28 | convolution fusion | flops 411303936 | bytes 9822208 | tf_op jit(solution)/shard_map/while/body/eval_jaxpr/cond/branch_1_fun/hgqk,khd->hgqd/dot_general | solution.py:61
  79.1 1.1 copy-done.4
  81.9 7.3 %conditional.6 = ((f32[2,8,192]{2,1,0:T(8,128)S(1)}, f32[2,8,192]{2,1,0:T(8,128)S(1)}, f32[2,8,192,128]{3,2,1,0:T(8,128)})) conditional(s32[]{:T(128)} %convert_element_type.77, (f32[2,8,192]{2,1,0:T(8,128)S(1)}, f32[2,8,192]{2,1,0:T(8,128)S(1)}, f32[2,8,192,128]{3,2,1,0:T(8,128)}) %tuple.76, (s32[]{:T(128)}, s32[]{:T(128)}, ...), branch_computations={%region_3.3_spmd, %region_4.6_spmd} | conditional | flops 826645184 | bytes 36510048 | solution.py:69
  82.1 1.3 fusion.4
  83.4 2.1 %fusion.6 = f32[2,8,192]{2,1,0:T(8,128)S(1)} fusion(f32[2,512,192,8]{1,2,3,0:T(8,128)S(1)} %get-tuple-element.501, f32[2,8,192]{2,1,0:T(8,128)S(1)} %max.4, pred[192,512]{1,0:T(8,128)(4,1)S(1)} %broadcast_compare_fusion), kind=kLoop, calls=%fused_computation.6 | loop fusion | flops 7861248 | bytes 6414336 | tf_op jit(solution)/shard_map/while/body/eval_jaxpr/cond/branch_1_fun/reduce_sum | solution.py:60
  85.6 2.5 %multiply_add_fusion = f32[2,8,192,128]{3,2,1,0:T(8,128)S(1)} fusion(f32[2,8,192,128]{3,2,1,0:T(8,128)S(1)} %copy-done, f32[2,512,192,8]{1,2,3,0:T(8,128)S(1)} %get-tuple-element.501, f32[2,8,192]{2,1,0:T(8,128)S(1)} %max.4, pred[192,512]{1,0:T(8,128)(4,1)S(1)} %broadcast_compare_fusion, f32[2,8,192]{2,1,0:T(8,128)S(1)} %get-tuple-element.497, ...), kind=kOutput, calls=%fused_computation.9 | convolution fusion | flops 411303936 | bytes 9822208 | tf_op jit(solution)/shard_map/while/body/eval_jaxpr/cond/branch_1_fun/hgqk,khd->hgqd/dot_general | solution.py:61
  89.8 7.2 %conditional.7 = ((f32[2,8,192]{2,1,0:T(8,128)S(1)}, f32[2,8,192]{2,1,0:T(8,128)S(1)}, f32[2,8,192,128]{3,2,1,0:T(8,128)})) conditional(s32[]{:T(128)} %convert_element_type.78, (f32[2,8,192]{2,1,0:T(8,128)S(1)}, f32[2,8,192]{2,1,0:T(8,128)S(1)}, f32[2,8,192,128]{3,2,1,0:T(8,128)}) %tuple.78, (s32[]{:T(128)}, s32[]{:T(128)}, ...), branch_computations={%region_7.7_spmd, %region_8.10_spmd} | conditional | flops 826645184 | bytes 36510048 | solution.py:69
  90.0 1.3 fusion.18
  91.3 2.1 %fusion.20 = f32[2,8,192]{2,1,0:T(8,128)S(1)} fusion(f32[2,512,192,8]{1,2,3,0:T(8,128)S(1)} %get-tuple-element.503, f32[2,8,192]{2,1,0:T(8,128)S(1)} %max.5, pred[192,512]{1,0:T(8,128)(4,1)S(1)} %broadcast_compare_fusion.1), kind=kLoop, calls=%fused_computation.25 | loop fusion | flops 7861248 | bytes 6414336 | tf_op jit(solution)/shard_map/while/body/eval_jaxpr/cond/branch_1_fun/reduce_sum | solution.py:60
  93.5 2.5 %multiply_add_fusion.2 = f32[2,8,192,128]{3,2,1,0:T(8,128)S(1)} fusion(f32[2,8,192,128]{3,2,1,0:T(8,128)S(1)} %copy-done.3, f32[2,512,192,8]{1,2,3,0:T(8,128)S(1)} %get-tuple-element.503, f32[2,8,192]{2,1,0:T(8,128)S(1)} %max.5, pred[192,512]{1,0:T(8,128)(4,1)S(1)} %broadcast_compare_fusion.1, f32[2,8,192]{2,1,0:T(8,128)S(1)} %get-tuple-element.499, ...), kind=kOutput, calls=%fused_computation.28 | convolution fusion | flops 411303936 | bytes 9822208 | tf_op jit(solution)/shard_map/while/body/eval_jaxpr/cond/branch_1_fun/hgqk,khd->hgqd/dot_general | solution.py:61
  95.9 1.1 copy-done.4
  98.8 7.3 %conditional.6 = ((f32[2,8,192]{2,1,0:T(8,128)S(1)}, f32[2,8,192]{2,1,0:T(8,128)S(1)}, f32[2,8,192,128]{3,2,1,0:T(8,128)})) conditional(s32[]{:T(128)} %convert_element_type.77, (f32[2,8,192]{2,1,0:T(8,128)S(1)}, f32[2,8,192]{2,1,0:T(8,128)S(1)}, f32[2,8,192,128]{3,2,1,0:T(8,128)}) %tuple.76, (s32[]{:T(128)}, s32[]{:T(128)}, ...), branch_computations={%region_3.3_spmd, %region_4.6_spmd} | conditional | flops 826645184 | bytes 36510048 | solution.py:69
  98.9 1.3 fusion.4
  100.3 2.1 %fusion.6 = f32[2,8,192]{2,1,0:T(8,128)S(1)} fusion(f32[2,512,192,8]{1,2,3,0:T(8,128)S(1)} %get-tuple-element.501, f32[2,8,192]{2,1,0:T(8,128)S(1)} %max.4, pred[192,512]{1,0:T(8,128)(4,1)S(1)} %broadcast_compare_fusion), kind=kLoop, calls=%fused_computation.6 | loop fusion | flops 7861248 | bytes 6414336 | tf_op jit(solution)/shard_map/while/body/eval_jaxpr/cond/branch_1_fun/reduce_sum | solution.py:60
  102.4 2.5 %multiply_add_fusion = f32[2,8,192,128]{3,2,1,0:T(8,128)S(1)} fusion(f32[2,8,192,128]{3,2,1,0:T(8,128)S(1)} %copy-done, f32[2,512,192,8]{1,2,3,0:T(8,128)S(1)} %get-tuple-element.501, f32[2,8,192]{2,1,0:T(8,128)S(1)} %max.4, pred[192,512]{1,0:T(8,128)(4,1)S(1)} %broadcast_compare_fusion, f32[2,8,192]{2,1,0:T(8,128)S(1)} %get-tuple-element.497, ...), kind=kOutput, calls=%fused_computation.9 | convolution fusion | flops 411303936 | bytes 9822208 | tf_op jit(solution)/shard_map/while/body/eval_jaxpr/cond/branch_1_fun/hgqk,khd->hgqd/dot_general | solution.py:61
  106.7 7.3 %conditional.7 = ((f32[2,8,192]{2,1,0:T(8,128)S(1)}, f32[2,8,192]{2,1,0:T(8,128)S(1)}, f32[2,8,192,128]{3,2,1,0:T(8,128)})) conditional(s32[]{:T(128)} %convert_element_type.78, (f32[2,8,192]{2,1,0:T(8,128)S(1)}, f32[2,8,192]{2,1,0:T(8,128)S(1)}, f32[2,8,192,128]{3,2,1,0:T(8,128)}) %tuple.78, (s32[]{:T(128)}, s32[]{:T(128)}, ...), branch_computations={%region_7.7_spmd, %region_8.10_spmd} | conditional | flops 826645184 | bytes 36510048 | solution.py:69
  106.9 1.3 fusion.18
  108.2 2.1 %fusion.20 = f32[2,8,192]{2,1,0:T(8,128)S(1)} fusion(f32[2,512,192,8]{1,2,3,0:T(8,128)S(1)} %get-tuple-element.503, f32[2,8,192]{2,1,0:T(8,128)S(1)} %max.5, pred[192,512]{1,0:T(8,128)(4,1)S(1)} %broadcast_compare_fusion.1), kind=kLoop, calls=%fused_computation.25 | loop fusion | flops 7861248 | bytes 6414336 | tf_op jit(solution)/shard_map/while/body/eval_jaxpr/cond/branch_1_fun/reduce_sum | solution.py:60
  110.3 2.5 %multiply_add_fusion.2 = f32[2,8,192,128]{3,2,1,0:T(8,128)S(1)} fusion(f32[2,8,192,128]{3,2,1,0:T(8,128)S(1)} %copy-done.3, f32[2,512,192,8]{1,2,3,0:T(8,128)S(1)} %get-tuple-element.503, f32[2,8,192]{2,1,0:T(8,128)S(1)} %max.5, pred[192,512]{1,0:T(8,128)(4,1)S(1)} %broadcast_compare_fusion.1, f32[2,8,192]{2,1,0:T(8,128)S(1)} %get-tuple-element.499, ...), kind=kOutput, calls=%fused_computation.28 | convolution fusion | flops 411303936 | bytes 9822208 | tf_op jit(solution)/shard_map/while/body/eval_jaxpr/cond/branch_1_fun/hgqk,khd->hgqd/dot_general | solution.py:61
  112.8 1.1 copy-done.4
  115.6 7.3 %conditional.6 = ((f32[2,8,192]{2,1,0:T(8,128)S(1)}, f32[2,8,192]{2,1,0:T(8,128)S(1)}, f32[2,8,192,128]{3,2,1,0:T(8,128)})) conditional(s32[]{:T(128)} %convert_element_type.77, (f32[2,8,192]{2,1,0:T(8,128)S(1)}, f32[2,8,192]{2,1,0:T(8,128)S(1)}, f32[2,8,192,128]{3,2,1,0:T(8,128)}) %tuple.76, (s32[]{:T(128)}, s32[]{:T(128)}, ...), branch_computations={%region_3.3_spmd, %region_4.6_spmd} | conditional | flops 826645184 | bytes 36510048 | solution.py:69
  115.8 1.3 fusion.4
  117.1 2.1 %fusion.6 = f32[2,8,192]{2,1,0:T(8,128)S(1)} fusion(f32[2,512,192,8]{1,2,3,0:T(8,128)S(1)} %get-tuple-element.501, f32[2,8,192]{2,1,0:T(8,128)S(1)} %max.4, pred[192,512]{1,0:T(8,128)(4,1)S(1)} %broadcast_compare_fusion), kind=kLoop, calls=%fused_computation.6 | loop fusion | flops 7861248 | bytes 6414336 | tf_op jit(solution)/shard_map/while/body/eval_jaxpr/cond/branch_1_fun/reduce_sum | solution.py:60
  119.3 2.5 %multiply_add_fusion = f32[2,8,192,128]{3,2,1,0:T(8,128)S(1)} fusion(f32[2,8,192,128]{3,2,1,0:T(8,128)S(1)} %copy-done, f32[2,512,192,8]{1,2,3,0:T(8,128)S(1)} %get-tuple-element.501, f32[2,8,192]{2,1,0:T(8,128)S(1)} %max.4, pred[192,512]{1,0:T(8,128)(4,1)S(1)} %broadcast_compare_fusion, f32[2,8,192]{2,1,0:T(8,128)S(1)} %get-tuple-element.497, ...), kind=kOutput, calls=%fused_computation.9 | convolution fusion | flops 411303936 | bytes 9822208 | tf_op jit(solution)/shard_map/while/body/eval_jaxpr/cond/branch_1_fun/hgqk,khd->hgqd/dot_general | solution.py:61
  123.5 7.3 %conditional.7 = ((f32[2,8,192]{2,1,0:T(8,128)S(1)}, f32[2,8,192]{2,1,0:T(8,128)S(1)}, f32[2,8,192,128]{3,2,1,0:T(8,128)})) conditional(s32[]{:T(128)} %convert_element_type.78, (f32[2,8,192]{2,1,0:T(8,128)S(1)}, f32[2,8,192]{2,1,0:T(8,128)S(1)}, f32[2,8,192,128]{3,2,1,0:T(8,128)}) %tuple.78, (s32[]{:T(128)}, s32[]{:T(128)}, ...), branch_computations={%region_7.7_spmd, %region_8.10_spmd} | conditional | flops 826645184 | bytes 36510048 | solution.py:69
  123.7 1.3 fusion.18
  125.1 2.1 %fusion.20 = f32[2,8,192]{2,1,0:T(8,128)S(1)} fusion(f32[2,512,192,8]{1,2,3,0:T(8,128)S(1)} %get-tuple-element.503, f32[2,8,192]{2,1,0:T(8,128)S(1)} %max.5, pred[192,512]{1,0:T(8,128)(4,1)S(1)} %broadcast_compare_fusion.1), kind=kLoop, calls=%fused_computation.25 | loop fusion | flops 7861248 | bytes 6414336 | tf_op jit(solution)/shard_map/while/body/eval_jaxpr/cond/branch_1_fun/reduce_sum | solution.py:60
  127.2 2.5 %multiply_add_fusion.2 = f32[2,8,192,128]{3,2,1,0:T(8,128)S(1)} fusion(f32[2,8,192,128]{3,2,1,0:T(8,128)S(1)} %copy-done.3, f32[2,512,192,8]{1,2,3,0:T(8,128)S(1)} %get-tuple-element.503, f32[2,8,192]{2,1,0:T(8,128)S(1)} %max.5, pred[192,512]{1,0:T(8,128)(4,1)S(1)} %broadcast_compare_fusion.1, f32[2,8,192]{2,1,0:T(8,128)S(1)} %get-tuple-element.499, ...), kind=kOutput, calls=%fused_computation.28 | convolution fusion | flops 411303936 | bytes 9822208 | tf_op jit(solution)/shard_map/while/body/eval_jaxpr/cond/branch_1_fun/hgqk,khd->hgqd/dot_general | solution.py:61
  129.7 1.1 copy-done.4
  132.5 7.3 %conditional.6 = ((f32[2,8,192]{2,1,0:T(8,128)S(1)}, f32[2,8,192]{2,1,0:T(8,128)S(1)}, f32[2,8,192,128]{3,2,1,0:T(8,128)})) conditional(s32[]{:T(128)} %convert_element_type.77, (f32[2,8,192]{2,1,0:T(8,128)S(1)}, f32[2,8,192]{2,1,0:T(8,128)S(1)}, f32[2,8,192,128]{3,2,1,0:T(8,128)}) %tuple.76, (s32[]{:T(128)}, s32[]{:T(128)}, ...), branch_computations={%region_3.3_spmd, %region_4.6_spmd} | conditional | flops 826645184 | bytes 36510048 | solution.py:69
  132.7 1.3 fusion.4
  134.0 2.1 %fusion.6 = f32[2,8,192]{2,1,0:T(8,128)S(1)} fusion(f32[2,512,192,8]{1,2,3,0:T(8,128)S(1)} %get-tuple-element.501, f32[2,8,192]{2,1,0:T(8,128)S(1)} %max.4, pred[192,512]{1,0:T(8,128)(4,1)S(1)} %broadcast_compare_fusion), kind=kLoop, calls=%fused_computation.6 | loop fusion | flops 7861248 | bytes 6414336 | tf_op jit(solution)/shard_map/while/body/eval_jaxpr/cond/branch_1_fun/reduce_sum | solution.py:60
  136.2 2.5 %multiply_add_fusion = f32[2,8,192,128]{3,2,1,0:T(8,128)S(1)} fusion(f32[2,8,192,128]{3,2,1,0:T(8,128)S(1)} %copy-done, f32[2,512,192,8]{1,2,3,0:T(8,128)S(1)} %get-tuple-element.501, f32[2,8,192]{2,1,0:T(8,128)S(1)} %max.4, pred[192,512]{1,0:T(8,128)(4,1)S(1)} %broadcast_compare_fusion, f32[2,8,192]{2,1,0:T(8,128)S(1)} %get-tuple-element.497, ...), kind=kOutput, calls=%fused_computation.9 | convolution fusion | flops 411303936 | bytes 9822208 | tf_op jit(solution)/shard_map/while/body/eval_jaxpr/cond/branch_1_fun/hgqk,khd->hgqd/dot_general | solution.py:61
  140.4 7.3 %conditional.7 = ((f32[2,8,192]{2,1,0:T(8,128)S(1)}, f32[2,8,192]{2,1,0:T(8,128)S(1)}, f32[2,8,192,128]{3,2,1,0:T(8,128)})) conditional(s32[]{:T(128)} %convert_element_type.78, (f32[2,8,192]{2,1,0:T(8,128)S(1)}, f32[2,8,192]{2,1,0:T(8,128)S(1)}, f32[2,8,192,128]{3,2,1,0:T(8,128)}) %tuple.78, (s32[]{:T(128)}, s32[]{:T(128)}, ...), branch_computations={%region_7.7_spmd, %region_8.10_spmd} | conditional | flops 826645184 | bytes 36510048 | solution.py:69
  140.6 1.3 fusion.18
  141.9 2.1 %fusion.20 = f32[2,8,192]{2,1,0:T(8,128)S(1)} fusion(f32[2,512,192,8]{1,2,3,0:T(8,128)S(1)} %get-tuple-element.503, f32[2,8,192]{2,1,0:T(8,128)S(1)} %max.5, pred[192,512]{1,0:T(8,128)(4,1)S(1)} %broadcast_compare_fusion.1), kind=kLoop, calls=%fused_computation.25 | loop fusion | flops 7861248 | bytes 6414336 | tf_op jit(solution)/shard_map/while/body/eval_jaxpr/cond/branch_1_fun/reduce_sum | solution.py:60
  144.1 2.5 %multiply_add_fusion.2 = f32[2,8,192,128]{3,2,1,0:T(8,128)S(1)} fusion(f32[2,8,192,128]{3,2,1,0:T(8,128)S(1)} %copy-done.3, f32[2,512,192,8]{1,2,3,0:T(8,128)S(1)} %get-tuple-element.503, f32[2,8,192]{2,1,0:T(8,128)S(1)} %max.5, pred[192,512]{1,0:T(8,128)(4,1)S(1)} %broadcast_compare_fusion.1, f32[2,8,192]{2,1,0:T(8,128)S(1)} %get-tuple-element.499, ...), kind=kOutput, calls=%fused_computation.28 | convolution fusion | flops 411303936 | bytes 9822208 | tf_op jit(solution)/shard_map/while/body/eval_jaxpr/cond/branch_1_fun/hgqk,khd->hgqd/dot_general | solution.py:61
  149.4 7.3 %conditional.6 = ((f32[2,8,192]{2,1,0:T(8,128)S(1)}, f32[2,8,192]{2,1,0:T(8,128)S(1)}, f32[2,8,192,128]{3,2,1,0:T(8,128)})) conditional(s32[]{:T(128)} %convert_element_type.77, (f32[2,8,192]{2,1,0:T(8,128)S(1)}, f32[2,8,192]{2,1,0:T(8,128)S(1)}, f32[2,8,192,128]{3,2,1,0:T(8,128)}) %tuple.76, (s32[]{:T(128)}, s32[]{:T(128)}, ...), branch_computations={%region_3.3_spmd, %region_4.6_spmd} | conditional | flops 826645184 | bytes 36510048 | solution.py:69
  149.5 1.3 fusion.4
  150.9 2.1 %fusion.6 = f32[2,8,192]{2,1,0:T(8,128)S(1)} fusion(f32[2,512,192,8]{1,2,3,0:T(8,128)S(1)} %get-tuple-element.501, f32[2,8,192]{2,1,0:T(8,128)S(1)} %max.4, pred[192,512]{1,0:T(8,128)(4,1)S(1)} %broadcast_compare_fusion), kind=kLoop, calls=%fused_computation.6 | loop fusion | flops 7861248 | bytes 6414336 | tf_op jit(solution)/shard_map/while/body/eval_jaxpr/cond/branch_1_fun/reduce_sum | solution.py:60
  153.0 2.5 %multiply_add_fusion = f32[2,8,192,128]{3,2,1,0:T(8,128)S(1)} fusion(f32[2,8,192,128]{3,2,1,0:T(8,128)S(1)} %copy-done, f32[2,512,192,8]{1,2,3,0:T(8,128)S(1)} %get-tuple-element.501, f32[2,8,192]{2,1,0:T(8,128)S(1)} %max.4, pred[192,512]{1,0:T(8,128)(4,1)S(1)} %broadcast_compare_fusion, f32[2,8,192]{2,1,0:T(8,128)S(1)} %get-tuple-element.497, ...), kind=kOutput, calls=%fused_computation.9 | convolution fusion | flops 411303936 | bytes 9822208 | tf_op jit(solution)/shard_map/while/body/eval_jaxpr/cond/branch_1_fun/hgqk,khd->hgqd/dot_general | solution.py:61
  157.3 7.3 %conditional.7 = ((f32[2,8,192]{2,1,0:T(8,128)S(1)}, f32[2,8,192]{2,1,0:T(8,128)S(1)}, f32[2,8,192,128]{3,2,1,0:T(8,128)})) conditional(s32[]{:T(128)} %convert_element_type.78, (f32[2,8,192]{2,1,0:T(8,128)S(1)}, f32[2,8,192]{2,1,0:T(8,128)S(1)}, f32[2,8,192,128]{3,2,1,0:T(8,128)}) %tuple.78, (s32[]{:T(128)}, s32[]{:T(128)}, ...), branch_computations={%region_7.7_spmd, %region_8.10_spmd} | conditional | flops 826645184 | bytes 36510048 | solution.py:69
  157.5 1.3 fusion.18
  158.8 2.1 %fusion.20 = f32[2,8,192]{2,1,0:T(8,128)S(1)} fusion(f32[2,512,192,8]{1,2,3,0:T(8,128)S(1)} %get-tuple-element.503, f32[2,8,192]{2,1,0:T(8,128)S(1)} %max.5, pred[192,512]{1,0:T(8,128)(4,1)S(1)} %broadcast_compare_fusion.1), kind=kLoop, calls=%fused_computation.25 | loop fusion | flops 7861248 | bytes 6414336 | tf_op jit(solution)/shard_map/while/body/eval_jaxpr/cond/branch_1_fun/reduce_sum | solution.py:60
  160.9 2.5 %multiply_add_fusion.2 = f32[2,8,192,128]{3,2,1,0:T(8,128)S(1)} fusion(f32[2,8,192,128]{3,2,1,0:T(8,128)S(1)} %copy-done.3, f32[2,512,192,8]{1,2,3,0:T(8,128)S(1)} %get-tuple-element.503, f32[2,8,192]{2,1,0:T(8,128)S(1)} %max.5, pred[192,512]{1,0:T(8,128)(4,1)S(1)} %broadcast_compare_fusion.1, f32[2,8,192]{2,1,0:T(8,128)S(1)} %get-tuple-element.499, ...), kind=kOutput, calls=%fused_computation.28 | convolution fusion | flops 411303936 | bytes 9822208 | tf_op jit(solution)/shard_map/while/body/eval_jaxpr/cond/branch_1_fun/hgqk,khd->hgqd/dot_general | solution.py:61
  163.4 1.1 copy-done.4
  164.5 2.0 %fusion.34 = bf16[192,2,8,128]{3,0,2,1:T(8,128)(2,1)S(1)} fusion(f32[2,8,192,128]{3,2,1,0:T(8,128)} %get-tuple-element.369, f32[2,8,192]{2,1,0:T(8,128)S(1)} %get-tuple-element.370), kind=kLoop, calls=%fused_computation.55 | loop fusion | flops 786432 | bytes 2371584 | tf_op jit(solution)/shard_map/convert_element_type | solution.py:133
  168.7 17.0 %all_to_all.19 = bf16[4,96,2048]{2,1,0:T(8,128)(2,1)S(1)} all-to-all(bf16[4,96,2048]{2,1,0:T(8,128)(2,1)S(1)} %bitcast.90), channel_id=1, replica_groups=mesh['heads'=4,'ctx'=8] {'heads'}, dimensions={0} | all-to-all | bytes 3145728 | tf_op jit(solution)/shard_map/all_to_all | solution.py:139
  185.7 1.2 copy.63
  (163 shorter events, 24.3 us)
Async XLA Ops:
  6.5 5.2 %copy-start.5 = (bf16[384,2048]{1,0:T(8,128)(2,1)S(1)}, bf16[384,2048]{1,0:T(8,128)(2,1)}, u32[]{:S(2)}) copy-start(bf16[384,2048]{1,0:T(8,128)(2,1)} %param.10) | copy-start | bytes 4718596
  6.5 28.1 %all-gather.3.cloned.1.call-start = ((), (), s32[]{:S(2)}) async-start(), calls=%async_computation.1 | async-start | bytes 1769472 | tf_op jit(solution)/shard_map/all_gather | solution.py:104
  9.6 51.1 %all-gather.5.cloned.1.call-start = ((), (), s32[]{:S(2)}) async-start(), calls=%async_computation.2 | async-start | bytes 1769472 | tf_op jit(solution)/shard_map/all_gather | solution.py:105
  66.5 2.1 %copy-start = (f32[2,8,192,128]{3,2,1,0:T(8,128)S(1)}, f32[2,8,192,128]{3,2,1,0:T(8,128)}, u32[]{:S(2)}) copy-start(f32[2,8,192,128]{3,2,1,0:T(8,128)} %get-tuple-element.331) | copy-start | bytes 4718596 | tf_op jit(solution)/shard_map/while/body/eval_jaxpr/cond
  71.2 1.1 copy-start.1
  74.4 2.1 %copy-start.3 = (f32[2,8,192,128]{3,2,1,0:T(8,128)S(1)}, f32[2,8,192,128]{3,2,1,0:T(8,128)}, u32[]{:S(2)}) copy-start(f32[2,8,192,128]{3,2,1,0:T(8,128)} %get-tuple-element.339) | copy-start | bytes 4718596 | tf_op jit(solution)/shard_map/while/body/eval_jaxpr/cond
  79.1 1.1 copy-start.4
  83.4 2.1 %copy-start = (f32[2,8,192,128]{3,2,1,0:T(8,128)S(1)}, f32[2,8,192,128]{3,2,1,0:T(8,128)}, u32[]{:S(2)}) copy-start(f32[2,8,192,128]{3,2,1,0:T(8,128)} %get-tuple-element.331) | copy-start | bytes 4718596 | tf_op jit(solution)/shard_map/while/body/eval_jaxpr/cond
  88.0 1.1 copy-start.1
  91.3 2.1 %copy-start.3 = (f32[2,8,192,128]{3,2,1,0:T(8,128)S(1)}, f32[2,8,192,128]{3,2,1,0:T(8,128)}, u32[]{:S(2)}) copy-start(f32[2,8,192,128]{3,2,1,0:T(8,128)} %get-tuple-element.339) | copy-start | bytes 4718596 | tf_op jit(solution)/shard_map/while/body/eval_jaxpr/cond
  95.9 1.1 copy-start.4
  100.3 2.1 %copy-start = (f32[2,8,192,128]{3,2,1,0:T(8,128)S(1)}, f32[2,8,192,128]{3,2,1,0:T(8,128)}, u32[]{:S(2)}) copy-start(f32[2,8,192,128]{3,2,1,0:T(8,128)} %get-tuple-element.331) | copy-start | bytes 4718596 | tf_op jit(solution)/shard_map/while/body/eval_jaxpr/cond
  104.9 1.1 copy-start.1
  108.2 2.1 %copy-start.3 = (f32[2,8,192,128]{3,2,1,0:T(8,128)S(1)}, f32[2,8,192,128]{3,2,1,0:T(8,128)}, u32[]{:S(2)}) copy-start(f32[2,8,192,128]{3,2,1,0:T(8,128)} %get-tuple-element.339) | copy-start | bytes 4718596 | tf_op jit(solution)/shard_map/while/body/eval_jaxpr/cond
  112.8 1.1 copy-start.4
  117.1 2.1 %copy-start = (f32[2,8,192,128]{3,2,1,0:T(8,128)S(1)}, f32[2,8,192,128]{3,2,1,0:T(8,128)}, u32[]{:S(2)}) copy-start(f32[2,8,192,128]{3,2,1,0:T(8,128)} %get-tuple-element.331) | copy-start | bytes 4718596 | tf_op jit(solution)/shard_map/while/body/eval_jaxpr/cond
  121.7 1.1 copy-start.1
  125.0 2.1 %copy-start.3 = (f32[2,8,192,128]{3,2,1,0:T(8,128)S(1)}, f32[2,8,192,128]{3,2,1,0:T(8,128)}, u32[]{:S(2)}) copy-start(f32[2,8,192,128]{3,2,1,0:T(8,128)} %get-tuple-element.339) | copy-start | bytes 4718596 | tf_op jit(solution)/shard_map/while/body/eval_jaxpr/cond
  129.7 1.1 copy-start.4
  134.0 2.1 %copy-start = (f32[2,8,192,128]{3,2,1,0:T(8,128)S(1)}, f32[2,8,192,128]{3,2,1,0:T(8,128)}, u32[]{:S(2)}) copy-start(f32[2,8,192,128]{3,2,1,0:T(8,128)} %get-tuple-element.331) | copy-start | bytes 4718596 | tf_op jit(solution)/shard_map/while/body/eval_jaxpr/cond
  138.6 1.1 copy-start.1
  141.9 2.1 %copy-start.3 = (f32[2,8,192,128]{3,2,1,0:T(8,128)S(1)}, f32[2,8,192,128]{3,2,1,0:T(8,128)}, u32[]{:S(2)}) copy-start(f32[2,8,192,128]{3,2,1,0:T(8,128)} %get-tuple-element.339) | copy-start | bytes 4718596 | tf_op jit(solution)/shard_map/while/body/eval_jaxpr/cond
  146.5 1.1 copy-start.4
  150.9 2.1 %copy-start = (f32[2,8,192,128]{3,2,1,0:T(8,128)S(1)}, f32[2,8,192,128]{3,2,1,0:T(8,128)}, u32[]{:S(2)}) copy-start(f32[2,8,192,128]{3,2,1,0:T(8,128)} %get-tuple-element.331) | copy-start | bytes 4718596 | tf_op jit(solution)/shard_map/while/body/eval_jaxpr/cond
  155.5 1.1 copy-start.1
  158.8 2.1 %copy-start.3 = (f32[2,8,192,128]{3,2,1,0:T(8,128)S(1)}, f32[2,8,192,128]{3,2,1,0:T(8,128)}, u32[]{:S(2)}) copy-start(f32[2,8,192,128]{3,2,1,0:T(8,128)} %get-tuple-element.339) | copy-start | bytes 4718596 | tf_op jit(solution)/shard_map/while/body/eval_jaxpr/cond
  163.4 1.1 copy-start.4
  164.5 2.7 %copy-start.2 = (f32[2,8,192,128]{3,2,1,0:T(8,128)S(1)}, f32[2,8,192,128]{3,2,1,0:T(8,128)}, u32[]{:S(2)}) copy-start(f32[2,8,192,128]{3,2,1,0:T(8,128)} %get-tuple-element.367) | copy-start | bytes 4718596
Sparse Core Ops, SparseCore 0:
  9.8 24.8 all-gather.2
  36.3 24.3 all-gather.4
where the time goes:
time: 194 us
  matrix products  45.1 us (23%)
  waiting for transfers between devices  43.3 us (22%)
  other arithmetic  35.4 us (18%)
  local copies, waits for them, and re-layouts  30.4 us (16%)
  blocking collectives  17 us (9%)
  between operations  13.6 us (7%)
  loops' own time  8.96 us (5%)
    dot_general x12, matrix products, update(): jnp.einsum('hgqk,khd->hgqd', weights.astype(jnp.bfloat16), values_part, p...  29.4 us
    all_gather x1, waiting for transfers between devices, local(): lax.all_gather(values, 'ctx', axis=0, tiled=True)  26 us
    reduce_sum x12, other arithmetic, update(): new_sum = prev_sum * factor + jnp.sum(weights, axis=-1)  25.1 us
    all_gather x1, waiting for transfers between devices, local(): lax.all_gather(flat_keys, 'ctx', axis=0, tiled=True)  17.2 us
    all_to_all x1, blocking collectives, local(): lax.all_to_all(combined, 'heads', split_axis=0, concat_axis=1, tiled=True)  17 us
    dot_general x12, matrix products, update(): jnp.einsum('qhgd,khd->hgqk', queries_part, keys_part, preferred_element_t...  15.6 us
    cond x60, local copies, waits for them, and re-layouts  13.8 us
    another operation x1, loops' own time, local(): lax.fori_loop(0, piece_rows // block_rows, one_block, (fresh_state(), fre...  7.72 us
  transfers between devices with their start and end apart: 2, of which 2 were waited for; matrix products, arithmetic and copies ran while one was open for 4% of the time, Pallas kernels for 0%

commit v1 on v0

v1 whole, which is shorter than its diff:
```python
import functools
import math

import jax
import jax.numpy as jnp
import numpy as np
from jax import lax
from jax.experimental import pallas as pl
from jax.experimental.pallas import tpu as pltpu
from jax.sharding import PartitionSpec as P

HD = 128
HALF = HD // 2
NEG_FILL = -1e30
EXP2_SCALE = math.log2(math.e) / math.sqrt(HD)


def inverse_frequencies():
    base = 500000.0 ** (-2.0 * np.arange(HALF) / HD)
    wave = 2.0 * math.pi / base
    blend = (8192.0 / wave - 1.0) / 3.0
    middle = (1.0 - blend) * base / 8.0 + blend * base
    freq = np.where(wave < 2048.0, base, np.where(wave > 8192.0, base / 8.0, middle))
    return np.concatenate([freq, freq]).astype(np.float32)[None, :]


def cos_sin(angle):
    turns = jnp.round(angle * (2.0 / math.pi))
    rest = angle - turns * 1.5703125
    rest = rest - turns * 4.837512969970703e-4
    rest = rest - turns * 7.54978995489188e-8
    quadrant = turns.astype(jnp.int32) & 3
    sq = rest * rest
    sine = rest + rest * sq * (-1.6666654611e-1 + sq * (8.3321608736e-3 - sq * 1.9515295891e-4))
    cosine = (
        1.0
        - 0.5 * sq
        + sq * sq * (4.166664568298827e-2 + sq * (-1.388731625493765e-3 + sq * 2.443315711809948e-5))
    )
    odd = (quadrant & 1) == 1
    cos_out = jnp.where(odd, sine, cosine)
    sin_out = jnp.where(odd, cosine, sine)
    cos_out = jnp.where((quadrant == 1) | (quadrant == 2), -cos_out, cos_out)
    sin_out = jnp.where(quadrant >= 2, -sin_out, sin_out)
    return cos_out, sin_out


def rotate(x, cosine, sine):
    return x * cosine + pltpu.roll(x, HALF, 1) * sine


def prep_kernel(heads, pos_ref, freq_ref, k_ref, v_ref, table_ref, *pack_refs):
    sign = jnp.where(lax.broadcasted_iota(jnp.int32, (HD, HD), 1) < HALF, -1.0, 1.0)
    for tile in range(k_ref.shape[0] // HD):
        rows = slice(tile * HD, (tile + 1) * HD)
        pos = pos_ref[:, rows].astype(jnp.float32)
        pos = jnp.broadcast_to(pos, (HD, HD)).T
        cosine, sine = cos_sin(pos * freq_ref[...])
        sine = sine * sign
        table_ref[rows, :HD] = cosine
        table_ref[rows, HD:] = sine
        for head in range(heads):
            cols = slice(head * HD, (head + 1) * HD)
            key = rotate(k_ref[rows, cols].astype(jnp.float32), cosine, sine)
            pack_refs[head][rows, :HD] = key.astype(jnp.bfloat16)
            pack_refs[head][rows, HD:] = v_ref[rows, cols].T


def prep(keys, values, positions):
    rows, cols = keys.shape
    heads = cols // HD
    return pl.pallas_call(
        functools.partial(prep_kernel, heads),
        out_shape=[jax.ShapeDtypeStruct((rows, 2 * HD), jnp.float32)]
        + [jax.ShapeDtypeStruct((rows, 2 * HD), jnp.bfloat16)] * heads,
        compiler_params=pltpu.CompilerParams(vmem_limit_bytes=32 << 20),
        name="prep",
    )(positions.reshape(1, rows), jnp.asarray(inverse_frequencies()), keys, values)


def flash_kernel(blocks, group, parts, q_ref, table_ref, *refs):
    kv_refs, out_refs = refs[:blocks], refs[blocks:]
    rows = q_ref.shape[0]
    piece = rows // parts
    me = lax.axis_index("heads")
    rank = lax.axis_index("ctx")
    chip, core = rank // 2, rank % 2
    query_cols, row_index = [], []
    starts = [pl.multiple_of((me ^ k) * piece, piece) for k in range(parts)]
    lane = lax.broadcasted_iota(jnp.int32, (1, piece), 1)
    for start in starts:
        row_index.append(lane + start)
    row_index = jnp.concatenate(row_index, axis=1)
    pieces = [q_ref[pl.ds(start, piece), :].astype(jnp.float32) for start in starts]
    queries = jnp.concatenate(pieces, axis=0)
    tables = jnp.concatenate([table_ref[pl.ds(start, piece), :] for start in starts], axis=0)
    for head in range(group):
        x = queries[:, head * HD : (head + 1) * HD]
        x = rotate(x, tables[:, :HD], tables[:, HD:])
        query_cols.append(x.T.astype(jnp.bfloat16))
    pair = 2 if group % 2 == 0 else 1
    tiles = [
        jnp.concatenate(query_cols[i : i + pair], axis=1) if pair > 1 else query_cols[i]
        for i in range(0, group, pair)
    ]
    tile_index = jnp.concatenate([row_index] * pair, axis=1)
    width = rows * pair
    work = [(b, i) for b in range(blocks) for i in range(len(tiles))]
    key_index = lax.broadcasted_iota(jnp.int32, (rows, width), 0)

    def score(b, i):
        return jnp.dot(kv_refs[b][:, :HD], tiles[i], preferred_element_type=jnp.float32)

    states = [None] * len(tiles)
    upcoming = score(*work[0])
    for step, (b, i) in enumerate(work):
        s = upcoming
        if step + 1 < len(work):
            upcoming = score(*work[step + 1])
        valid = None
        if b < 2:
            shift = 0 if b == 0 else jnp.where(core == 1, -rows, rows)
            s = jnp.where(key_index + shift <= tile_index, s, NEG_FILL)
        else:
            valid = chip >= b // 2
        top = jnp.max(s, axis=0, keepdims=True)
        values_t = jnp.concatenate(
            [kv_refs[b][t * HD : (t + 1) * HD, HD:] for t in range(rows // HD)], axis=1
        )
        if b == 0:
            p = jnp.exp2((s - top) * EXP2_SCALE)
            total = jnp.sum(p, axis=0, keepdims=True)
            acc = jnp.dot(values_t, p.astype(jnp.bfloat16), preferred_element_type=jnp.float32)
            states[i] = (top, total, acc)
            continue
        prev_top, total, acc = states[i]
        new_top = jnp.maximum(prev_top, top)
        p = jnp.exp2(s * EXP2_SCALE - new_top * EXP2_SCALE)
        part = jnp.sum(p, axis=0, keepdims=True)
        mixed = jnp.dot(values_t, p.astype(jnp.bfloat16), preferred_element_type=jnp.float32)
        factor = jnp.exp2((prev_top - new_top) * EXP2_SCALE)
        if valid is not None:
            factor = jnp.where(valid, factor, 1.0)
            part = jnp.where(valid, part, 0.0)
            new_top = jnp.where(valid, new_top, prev_top)
        states[i] = (new_top, total * factor + part, acc * factor + mixed)
    for i, (_, total, acc) in enumerate(states):
        result = acc * (1.0 / total)
        for g in range(pair):
            head = i * pair + g
            block = result[:, g * rows : (g + 1) * rows].T.astype(jnp.bfloat16)
            for k in range(parts):
                out_refs[k][:, head * HD : (head + 1) * HD] = block[k * piece : (k + 1) * piece]


def flash(queries, table, blocks, first, count, group, parts):
    rows = queries.shape[0]
    keys = sum(b.shape[0] for b in blocks)
    whole = lambda i: (0, 0)
    return pl.pallas_call(
        functools.partial(flash_kernel, len(blocks), group, parts),
        grid=(count // group,),
        in_specs=[
            pl.BlockSpec((rows, group * HD), lambda i: (0, first // group + i)),
            pl.BlockSpec(table.shape, whole),
        ]
        + [pl.BlockSpec(b.shape, whole) for b in blocks],
        out_specs=[pl.BlockSpec((rows // parts, group * HD), lambda i: (0, i))] * parts,
        out_shape=[jax.ShapeDtypeStruct((rows // parts, count * HD), jnp.bfloat16)] * parts,
        compiler_params=pltpu.CompilerParams(vmem_limit_bytes=40 << 20),
        cost_estimate=pl.CostEstimate(
            flops=4 * rows * count * keys * HD,
            bytes_accessed=4 * rows * count * HD + 4 * keys * HD,
            transcendentals=rows * count * keys,
        ),
        name="flash",
    )(queries, table, *blocks)


def place_kernel(heads, parts, *refs):
    pieces, out_ref, sems = refs[: heads * parts], refs[-2], refs[-1]
    me = lax.axis_index("heads")
    copies = []
    for head in range(heads):
        for k in range(parts):
            src = pieces[head * parts + k]
            cols = src.shape[1]
            start = pl.multiple_of(((me ^ k) * heads + head) * cols, cols)
            copies.append(
                pltpu.make_async_copy(src, out_ref.at[:, pl.ds(start, cols)], sems.at[len(copies)])
            )
    for c in copies:
        c.start()
    for c in copies:
        c.wait()


def place(pieces, heads, parts):
    rows, cols = pieces[0].shape
    return pl.pallas_call(
        functools.partial(place_kernel, heads, parts),
        in_specs=[pl.BlockSpec(memory_space=pltpu.VMEM)] * len(pieces),
        out_specs=pl.BlockSpec(memory_space=pl.ANY),
        out_shape=jax.ShapeDtypeStruct((rows, cols * len(pieces)), jnp.bfloat16),
        compiler_params=pltpu.CompilerParams(vmem_limit_bytes=16 << 20),
        scratch_shapes=[pltpu.SemaphoreType.DMA((len(pieces),))],
        name="place",
    )(*pieces)


def local(ctx_size, parts, queries, keys, values, positions):
    kv_heads = keys.shape[1] // HD
    group_size = queries.shape[1] // (kv_heads * HD)
    chips = ctx_size // 2
    up = [(c, c + 2) for c in range(ctx_size - 2)]
    swap = [(c, c ^ 1) for c in range(ctx_size)]
    table, *packs = prep(keys, values, positions)
    pieces = []
    for head in range(kv_heads):
        block = packs[head]
        blocks = [block, lax.ppermute(block, "ctx", swap)]
        for _ in range(1, chips):
            block = lax.ppermute(block, "ctx", up)
            blocks += [block, lax.ppermute(block, "ctx", swap)]
        outs = flash(queries, table, blocks, head * group_size, group_size, group_size // 2, parts)
        for k in range(parts):
            perm = [(i, i ^ k) for i in range(parts)]
            pieces.append(lax.ppermute(outs[k], "heads", perm) if k else outs[k])
    return place(pieces, kv_heads, parts)


def solution(mesh):
    return jax.shard_map(
        functools.partial(local, mesh.shape["ctx"], mesh.shape["heads"]),
        mesh=mesh,
        in_specs=(P("ctx", "heads"), P("ctx", "heads"), P("ctx", "heads"), P("ctx")),
        out_specs=P(("ctx", "heads"), None),
        check_vma=False,
    )
```

time: 194 us -> 82.9 us (0.43)
  the two profiles are of different devices: /device:TPU:25 before, /device:TPU:24 now
where the time goes in v1:
time: 82.9 us; the launch traced here: 81.8 us
  Pallas kernels  30.7 us (37%)
  waiting for transfers between devices  29.7 us (36%)
  starting transfers between devices  16.5 us (20%)
  local copies, waits for them, and re-layouts  4.6 us (6%)
    pallas_call x2, Pallas kernels, flash(): pl.pallas_call(functools.partial(flash_kernel, len(blocks), group, parts)...  29.1 us
    ppermute x6, waiting for transfers between devices, local(): block = lax.ppermute(block, 'ctx', up)  21.3 us
    ppermute x6, waiting for transfers between devices, local(): pieces.append(lax.ppermute(outs[k], 'heads', perm) if k else outs[k])  8.41 us
    ppermute x6, starting transfers between devices, local(): block = lax.ppermute(block, 'ctx', up)  7.71 us
    ppermute x6, starting transfers between devices, local(): pieces.append(lax.ppermute(outs[k], 'heads', perm) if k else outs[k])  7.11 us
    unnamed x8, local copies, waits for them, and re-layouts  3.91 us
  transfers between devices with their start and end apart: 20, of which 8 were waited for; matrix products, arithmetic and copies ran while one was open for 0% of the time, Pallas kernels for 36%

profile of v1, /device:TPU:24, one launch (start us, length us, event | category | flops | bytes accessed | tf_op | source)
XLA Modules:
  0.0 81.8 jit_solution(14895636404508332631)
XLA Ops:
  0.0 0.7 reshape.3.pos_ref
  0.7 0.0 copy-start
  0.7 0.9 %copy-done = bf16[384,256]{1,0:T(8,128)(2,1)S(1)} copy-done((bf16[384,256]{1,0:T(8,128)(2,1)S(1)}, bf16[384,256]{1,0:T(8,128)(2,1)}, u32[]{:S(2)}) %copy-start) | copy-done | bytes 196632
  1.6 0.0 copy-start.1
  1.6 0.9 %copy-done.1 = bf16[384,256]{1,0:T(8,128)(2,1)S(1)} copy-done((bf16[384,256]{1,0:T(8,128)(2,1)S(1)}, bf16[384,256]{1,0:T(8,128)(2,1)}, u32[]{:S(2)}) %copy-start.1) | copy-done | bytes 196632
  2.5 0.0 copy-start.2
  2.5 0.7 copy-done.2
  3.2 0.4 prep.1
  3.7 1.3 %collective-permute-start.1 = (bf16[384,256]{1,0:T(8,128)(2,1)S(1)}, bf16[384,256]{1,0:T(8,128)(2,1)S(1)}, u32[]{:S(2)}, u32[]{:S(2)}) collective-permute-start(bf16[384,256]{1,0:T(8,128)(2,1)S(1)} %get-tuple-element.17.refs_0_), channel_id=1, source_target_pairs={{0,2},{1,3},{2,4},{3,5},{4,6},{5,7},{8,10},{9,11},{10,12},{11,13},... | collective-permute-start | bytes 589832 | tf_op jit(solution)/shard_map/ppermute | solution.py:223
  5.0 1.3 %collective-permute-start.11 = (bf16[384,256]{1,0:T(8,128)(2,1)S(1)}, bf16[384,256]{1,0:T(8,128)(2,1)S(1)}, u32[]{:S(2)}, u32[]{:S(2)}) collective-permute-start(bf16[384,256]{1,0:T(8,128)(2,1)S(1)} %get-tuple-element.22.refs_0_), channel_id=1, source_target_pairs={{0,2},{1,3},{2,4},{3,5},{4,6},{5,7},{8,10},{9,11},{10,12},{11,13},... | collective-permute-start | bytes 589832 | tf_op jit(solution)/shard_map/ppermute | solution.py:223
  6.3 7.1 %collective-permute-done.1.refs_2_ = bf16[384,256]{1,0:T(8,128)(2,1)S(1)} collective-permute-done((bf16[384,256]{1,0:T(8,128)(2,1)S(1)}, bf16[384,256]{1,0:T(8,128)(2,1)S(1)}, u32[]{:S(2)}, u32[]{:S(2)}) %collective-permute-start.1) | collective-permute-done | bytes 196640 | tf_op jit(solution)/shard_map/ppermute | solution.py:223
  13.3 1.3 %collective-permute-start.3 = (bf16[384,256]{1,0:T(8,128)(2,1)S(1)}, bf16[384,256]{1,0:T(8,128)(2,1)S(1)}, u32[]{:S(2)}, u32[]{:S(2)}) collective-permute-start(bf16[384,256]{1,0:T(8,128)(2,1)S(1)} %collective-permute-done.1.refs_2_), channel_id=1, source_target_pairs={{0,2},{1,3},{2,4},{3,5},{4,6},{5,7},{8,10},{9,11},{10,12},{11,13},... | collective-permute-start | bytes 589832 | tf_op jit(solution)/shard_map/ppermute | solution.py:223
  14.6 2.5 %collective-permute-done.11.refs_2_ = bf16[384,256]{1,0:T(8,128)(2,1)S(1)} collective-permute-done((bf16[384,256]{1,0:T(8,128)(2,1)S(1)}, bf16[384,256]{1,0:T(8,128)(2,1)S(1)}, u32[]{:S(2)}, u32[]{:S(2)}) %collective-permute-start.11) | collective-permute-done | bytes 196640 | tf_op jit(solution)/shard_map/ppermute | solution.py:223
  17.1 1.3 %collective-permute-start.13 = (bf16[384,256]{1,0:T(8,128)(2,1)S(1)}, bf16[384,256]{1,0:T(8,128)(2,1)S(1)}, u32[]{:S(2)}, u32[]{:S(2)}) collective-permute-start(bf16[384,256]{1,0:T(8,128)(2,1)S(1)} %collective-permute-done.11.refs_2_), channel_id=1, source_target_pairs={{0,2},{1,3},{2,4},{3,5},{4,6},{5,7},{8,10},{9,11},{10,12},{11,13},... | collective-permute-start | bytes 589832 | tf_op jit(solution)/shard_map/ppermute | solution.py:223
  18.4 3.5 %collective-permute-done.3.refs_4_ = bf16[384,256]{1,0:T(8,128)(2,1)S(1)} collective-permute-done((bf16[384,256]{1,0:T(8,128)(2,1)S(1)}, bf16[384,256]{1,0:T(8,128)(2,1)S(1)}, u32[]{:S(2)}, u32[]{:S(2)}) %collective-permute-start.3) | collective-permute-done | bytes 196640 | tf_op jit(solution)/shard_map/ppermute | solution.py:223
  21.9 1.3 %collective-permute-start.5 = (bf16[384,256]{1,0:T(8,128)(2,1)S(1)}, bf16[384,256]{1,0:T(8,128)(2,1)S(1)}, u32[]{:S(2)}, u32[]{:S(2)}) collective-permute-start(bf16[384,256]{1,0:T(8,128)(2,1)S(1)} %collective-permute-done.3.refs_4_), channel_id=1, source_target_pairs={{0,2},{1,3},{2,4},{3,5},{4,6},{5,7},{8,10},{9,11},{10,12},{11,13},... | collective-permute-start | bytes 589832 | tf_op jit(solution)/shard_map/ppermute | solution.py:223
  23.2 0.1 collective-permute-start
  23.3 0.5 collective-permute-start.2
  23.8 0.1 collective-permute-start.4
  23.9 3.0 %collective-permute-done.13.refs_4_ = bf16[384,256]{1,0:T(8,128)(2,1)S(1)} collective-permute-done((bf16[384,256]{1,0:T(8,128)(2,1)S(1)}, bf16[384,256]{1,0:T(8,128)(2,1)S(1)}, u32[]{:S(2)}, u32[]{:S(2)}) %collective-permute-start.13) | collective-permute-done | bytes 196640 | tf_op jit(solution)/shard_map/ppermute | solution.py:223
  26.8 1.3 %collective-permute-start.15 = (bf16[384,256]{1,0:T(8,128)(2,1)S(1)}, bf16[384,256]{1,0:T(8,128)(2,1)S(1)}, u32[]{:S(2)}, u32[]{:S(2)}) collective-permute-start(bf16[384,256]{1,0:T(8,128)(2,1)S(1)} %collective-permute-done.13.refs_4_), channel_id=1, source_target_pairs={{0,2},{1,3},{2,4},{3,5},{4,6},{5,7},{8,10},{9,11},{10,12},{11,13},... | collective-permute-start | bytes 589832 | tf_op jit(solution)/shard_map/ppermute | solution.py:223
  28.1 1.4 %collective-permute-done.5.refs_6_ = bf16[384,256]{1,0:T(8,128)(2,1)S(1)} collective-permute-done((bf16[384,256]{1,0:T(8,128)(2,1)S(1)}, bf16[384,256]{1,0:T(8,128)(2,1)S(1)}, u32[]{:S(2)}, u32[]{:S(2)}) %collective-permute-start.5) | collective-permute-done | bytes 196640 | tf_op jit(solution)/shard_map/ppermute | solution.py:223
  29.5 0.0 collective-permute-start.6
  29.5 0.0 collective-permute-done.refs_1_
  29.5 0.5 collective-permute-start.10
  30.0 0.0 collective-permute-done.2.refs_3_
  30.0 0.1 collective-permute-start.12
  30.1 0.0 collective-permute-done.4.refs_5_
  30.1 0.4 collective-permute-start.14
  30.5 3.9 %collective-permute-done.15.refs_6_ = bf16[384,256]{1,0:T(8,128)(2,1)S(1)} collective-permute-done((bf16[384,256]{1,0:T(8,128)(2,1)S(1)}, bf16[384,256]{1,0:T(8,128)(2,1)S(1)}, u32[]{:S(2)}, u32[]{:S(2)}) %collective-permute-start.15) | collective-permute-done | bytes 196640 | tf_op jit(solution)/shard_map/ppermute | solution.py:223
  34.4 0.0 collective-permute-start.16
  34.4 0.0 collective-permute-done.6.refs_7_
  34.4 0.0 copy-start.3
  34.4 1.4 %copy-done.3 = bf16[384,2048]{1,0:T(8,128)(2,1)S(1)} copy-done((bf16[384,2048]{1,0:T(8,128)(2,1)S(1)}, bf16[384,2048]{1,0:T(8,128)(2,1)}, u32[]{:S(2)}) %copy-start.3) | copy-done | bytes 1572888
  35.8 14.5 %flash.2 = (bf16[96,1024]{1,0:T(8,128)(2,1)S(1)}, bf16[96,1024]{1,0:T(8,128)(2,1)S(1)}, bf16[96,1024]{1,0:T(8,128)(2,1)S(1)}, bf16[96,1024]{1,0:T(8,128)(2,1)S(1)}) custom-call(bf16[384,2048]{1,0:T(8,128)(2,1)S(1)} %copy-done.3, f32[384,256]{1,0:T(8,128)S(1)} %get-tuple-element.16.table_ref, bf16[384,256]{1,0:T(8,128)(2,1)S(1)} %get-tuple-element.17.refs_0_, ...), custom_call_target="tpu_custom_call" | custom-call | flops 4831838208 | bytes 3145728 | tf_op jit(solution)/shard_map/flash/pallas_call | solution.py:160
  50.3 1.6 %collective-permute-start.7 = (bf16[96,1024]{1,0:T(8,128)(2,1)S(1)}, bf16[96,1024]{1,0:T(8,128)(2,1)S(1)}, u32[]{:S(2)}, u32[]{:S(2)}) collective-permute-start(bf16[96,1024]{1,0:T(8,128)(2,1)S(1)} %get-tuple-element.19), channel_id=1, source_target_pairs={{0,8},{8,0},{16,24},{24,16},{1,9},{9,1},{17,25},{25,17},{2,10},{10... | collective-permute-start | bytes 589832 | tf_op jit(solution)/shard_map/ppermute | solution.py:228
  51.9 0.0 collective-permute-done.10.refs_1_
  51.9 1.5 %collective-permute-start.8 = (bf16[96,1024]{1,0:T(8,128)(2,1)S(1)}, bf16[96,1024]{1,0:T(8,128)(2,1)S(1)}, u32[]{:S(2)}, u32[]{:S(2)}) collective-permute-start(bf16[96,1024]{1,0:T(8,128)(2,1)S(1)} %get-tuple-element.20), channel_id=1, source_target_pairs={{0,16},{8,24},{16,0},{24,8},{1,17},{9,25},{17,1},{25,9},{2,18},{10... | collective-permute-start | bytes 589832 | tf_op jit(solution)/shard_map/ppermute | solution.py:228
  53.4 0.0 collective-permute-done.12.refs_3_
  53.4 0.5 collective-permute-start.9
  53.9 0.0 collective-permute-done.14.refs_5_
  53.9 0.0 collective-permute-done.16.refs_7_
  53.9 14.6 %flash.3 = (bf16[96,1024]{1,0:T(8,128)(2,1)S(1)}, bf16[96,1024]{1,0:T(8,128)(2,1)S(1)}, bf16[96,1024]{1,0:T(8,128)(2,1)S(1)}, bf16[96,1024]{1,0:T(8,128)(2,1)S(1)}) custom-call(bf16[384,2048]{1,0:T(8,128)(2,1)S(1)} %copy-done.3, f32[384,256]{1,0:T(8,128)S(1)} %get-tuple-element.16.table_ref, bf16[384,256]{1,0:T(8,128)(2,1)S(1)} %get-tuple-element.22.refs_0_, ...), custom_call_target="tpu_custom_call" | custom-call | flops 4831838208 | bytes 3145728 | tf_op jit(solution)/shard_map/flash/pallas_call | solution.py:160
  68.5 1.6 %collective-permute-start.17 = (bf16[96,1024]{1,0:T(8,128)(2,1)S(1)}, bf16[96,1024]{1,0:T(8,128)(2,1)S(1)}, u32[]{:S(2)}, u32[]{:S(2)}) collective-permute-start(bf16[96,1024]{1,0:T(8,128)(2,1)S(1)} %get-tuple-element.24), channel_id=1, source_target_pairs={{0,8},{8,0},{16,24},{24,16},{1,9},{9,1},{17,25},{25,17},{2,10},{10... | collective-permute-start | bytes 589832 | tf_op jit(solution)/shard_map/ppermute | solution.py:228
  70.0 1.5 %collective-permute-start.18 = (bf16[96,1024]{1,0:T(8,128)(2,1)S(1)}, bf16[96,1024]{1,0:T(8,128)(2,1)S(1)}, u32[]{:S(2)}, u32[]{:S(2)}) collective-permute-start(bf16[96,1024]{1,0:T(8,128)(2,1)S(1)} %get-tuple-element.25), channel_id=1, source_target_pairs={{0,16},{8,24},{16,0},{24,8},{1,17},{9,25},{17,1},{25,9},{2,18},{10... | collective-permute-start | bytes 589832 | tf_op jit(solution)/shard_map/ppermute | solution.py:228
  71.5 0.0 collective-permute-done.7.refs_1_
  71.6 0.5 collective-permute-start.19
  72.0 0.0 collective-permute-done.8.refs_2_
  72.0 0.0 collective-permute-done.9.refs_3_
  72.0 4.3 %collective-permute-done.17.refs_5_ = bf16[96,1024]{1,0:T(8,128)(2,1)S(1)} collective-permute-done((bf16[96,1024]{1,0:T(8,128)(2,1)S(1)}, bf16[96,1024]{1,0:T(8,128)(2,1)S(1)}, u32[]{:S(2)}, u32[]{:S(2)}) %collective-permute-start.17) | collective-permute-done | bytes 196640 | tf_op jit(solution)/shard_map/ppermute | solution.py:228
  76.3 4.1 %collective-permute-done.18.refs_6_ = bf16[96,1024]{1,0:T(8,128)(2,1)S(1)} collective-permute-done((bf16[96,1024]{1,0:T(8,128)(2,1)S(1)}, bf16[96,1024]{1,0:T(8,128)(2,1)S(1)}, u32[]{:S(2)}, u32[]{:S(2)}) %collective-permute-start.18) | collective-permute-done | bytes 196640 | tf_op jit(solution)/shard_map/ppermute | solution.py:228
  80.4 0.0 collective-permute-done.19.refs_7_
  80.4 1.2 %place.1 = bf16[96,8192]{1,0:T(8,128)(2,1)} custom-call(bf16[96,1024]{1,0:T(8,128)(2,1)S(1)} %get-tuple-element.18.refs_0_, bf16[96,1024]{1,0:T(8,128)(2,1)S(1)} %collective-permute-done.7.refs_1_, bf16[96,1024]{1,0:T(8,128)(2,1)S(1)} %collective-permute-done.8.refs_2_, bf16[96,1024]{1,0:T(8,128)(2,1)S(1)} %collective-permute-done.9.refs_3_, ...), custom_call_target="tpu_custom_call" | custom-call | tf_op jit(solution)/shard_map/place/pallas_call | solution.py:200
Async XLA Ops:
  0.7 0.9 %copy-start = (bf16[384,256]{1,0:T(8,128)(2,1)S(1)}, bf16[384,256]{1,0:T(8,128)(2,1)}, u32[]{:S(2)}) copy-start(bf16[384,256]{1,0:T(8,128)(2,1)} %k_ref.1) | copy-start | bytes 589828
  1.6 0.9 %copy-start.1 = (bf16[384,256]{1,0:T(8,128)(2,1)S(1)}, bf16[384,256]{1,0:T(8,128)(2,1)}, u32[]{:S(2)}) copy-start(bf16[384,256]{1,0:T(8,128)(2,1)} %v_ref.1) | copy-start | bytes 589828
  2.5 0.7 copy-start.2
  3.7 9.7 %collective-permute-start.1 = (bf16[384,256]{1,0:T(8,128)(2,1)S(1)}, bf16[384,256]{1,0:T(8,128)(2,1)S(1)}, u32[]{:S(2)}, u32[]{:S(2)}) collective-permute-start(bf16[384,256]{1,0:T(8,128)(2,1)S(1)} %get-tuple-element.17.refs_0_), channel_id=1, source_target_pairs={{0,2},{1,3},{2,4},{3,5},{4,6},{5,7},{8,10},{9,11},{10,12},{11,13},... | collective-permute-start | bytes 589832 | tf_op jit(solution)/shard_map/ppermute | solution.py:223
  5.0 12.2 %collective-permute-start.11 = (bf16[384,256]{1,0:T(8,128)(2,1)S(1)}, bf16[384,256]{1,0:T(8,128)(2,1)S(1)}, u32[]{:S(2)}, u32[]{:S(2)}) collective-permute-start(bf16[384,256]{1,0:T(8,128)(2,1)S(1)} %get-tuple-element.22.refs_0_), channel_id=1, source_target_pairs={{0,2},{1,3},{2,4},{3,5},{4,6},{5,7},{8,10},{9,11},{10,12},{11,13},... | collective-permute-start | bytes 589832 | tf_op jit(solution)/shard_map/ppermute | solution.py:223
  13.3 8.6 %collective-permute-start.3 = (bf16[384,256]{1,0:T(8,128)(2,1)S(1)}, bf16[384,256]{1,0:T(8,128)(2,1)S(1)}, u32[]{:S(2)}, u32[]{:S(2)}) collective-permute-start(bf16[384,256]{1,0:T(8,128)(2,1)S(1)} %collective-permute-done.1.refs_2_), channel_id=1, source_target_pairs={{0,2},{1,3},{2,4},{3,5},{4,6},{5,7},{8,10},{9,11},{10,12},{11,13},... | collective-permute-start | bytes 589832 | tf_op jit(solution)/shard_map/ppermute | solution.py:223
  17.1 9.7 %collective-permute-start.13 = (bf16[384,256]{1,0:T(8,128)(2,1)S(1)}, bf16[384,256]{1,0:T(8,128)(2,1)S(1)}, u32[]{:S(2)}, u32[]{:S(2)}) collective-permute-start(bf16[384,256]{1,0:T(8,128)(2,1)S(1)} %collective-permute-done.11.refs_2_), channel_id=1, source_target_pairs={{0,2},{1,3},{2,4},{3,5},{4,6},{5,7},{8,10},{9,11},{10,12},{11,13},... | collective-permute-start | bytes 589832 | tf_op jit(solution)/shard_map/ppermute | solution.py:223
  21.9 7.6 %collective-permute-start.5 = (bf16[384,256]{1,0:T(8,128)(2,1)S(1)}, bf16[384,256]{1,0:T(8,128)(2,1)S(1)}, u32[]{:S(2)}, u32[]{:S(2)}) collective-permute-start(bf16[384,256]{1,0:T(8,128)(2,1)S(1)} %collective-permute-done.3.refs_4_), channel_id=1, source_target_pairs={{0,2},{1,3},{2,4},{3,5},{4,6},{5,7},{8,10},{9,11},{10,12},{11,13},... | collective-permute-start | bytes 589832 | tf_op jit(solution)/shard_map/ppermute | solution.py:223
  23.2 6.3 %collective-permute-start = (bf16[384,256]{1,0:T(8,128)(2,1)S(1)}, bf16[384,256]{1,0:T(8,128)(2,1)S(1)}, u32[]{:S(2)}, u32[]{:S(2)}) collective-permute-start(bf16[384,256]{1,0:T(8,128)(2,1)S(1)} %get-tuple-element.17.refs_0_), channel_id=1, source_target_pairs={{0,1},{1,0},{2,3},{3,2},{4,5},{5,4},{6,7},{7,6},{8,9},{9,8},{10,11... | collective-permute-start | bytes 589832 | tf_op jit(solution)/shard_map/ppermute | solution.py:221
  23.3 6.7 %collective-permute-start.2 = (bf16[384,256]{1,0:T(8,128)(2,1)S(1)}, bf16[384,256]{1,0:T(8,128)(2,1)S(1)}, u32[]{:S(2)}, u32[]{:S(2)}) collective-permute-start(bf16[384,256]{1,0:T(8,128)(2,1)S(1)} %collective-permute-done.1.refs_2_), channel_id=1, source_target_pairs={{0,1},{1,0},{2,3},{3,2},{4,5},{5,4},{6,7},{7,6},{8,9},{9,8},{10,11... | collective-permute-start | bytes 589832 | tf_op jit(solution)/shard_map/ppermute | solution.py:224
  23.8 6.3 %collective-permute-start.4 = (bf16[384,256]{1,0:T(8,128)(2,1)S(1)}, bf16[384,256]{1,0:T(8,128)(2,1)S(1)}, u32[]{:S(2)}, u32[]{:S(2)}) collective-permute-start(bf16[384,256]{1,0:T(8,128)(2,1)S(1)} %collective-permute-done.3.refs_4_), channel_id=1, source_target_pairs={{0,1},{1,0},{2,3},{3,2},{4,5},{5,4},{6,7},{7,6},{8,9},{9,8},{10,11... | collective-permute-start | bytes 589832 | tf_op jit(solution)/shard_map/ppermute | solution.py:224
  26.8 7.6 %collective-permute-start.15 = (bf16[384,256]{1,0:T(8,128)(2,1)S(1)}, bf16[384,256]{1,0:T(8,128)(2,1)S(1)}, u32[]{:S(2)}, u32[]{:S(2)}) collective-permute-start(bf16[384,256]{1,0:T(8,128)(2,1)S(1)} %collective-permute-done.13.refs_4_), channel_id=1, source_target_pairs={{0,2},{1,3},{2,4},{3,5},{4,6},{5,7},{8,10},{9,11},{10,12},{11,13},... | collective-permute-start | bytes 589832 | tf_op jit(solution)/shard_map/ppermute | solution.py:223
  29.5 4.9 %collective-permute-start.6 = (bf16[384,256]{1,0:T(8,128)(2,1)S(1)}, bf16[384,256]{1,0:T(8,128)(2,1)S(1)}, u32[]{:S(2)}, u32[]{:S(2)}) collective-permute-start(bf16[384,256]{1,0:T(8,128)(2,1)S(1)} %collective-permute-done.5.refs_6_), channel_id=1, source_target_pairs={{0,1},{1,0},{2,3},{3,2},{4,5},{5,4},{6,7},{7,6},{8,9},{9,8},{10,11... | collective-permute-start | bytes 589832 | tf_op jit(solution)/shard_map/ppermute | solution.py:224
  29.5 22.4 %collective-permute-start.10 = (bf16[384,256]{1,0:T(8,128)(2,1)S(1)}, bf16[384,256]{1,0:T(8,128)(2,1)S(1)}, u32[]{:S(2)}, u32[]{:S(2)}) collective-permute-start(bf16[384,256]{1,0:T(8,128)(2,1)S(1)} %get-tuple-element.22.refs_0_), channel_id=1, source_target_pairs={{0,1},{1,0},{2,3},{3,2},{4,5},{5,4},{6,7},{7,6},{8,9},{9,8},{10,11... | collective-permute-start | bytes 589832 | tf_op jit(solution)/shard_map/ppermute | solution.py:221
  30.0 23.4 %collective-permute-start.12 = (bf16[384,256]{1,0:T(8,128)(2,1)S(1)}, bf16[384,256]{1,0:T(8,128)(2,1)S(1)}, u32[]{:S(2)}, u32[]{:S(2)}) collective-permute-start(bf16[384,256]{1,0:T(8,128)(2,1)S(1)} %collective-permute-done.11.refs_2_), channel_id=1, source_target_pairs={{0,1},{1,0},{2,3},{3,2},{4,5},{5,4},{6,7},{7,6},{8,9},{9,8},{10,11... | collective-permute-start | bytes 589832 | tf_op jit(solution)/shard_map/ppermute | solution.py:224
  30.1 23.8 %collective-permute-start.14 = (bf16[384,256]{1,0:T(8,128)(2,1)S(1)}, bf16[384,256]{1,0:T(8,128)(2,1)S(1)}, u32[]{:S(2)}, u32[]{:S(2)}) collective-permute-start(bf16[384,256]{1,0:T(8,128)(2,1)S(1)} %collective-permute-done.13.refs_4_), channel_id=1, source_target_pairs={{0,1},{1,0},{2,3},{3,2},{4,5},{5,4},{6,7},{7,6},{8,9},{9,8},{10,11... | collective-permute-start | bytes 589832 | tf_op jit(solution)/shard_map/ppermute | solution.py:224
  34.4 19.5 %collective-permute-start.16 = (bf16[384,256]{1,0:T(8,128)(2,1)S(1)}, bf16[384,256]{1,0:T(8,128)(2,1)S(1)}, u32[]{:S(2)}, u32[]{:S(2)}) collective-permute-start(bf16[384,256]{1,0:T(8,128)(2,1)S(1)} %collective-permute-done.15.refs_6_), channel_id=1, source_target_pairs={{0,1},{1,0},{2,3},{3,2},{4,5},{5,4},{6,7},{7,6},{8,9},{9,8},{10,11... | collective-permute-start | bytes 589832 | tf_op jit(solution)/shard_map/ppermute | solution.py:224
  34.4 1.4 %copy-start.3 = (bf16[384,2048]{1,0:T(8,128)(2,1)S(1)}, bf16[384,2048]{1,0:T(8,128)(2,1)}, u32[]{:S(2)}) copy-start(bf16[384,2048]{1,0:T(8,128)(2,1)} %q_ref.3) | copy-start | bytes 4718596
  50.3 21.2 %collective-permute-start.7 = (bf16[96,1024]{1,0:T(8,128)(2,1)S(1)}, bf16[96,1024]{1,0:T(8,128)(2,1)S(1)}, u32[]{:S(2)}, u32[]{:S(2)}) collective-permute-start(bf16[96,1024]{1,0:T(8,128)(2,1)S(1)} %get-tuple-element.19), channel_id=1, source_target_pairs={{0,8},{8,0},{16,24},{24,16},{1,9},{9,1},{17,25},{25,17},{2,10},{10... | collective-permute-start | bytes 589832 | tf_op jit(solution)/shard_map/ppermute | solution.py:228
  51.9 20.1 %collective-permute-start.8 = (bf16[96,1024]{1,0:T(8,128)(2,1)S(1)}, bf16[96,1024]{1,0:T(8,128)(2,1)S(1)}, u32[]{:S(2)}, u32[]{:S(2)}) collective-permute-start(bf16[96,1024]{1,0:T(8,128)(2,1)S(1)} %get-tuple-element.20), channel_id=1, source_target_pairs={{0,16},{8,24},{16,0},{24,8},{1,17},{9,25},{17,1},{25,9},{2,18},{10... | collective-permute-start | bytes 589832 | tf_op jit(solution)/shard_map/ppermute | solution.py:228
  53.4 18.6 %collective-permute-start.9 = (bf16[96,1024]{1,0:T(8,128)(2,1)S(1)}, bf16[96,1024]{1,0:T(8,128)(2,1)S(1)}, u32[]{:S(2)}, u32[]{:S(2)}) collective-permute-start(bf16[96,1024]{1,0:T(8,128)(2,1)S(1)} %get-tuple-element.21), channel_id=1, source_target_pairs={{0,24},{8,16},{16,8},{24,0},{1,25},{9,17},{17,9},{25,1},{2,26},{10... | collective-permute-start | bytes 589832 | tf_op jit(solution)/shard_map/ppermute | solution.py:228
  68.5 7.9 %collective-permute-start.17 = (bf16[96,1024]{1,0:T(8,128)(2,1)S(1)}, bf16[96,1024]{1,0:T(8,128)(2,1)S(1)}, u32[]{:S(2)}, u32[]{:S(2)}) collective-permute-start(bf16[96,1024]{1,0:T(8,128)(2,1)S(1)} %get-tuple-element.24), channel_id=1, source_target_pairs={{0,8},{8,0},{16,24},{24,16},{1,9},{9,1},{17,25},{25,17},{2,10},{10... | collective-permute-start | bytes 589832 | tf_op jit(solution)/shard_map/ppermute | solution.py:228
  70.0 10.4 %collective-permute-start.18 = (bf16[96,1024]{1,0:T(8,128)(2,1)S(1)}, bf16[96,1024]{1,0:T(8,128)(2,1)S(1)}, u32[]{:S(2)}, u32[]{:S(2)}) collective-permute-start(bf16[96,1024]{1,0:T(8,128)(2,1)S(1)} %get-tuple-element.25), channel_id=1, source_target_pairs={{0,16},{8,24},{16,0},{24,8},{1,17},{9,25},{17,1},{25,9},{2,18},{10... | collective-permute-start | bytes 589832 | tf_op jit(solution)/shard_map/ppermute | solution.py:228
  71.6 8.9 %collective-permute-start.19 = (bf16[96,1024]{1,0:T(8,128)(2,1)S(1)}, bf16[96,1024]{1,0:T(8,128)(2,1)S(1)}, u32[]{:S(2)}, u32[]{:S(2)}) collective-permute-start(bf16[96,1024]{1,0:T(8,128)(2,1)S(1)} %get-tuple-element.26), channel_id=1, source_target_pairs={{0,24},{8,16},{16,8},{24,0},{1,25},{9,17},{17,9},{25,1},{2,26},{10... | collective-permute-start | bytes 589832 | tf_op jit(solution)/shard_map/ppermute | solution.py:228

commit v2 on v1

v2 whole, which is shorter than its diff:
```python
import functools
import math

import jax
import jax.numpy as jnp
import numpy as np
from jax import lax
from jax.experimental import pallas as pl
from jax.experimental.pallas import tpu as pltpu
from jax.sharding import PartitionSpec as P

HD = 128
HALF = HD // 2
NEG_FILL = -1e30
EXP2_SCALE = math.log2(math.e) / math.sqrt(HD)
TOTAL_LIMIT = 2.0**100
TILE = 1536
ONES = 16
LIMIT = 24 << 20


def inverse_frequencies():
    base = 500000.0 ** (-2.0 * np.arange(HALF) / HD)
    wave = 2.0 * math.pi / base
    blend = (8192.0 / wave - 1.0) / 3.0
    middle = (1.0 - blend) * base / 8.0 + blend * base
    return np.where(wave < 2048.0, base, np.where(wave > 8192.0, base / 8.0, middle)).astype(np.float32)


def frequency_row():
    lane = lax.broadcasted_iota(jnp.int32, (1, HD), 1) % HALF
    row = jnp.zeros((1, HD), jnp.float32)
    for i, freq in enumerate(inverse_frequencies()):
        row = jnp.where(lane == i, float(freq), row)
    return row


def cos_sin(angle):
    turns = jnp.round(angle * (2.0 / math.pi))
    rest = angle - turns * 1.5703125
    rest = rest - turns * 4.837512969970703e-4
    rest = rest - turns * 7.54978995489188e-8
    quadrant = turns.astype(jnp.int32) & 3
    sq = rest * rest
    sine = rest + rest * sq * (-1.6666654611e-1 + sq * (8.3321608736e-3 - sq * 1.9515295891e-4))
    cosine = (
        1.0
        - 0.5 * sq
        + sq * sq * (4.166664568298827e-2 + sq * (-1.388731625493765e-3 + sq * 2.443315711809948e-5))
    )
    odd = (quadrant & 1) == 1
    cos_out = jnp.where(odd, sine, cosine)
    sin_out = jnp.where(odd, cosine, sine)
    cos_out = jnp.where((quadrant == 1) | (quadrant == 2), -cos_out, cos_out)
    sin_out = jnp.where(quadrant >= 2, -sin_out, sin_out)
    return cos_out, sin_out


def rotate(x, cosine, sine):
    return x * cosine + pltpu.roll(x, HALF, 1) * sine


def prep_kernel(heads, pos_hbm, k_hbm, v_hbm, table_ref, *refs):
    pack_refs, (pos_ref, k_ref, v_ref, sems) = refs[:heads], refs[heads:]
    pairs = [(pos_hbm, pos_ref), (k_hbm, k_ref), (v_hbm, v_ref)]
    loads = [pltpu.make_async_copy(src, dst, sems.at[i]) for i, (src, dst) in enumerate(pairs)]
    for load in loads:
        load.start()
    freq = frequency_row()
    loads[0].wait()
    tiles = [slice(t * HD, (t + 1) * HD) for t in range(k_ref.shape[0] // HD)]
    sign = jnp.where(lax.broadcasted_iota(jnp.int32, (HD, HD), 1) < HALF, -1.0, 1.0)
    tables = []
    for rows in tiles:
        pos = pos_ref[rows].reshape(1, HD).astype(jnp.float32)
        pos = jnp.broadcast_to(pos, (HD, HD)).T
        cosine, sine = cos_sin(pos * freq)
        sine = sine * sign
        table_ref[rows, :HD] = cosine
        table_ref[rows, HD:] = sine
        tables.append((cosine, sine))
    for load in loads[1:]:
        load.wait()
    for rows, (cosine, sine) in zip(tiles, tables, strict=True):
        for head in range(heads):
            cols = slice(head * HD, (head + 1) * HD)
            key = rotate(k_ref[rows, cols].astype(jnp.float32), cosine, sine)
            pack_refs[head][rows, :HD] = key.astype(jnp.bfloat16)
            pack_refs[head][rows, HD:] = v_ref[rows, cols].T


def prep(keys, values, positions):
    rows, cols = keys.shape
    heads = cols // HD
    vmem, hbm = pl.BlockSpec(memory_space=pltpu.VMEM), pl.BlockSpec(memory_space=pltpu.HBM)
    return pl.pallas_call(
        functools.partial(prep_kernel, heads),
        in_specs=[hbm] * 3,
        out_specs=[vmem] * (1 + heads),
        out_shape=[jax.ShapeDtypeStruct((rows, 2 * HD), jnp.float32)]
        + [jax.ShapeDtypeStruct((rows, 2 * HD), jnp.bfloat16)] * heads,
        scratch_shapes=[
            pltpu.VMEM(positions.shape, positions.dtype),
            pltpu.VMEM(keys.shape, keys.dtype),
            pltpu.VMEM(values.shape, values.dtype),
            pltpu.SemaphoreType.DMA((3,)),
        ],
        compiler_params=pltpu.CompilerParams(vmem_limit_bytes=16 << 20),
        cost_estimate=pl.CostEstimate(flops=10**10, bytes_accessed=10**7, transcendentals=0),
        name="prep",
    )(positions, keys, values)


def piece_starts(rows, parts):
    piece = rows // parts
    me = lax.axis_index("heads")
    return piece, [pl.multiple_of((me ^ k) * piece, piece) for k in range(parts)]


def values_of(blocks):
    tiles = [b[t : t + HD, HD:] for b in blocks for t in range(0, b.shape[0], HD)]
    values_t = jnp.concatenate(tiles, axis=1)
    return jnp.concatenate([values_t, jnp.ones((ONES, values_t.shape[1]), jnp.bfloat16)], axis=0)


def attend(state, blocks, allowed=None):
    queries_ref, shift_ref, total_ref, acc_ref = state
    width = queries_ref.shape[1]
    tile = min(TILE, width)

    def step(i, carry):
        cols = pl.ds(pl.multiple_of(i * tile, tile), tile)
        keys = [b[:, :HD] for b in blocks]
        keys = keys[0] if len(keys) == 1 else jnp.concatenate(keys, axis=0)
        s = jnp.dot(keys, queries_ref[:, cols], preferred_element_type=jnp.float32)
        if allowed is not None:
            s = jnp.where(jnp.concatenate([allowed] * (tile // allowed.shape[1]), 1), s, NEG_FILL)
        p = jnp.exp2(s * EXP2_SCALE - shift_ref[:, cols]).astype(jnp.bfloat16)
        mixed = jnp.dot(values_of(blocks), p, preferred_element_type=jnp.float32)
        if allowed is None:
            total_ref[:, cols] += mixed[HD : HD + 1]
            acc_ref[:, cols] += mixed[:HD]
        else:
            total_ref[:, cols] = mixed[HD : HD + 1]
            acc_ref[:, cols] = mixed[:HD]
        return carry

    lax.fori_loop(0, width // tile, step, 0)


def first_kernel(heads, group, parts, q_ref, table_ref, *refs):
    own_refs, out_refs = refs[:heads], refs[heads:]
    rows = q_ref.shape[0]
    piece, starts = piece_starts(rows, parts)
    table = jnp.concatenate([table_ref[pl.ds(s, piece), :] for s in starts], axis=0)
    lane = lax.broadcasted_iota(jnp.int32, (1, piece), 1)
    row_index = jnp.concatenate([lane + s for s in starts], axis=1)
    allowed = lax.broadcasted_iota(jnp.int32, (rows, rows), 0) <= row_index
    for head, own_ref in enumerate(own_refs):
        state = out_refs[4 * head : 4 * head + 4]
        queries_ref, shift_ref = state[:2]
        own_t = jnp.concatenate([own_ref[pl.ds(s, piece), :HD] for s in starts], axis=0)
        own_t = own_t.astype(jnp.float32).T
        for g in range(group):
            cols = slice((head * group + g) * HD, (head * group + g + 1) * HD)
            x = jnp.concatenate([q_ref[pl.ds(s, piece), cols] for s in starts], axis=0)
            x = rotate(x.astype(jnp.float32), table[:, :HD], table[:, HD:])
            x = x.T.astype(jnp.bfloat16)
            out = slice(g * rows, (g + 1) * rows)
            queries_ref[:, out] = x
            own_score = jnp.sum(x.astype(jnp.float32) * own_t, axis=0, keepdims=True)
            shift_ref[:, out] = own_score * EXP2_SCALE
        attend(state, [own_ref], allowed)


def attend_first(queries, table, owns, group, parts):
    rows = queries.shape[0]
    width = group * rows
    vmem = pl.BlockSpec(memory_space=pltpu.VMEM)
    flat = pl.pallas_call(
        functools.partial(first_kernel, len(owns), group, parts),
        in_specs=[vmem] * (2 + len(owns)),
        out_specs=[vmem] * (4 * len(owns)),
        out_shape=[
            jax.ShapeDtypeStruct((HD, width), jnp.bfloat16),
            jax.ShapeDtypeStruct((1, width), jnp.float32),
            jax.ShapeDtypeStruct((1, width), jnp.float32),
            jax.ShapeDtypeStruct((HD, width), jnp.float32),
        ]
        * len(owns),
        compiler_params=pltpu.CompilerParams(vmem_limit_bytes=LIMIT),
        cost_estimate=cost(width * len(owns), rows),
        name="attend_first",
    )(queries, table, *owns)
    return [tuple(flat[4 * h : 4 * h + 4]) for h in range(len(owns))]


def cost(width, keys):
    return pl.CostEstimate(flops=8 * width * keys * HD, bytes_accessed=0, transcendentals=0)


def attend_groups(groups, refs, state):
    rank = lax.axis_index("ctx")
    chip, core = rank // 2, rank % 2
    refs = list(refs)
    for step in groups:
        blocks = [refs.pop(0) for _ in range(1 if step == 0 else 2)]
        there = core == 1 if step == 0 else chip >= step
        pl.when(there)(functools.partial(attend, state, blocks))


def next_kernel(groups, queries_ref, shift_ref, total_in, acc_in, *refs):
    del total_in, acc_in
    attend_groups(groups, refs[:-2], (queries_ref, shift_ref, refs[-2], refs[-1]))


def attend_next(state, groups, blocks):
    queries, shift, total, acc = state
    vmem = pl.BlockSpec(memory_space=pltpu.VMEM)
    total, acc = pl.pallas_call(
        functools.partial(next_kernel, groups),
        in_specs=[vmem] * (4 + len(blocks)),
        out_specs=[vmem] * 2,
        out_shape=[jax.ShapeDtypeStruct(x.shape, x.dtype) for x in (total, acc)],
        input_output_aliases={2: 0, 3: 1},
        compiler_params=pltpu.CompilerParams(vmem_limit_bytes=LIMIT),
        cost_estimate=cost(queries.shape[1], sum(b.shape[0] for b in blocks)),
        name="attend_next",
    )(queries, shift, total, acc, *blocks)
    return queries, shift, total, acc


def recompute(rows, parts, queries_ref, every, total_ref, acc_ref, top_ref, blocks_ref, sems):
    rank = lax.axis_index("ctx")
    chip, core = rank // 2, rank % 2
    piece, starts = piece_starts(rows, parts)
    lane = lax.broadcasted_iota(jnp.int32, (1, piece), 1)
    row_index = jnp.concatenate([lane + s for s in starts], axis=1)
    key_index = lax.broadcasted_iota(jnp.int32, (rows, rows), 0)
    width = queries_ref.shape[1]
    copies = [
        pltpu.make_async_copy(ref, blocks_ref.at[pl.ds(b * rows, rows)], sems.at[b])
        for b, ref in enumerate(every)
    ]
    for copy in copies:
        copy.start()
    top_ref[...] = jnp.full(top_ref.shape, NEG_FILL, jnp.float32)
    total_ref[...] = jnp.zeros(total_ref.shape, jnp.float32)
    acc_ref[...] = jnp.zeros(acc_ref.shape, jnp.float32)
    for copy in copies:
        copy.wait()

    def block_step(b, carry):
        valid = jnp.where(b == 1, core == 1, chip >= b // 2)
        ahead = jnp.where(b == 0, 0, rows)
        block_ref = blocks_ref.at[pl.ds(pl.multiple_of(b * rows, rows), rows)]

        def tile_step(t, carry):
            cols = pl.ds(pl.multiple_of(t * rows, rows), rows)
            s = jnp.dot(block_ref[:, :HD], queries_ref[:, cols], preferred_element_type=jnp.float32)
            s = jnp.where(key_index - ahead <= row_index, s, NEG_FILL)
            top = jnp.maximum(top_ref[:, cols], jnp.max(s, axis=0, keepdims=True))
            p = jnp.exp2((s - top) * EXP2_SCALE)
            factor = jnp.exp2((top_ref[:, cols] - top) * EXP2_SCALE)
            mixed = jnp.dot(
                values_of([block_ref]), p.astype(jnp.bfloat16), preferred_element_type=jnp.float32
            )
            total_ref[:, cols] = total_ref[:, cols] * factor + mixed[HD : HD + 1]
            acc_ref[:, cols] = acc_ref[:, cols] * factor + mixed[:HD]
            top_ref[:, cols] = top
            return carry

        @pl.when(valid)
        def _():
            lax.fori_loop(0, width // rows, tile_step, 0)

        return carry

    lax.fori_loop(0, len(every), block_step, 0)


def last_kernel(groups, count, every_count, rows, parts, queries_ref, shift_ref, total_in, acc_in, *refs):
    refs = list(refs)
    blocks, refs = refs[:count], refs[count:]
    every, refs = refs[:every_count], refs[every_count:]
    out_refs, (total_ref, acc_ref, top_ref, blocks_ref, sems) = refs[:parts], refs[parts:]
    total_ref[...] = total_in[...]
    acc_ref[...] = acc_in[...]
    attend_groups(groups, blocks, (queries_ref, shift_ref, total_ref, acc_ref))
    in_range = jnp.max(total_ref[...]) <= TOTAL_LIMIT

    @pl.when(jnp.logical_not(in_range))
    def _():
        recompute(rows, parts, queries_ref, every, total_ref, acc_ref, top_ref, blocks_ref, sems)

    piece = rows // parts

    def finish(g, carry):
        cols = pl.ds(pl.multiple_of(g * rows, rows), rows)
        out = pl.ds(pl.multiple_of(g * HD, HD), HD)
        result = (acc_ref[:, cols] * (1.0 / total_ref[:, cols])).T.astype(jnp.bfloat16)
        for k in range(parts):
            out_refs[k][:, out] = result[k * piece : (k + 1) * piece]
        return carry

    lax.fori_loop(0, queries_ref.shape[1] // rows, finish, 0, unroll=True)


def attend_last(state, groups, blocks, every, parts):
    queries, shift, total, acc = state
    rows = every[0].shape[0]
    group = queries.shape[1] // rows
    vmem, anywhere = pl.BlockSpec(memory_space=pltpu.VMEM), pl.BlockSpec(memory_space=pl.ANY)
    return pl.pallas_call(
        functools.partial(last_kernel, groups, len(blocks), len(every), rows, parts),
        in_specs=[vmem] * (4 + len(blocks)) + [anywhere] * len(every),
        out_specs=[vmem] * parts,
        out_shape=[jax.ShapeDtypeStruct((rows // parts, group * HD), jnp.bfloat16)] * parts,
        scratch_shapes=[
            pltpu.VMEM(total.shape, jnp.float32),
            pltpu.VMEM(acc.shape, jnp.float32),
            pltpu.VMEM(total.shape, jnp.float32),
            pltpu.VMEM((len(every) * rows, 2 * HD), jnp.bfloat16),
            pltpu.SemaphoreType.DMA((len(every),)),
        ],
        compiler_params=pltpu.CompilerParams(vmem_limit_bytes=LIMIT),
        cost_estimate=cost(queries.shape[1], sum(b.shape[0] for b in blocks)),
        name="attend_last",
    )(queries, shift, total, acc, *blocks, *every)


def place_kernel(heads, parts, *refs):
    pieces, out_ref, sems = refs[: heads * parts], refs[-2], refs[-1]
    me = lax.axis_index("heads")
    copies = []
    for head in range(heads):
        for k in range(parts):
            src = pieces[head * parts + k]
            cols = src.shape[1]
            start = pl.multiple_of(((me ^ k) * heads + head) * cols, cols)
            copies.append(
                pltpu.make_async_copy(src, out_ref.at[:, pl.ds(start, cols)], sems.at[len(copies)])
            )
    for c in copies:
        c.start()
    for c in copies:
        c.wait()


def place(pieces, heads, parts):
    rows, cols = pieces[0].shape
    return pl.pallas_call(
        functools.partial(place_kernel, heads, parts),
        in_specs=[pl.BlockSpec(memory_space=pltpu.VMEM)] * len(pieces),
        out_specs=pl.BlockSpec(memory_space=pl.ANY),
        out_shape=jax.ShapeDtypeStruct((rows, cols * len(pieces)), jnp.bfloat16),
        compiler_params=pltpu.CompilerParams(vmem_limit_bytes=16 << 20),
        scratch_shapes=[pltpu.SemaphoreType.DMA((len(pieces),))],
        name="place",
    )(*pieces)


def after(value, *earlier):
    return lax.optimization_barrier((value, *earlier))[0]


def local(ctx_size, parts, queries, keys, values, positions):
    kv_heads = keys.shape[1] // HD
    group = queries.shape[1] // (kv_heads * HD)
    chips = ctx_size // 2
    heads = range(kv_heads)
    swap = [(c, c ^ 1) for c in range(ctx_size)]

    def upward(step, cross=0):
        low = 2 * (step - 1)
        top = [(c, (c + 2 if c + 2 < ctx_size else low + c % 2) ^ cross) for c in range(low, ctx_size)]
        return swap[:low] + top

    direct = chips > 3 and kv_heads > 1

    table, *packs = prep(keys, values, positions)
    near = [[pack, lax.ppermute(pack, "ctx", upward(1))] for pack in packs]
    far = [[lax.ppermute(pack, "ctx", swap)] for pack in packs]
    states = attend_first(queries, table, packs, group, parts)
    latest = [states[-1][2], *(far[h][0] for h in heads)]

    def pass_on(head, step, *earlier):
        block = after(near[head][step], *earlier)
        near[head][step] = block
        if step + 1 == chips - 1 and direct and head == kv_heads - 1:
            near[head].append(lax.ppermute(block, "ctx", upward(step + 1)))
            far[head].append(lax.ppermute(block, "ctx", swap))
            far[head].append(lax.ppermute(block, "ctx", upward(step + 1, 1)))
            return
        if step + 1 < chips:
            near[head].append(lax.ppermute(block, "ctx", upward(step + 1)))
        if len(far[head]) == step:
            far[head].append(lax.ppermute(block, "ctx", swap))

    def blocks_of(head, steps):
        out = []
        for s in steps:
            out += [far[head][0]] if s == 0 else [near[head][s], far[head][s]]
        return out

    def state_after(head, earlier):
        queries_t, shift, total, acc = states[head]
        return queries_t, shift, after(total, *earlier), acc

    order = [(0, [0, 1])] + [(0, [s]) for s in range(2, chips - 1)]
    for head in range(1, kv_heads):
        order += [(head, [0, 1])] + [(head, [s]) for s in range(2, chips - 2)]
    done = [0] * kv_heads
    pass_on(0, 1, *latest)
    latest = latest[:1] + [near[h][1] for h in heads]
    for i, (head, steps) in enumerate(order):
        states[head] = attend_next(state_after(head, latest), steps, blocks_of(head, steps))
        done[head] = steps[-1]
        latest = [states[head][2]]
        if done[head] + 1 < chips and (head == kv_heads - 1 or done[head] + 1 < chips - 1):
            pass_on(head, done[head] + 1, *latest)
            latest.append(far[head][done[head] + 1])
        elif head < kv_heads - 1:
            pass_on(head + 1, 1, *latest)
            pass_on(head, chips - 1, *latest)
            latest.append(far[head + 1][1])
    pieces = []
    sent = []
    for head in heads:
        if chips - done[head] > 2:
            steps = list(range(done[head] + 1, chips - 1))
            states[head] = attend_next(state_after(head, latest), steps, blocks_of(head, steps))
            done[head], latest = chips - 2, [states[head][2]]
        steps = list(range(done[head] + 1, chips))
        outs = attend_last(
            state_after(head, latest),
            steps,
            blocks_of(head, steps),
            [b for pair in zip(near[head], far[head], strict=True) for b in pair],
            parts,
        )
        latest = [outs[0]]
        out = [after(outs[k], *sent) if k else outs[k] for k in range(parts)]
        out[1:] = [lax.ppermute(out[k], "heads", [(i, i ^ k) for i in range(parts)]) for k in range(1, parts)]
        sent = out[1:2]
        pieces += out
    return place(pieces, kv_heads, parts)


def solution(mesh):
    return jax.shard_map(
        functools.partial(local, mesh.shape["ctx"], mesh.shape["heads"]),
        mesh=mesh,
        in_specs=(P("ctx", "heads"), P("ctx", "heads"), P("ctx", "heads"), P("ctx")),
        out_specs=P(("ctx", "heads"), None),
        check_vma=False,
    )
```

time: 82.9 us -> 58.8 us (0.71); the launches traced: 81.8 us -> 58.6 us
  waiting for transfers between devices: 29.7 us -> 20.2 us
  Pallas kernels: 30.7 us -> 22.3 us
  starting transfers between devices: 16.5 us -> 13.2 us
  local copies, waits for them, and re-layouts: 4.6 us -> 2.54 us
    ppermute x20, waiting for transfers between devices: 29.7 us -> 20.2 us  [the longest x6 9.63 us: local(): lax.ppermute(out[k], 'heads', [(i, i ^ k) for i in range(parts)])]
    pallas_call x3 -> x8, Pallas kernels: 29.5 us -> 21.1 us  [the longest x4 9.27 us: attend_next(): pl.pallas_call(functools.partial(next_kernel, groups), in_specs=[vmem] *...]
    ppermute x20, starting transfers between devices: 16.5 us -> 13.2 us  [the longest x6 7.11 us: local(): lax.ppermute(out[k], 'heads', [(i, i ^ k) for i in range(parts)])]
    unnamed x8, local copies, waits for them, and re-layouts: 3.91 us -> 2.54 us
  transfers between devices with their start and end apart: 20 -> 20, of which waited for: 8 -> 9; matrix products, arithmetic and copies ran while one was open for 0% -> 0% of each run, Pallas kernels for 36% -> 34%
where the time goes in v2:
time: 58.8 us; the launch traced here: 58.6 us
  Pallas kernels  22.3 us (38%)
  waiting for transfers between devices  20.2 us (34%)
  starting transfers between devices  13.2 us (22%)
  local copies, waits for them, and re-layouts  2.54 us (4%)
    ppermute x6, waiting for transfers between devices, local(): lax.ppermute(out[k], 'heads', [(i, i ^ k) for i in range(parts)])  9.63 us
    pallas_call x4, Pallas kernels, attend_next(): pl.pallas_call(functools.partial(next_kernel, groups), in_specs=[vmem] *...  9.27 us
    ppermute x4, waiting for transfers between devices, pass_on(): near[head].append(lax.ppermute(block, 'ctx', upward(step + 1)))  7.18 us
    ppermute x6, starting transfers between devices, local(): lax.ppermute(out[k], 'heads', [(i, i ^ k) for i in range(parts)])  7.11 us
    pallas_call x2, Pallas kernels, attend_last(): pl.pallas_call(functools.partial(last_kernel, groups, len(blocks), len(ev...  5.94 us
    pallas_call x1, Pallas kernels, attend_first(): pl.pallas_call(functools.partial(first_kernel, len(owns), group, parts),...  4.86 us
    unnamed x8, local copies, waits for them, and re-layouts  2.54 us
    ppermute x2, waiting for transfers between devices, local(): near = [[pack, lax.ppermute(pack, 'ctx', upward(1))] for pack in packs]  2.42 us
  transfers between devices with their start and end apart: 20, of which 9 were waited for; matrix products, arithmetic and copies ran while one was open for 0% of the time, Pallas kernels for 34%

profile of v2, /device:TPU:24, one launch (start us, length us, event | category | flops | bytes accessed | tf_op | source)
XLA Modules:
  0.0 58.6 jit_solution(11930607722998023320)
XLA Ops:
  0.0 0.0 copy-start.1
  0.0 0.9 %copy-done.1 = bf16[384,256]{1,0:T(8,128)(2,1)S(1)} copy-done((bf16[384,256]{1,0:T(8,128)(2,1)S(1)}, bf16[384,256]{1,0:T(8,128)(2,1)}, u32[]{:S(2)}) %copy-start.1) | copy-done | bytes 196632
  0.9 0.0 copy-start.2
  0.9 0.9 %copy-done.2 = bf16[384,256]{1,0:T(8,128)(2,1)S(1)} copy-done((bf16[384,256]{1,0:T(8,128)(2,1)S(1)}, bf16[384,256]{1,0:T(8,128)(2,1)}, u32[]{:S(2)}) %copy-start.2) | copy-done | bytes 196632
  1.9 0.0 copy-start.3
  1.9 0.7 %copy-done.3 = s32[384]{0:T(512)S(1)} copy-done((s32[384]{0:T(512)S(1)}, s32[384]{0:T(512)}, u32[]{:S(2)}) %copy-start.3) | copy-done | bytes 1560
  2.5 0.0 copy-start
  2.5 1.1 %prep.1 = (f32[384,256]{1,0:T(8,128)S(1)}, bf16[384,256]{1,0:T(8,128)(2,1)S(1)}, bf16[384,256]{1,0:T(8,128)(2,1)S(1)}) custom-call(s32[384]{0:T(512)S(1)} %copy-done.3, bf16[384,256]{1,0:T(8,128)(2,1)S(1)} %copy-done.1, bf16[384,256]{1,0:T(8,128)(2,1)S(1)} %copy-done.2), custom_call_target="tpu_custom_call" | custom-call | flops 10000000000 | bytes 10000000 | tf_op jit(solution)/shard_map/prep/pallas_call | solution.py:96
  3.6 0.1 collective-permute-start
  3.7 0.1 collective-permute-start.1
  3.8 0.5 collective-permute-start.2
  4.3 1.7 %collective-permute-start.3 = (bf16[384,256]{1,0:T(8,128)(2,1)S(1)}, bf16[384,256]{1,0:T(8,128)(2,1)S(1)}, u32[]{:S(2)}, u32[]{:S(2)}) collective-permute-start(bf16[384,256]{1,0:T(8,128)(2,1)S(1)} %get-tuple-element.47.refs_1_.refs_2_), channel_id=1, source_target_pairs={{0,2},{1,3},{2,4},{3,5},{4,6},{5,7},{6,0},{7,1},{8,10},{9,11},{10,... | collective-permute-start | bytes 589832 | tf_op jit(solution)/shard_map/ppermute | solution.py:382
  6.0 0.0 copy-done
  6.0 4.9 %attend_first.1 = (bf16[128,3072]{1,0:T(8,128)(2,1)S(1)}, f32[1,3072]{1,0:T(1,128)S(1)}, f32[1,3072]{1,0:T(1,128)S(1)}, f32[128,3072]{1,0:T(8,128)S(1)}, bf16[12...) custom-call(bf16[384,2048]{1,0:T(8,128)(2,1)S(1)} %copy-done, ...), custom_call_target="tpu_custom_call" | custom-call | flops 2415919104 | tf_op jit(solution)/shard_map/attend_first/pallas_call | solution.py:180
  10.8 0.6 %collective-permute-done.refs_1_.refs_4_ = bf16[384,256]{1,0:T(8,128)(2,1)S(1)} collective-permute-done((bf16[384,256]{1,0:T(8,128)(2,1)S(1)}, bf16[384,256]{1,0:T(8,128)(2,1)S(1)}, u32[]{:S(2)}, u32[]{:S(2)}) %collective-permute-start) | collective-permute-done | bytes 196640 | tf_op jit(solution)/shard_map/ppermute | solution.py:382
  11.5 0.0 collective-permute-done.1.refs_0_.refs_3_
  11.5 0.0 collective-permute-done.2.refs_0_.refs_3_
  11.5 0.0 collective-permute-start.4
  11.5 1.2 %collective-permute-start.5 = (bf16[384,256]{1,0:T(8,128)(2,1)S(1)}, bf16[384,256]{1,0:T(8,128)(2,1)S(1)}, u32[]{:S(2)}, u32[]{:S(2)}) collective-permute-start(bf16[384,256]{1,0:T(8,128)(2,1)S(1)} %collective-permute-done.refs_1_.refs_4_), channel_id=1, source_target_pairs={{0,1},{1,0},{2,4},{3,5},{4,6},{5,7},{6,2},{7,3},{8,9},{9,8},{10,12... | collective-permute-start | bytes 589832 | tf_op jit(solution)/shard_map/ppermute | solution.py:396
  12.7 1.8 %collective-permute-done.3.refs_1_.refs_4_ = bf16[384,256]{1,0:T(8,128)(2,1)S(1)} collective-permute-done((bf16[384,256]{1,0:T(8,128)(2,1)S(1)}, bf16[384,256]{1,0:T(8,128)(2,1)S(1)}, u32[]{:S(2)}, u32[]{:S(2)}) %collective-permute-start.3) | collective-permute-done | bytes 196640 | tf_op jit(solution)/shard_map/ppermute | solution.py:382
  14.5 0.0 collective-permute-done.4.refs_2_.refs_5_
  14.5 2.3 %attend_next.4 = (f32[1,3072]{1,0:T(1,128)S(1)}, f32[128,3072]{1,0:T(8,128)S(1)}) custom-call(bf16[128,3072]{1,0:T(8,128)(2,1)S(1)} %get-tuple-element.48.queries_ref, f32[1,3072]{1,0:T(1,128)S(1)} %get-tuple-element.49.shift_ref, f32[1,3072]{1,0:T(1,128)S(1)} %get-tuple-element.53.total_in, ...), custom_call_target="tpu_custom_call", output_to_operand_aliasing={{0}: (2, {}), {1}: (3, {})} | custom-call | flops 3623878656 | tf_op jit(solution)/shard_map/attend_next/pallas_call | solution.py:220
  16.8 1.9 %collective-permute-done.5.refs_0_.refs_6_ = bf16[384,256]{1,0:T(8,128)(2,1)S(1)} collective-permute-done((bf16[384,256]{1,0:T(8,128)(2,1)S(1)}, bf16[384,256]{1,0:T(8,128)(2,1)S(1)}, u32[]{:S(2)}, u32[]{:S(2)}) %collective-permute-start.5) | collective-permute-done | bytes 196640 | tf_op jit(solution)/shard_map/ppermute | solution.py:396
  18.8 0.0 collective-permute-start.6
  18.8 0.5 collective-permute-start.10
  19.2 1.0 %collective-permute-done.6.refs_1_.refs_7_ = bf16[384,256]{1,0:T(8,128)(2,1)S(1)} collective-permute-done((bf16[384,256]{1,0:T(8,128)(2,1)S(1)}, bf16[384,256]{1,0:T(8,128)(2,1)S(1)}, u32[]{:S(2)}, u32[]{:S(2)}) %collective-permute-start.6) | collective-permute-done | bytes 196640 | tf_op jit(solution)/shard_map/ppermute | solution.py:398
  20.2 2.3 %attend_next.5 = (f32[1,3072]{1,0:T(1,128)S(1)}, f32[128,3072]{1,0:T(8,128)S(1)}) custom-call(bf16[128,3072]{1,0:T(8,128)(2,1)S(1)} %get-tuple-element.48.queries_ref, f32[1,3072]{1,0:T(1,128)S(1)} %get-tuple-element.49.shift_ref, f32[1,3072]{1,0:T(1,128)S(1)} %get-tuple-element.57.total_in, ...), custom_call_target="tpu_custom_call", output_to_operand_aliasing={{0}: (2, {}), {1}: (3, {})} | custom-call | flops 2415919104 | tf_op jit(solution)/shard_map/attend_next/pallas_call | solution.py:220
  22.6 0.2 collective-permute-start.7
  22.8 0.0 collective-permute-start.8
  22.8 3.6 %collective-permute-done.10.refs_0_.refs_8_ = bf16[384,256]{1,0:T(8,128)(2,1)S(1)} collective-permute-done((bf16[384,256]{1,0:T(8,128)(2,1)S(1)}, bf16[384,256]{1,0:T(8,128)(2,1)S(1)}, u32[]{:S(2)}, u32[]{:S(2)}) %collective-permute-start.10) | collective-permute-done | bytes 196640 | tf_op jit(solution)/shard_map/ppermute | solution.py:396
  26.4 0.0 collective-permute-done.7.refs_2_.refs_5_
  26.4 2.3 %attend_next.6 = (f32[1,3072]{1,0:T(1,128)S(1)}, f32[128,3072]{1,0:T(8,128)S(1)}) custom-call(bf16[128,3072]{1,0:T(8,128)(2,1)S(1)} %get-tuple-element.60.queries_ref, f32[1,3072]{1,0:T(1,128)S(1)} %get-tuple-element.61.shift_ref, f32[1,3072]{1,0:T(1,128)S(1)} %get-tuple-element.63.total_in, ...), custom_call_target="tpu_custom_call", output_to_operand_aliasing={{0}: (2, {}), {1}: (3, {})} | custom-call | flops 3623878656 | tf_op jit(solution)/shard_map/attend_next/pallas_call | solution.py:220
  28.7 1.6 %collective-permute-done.8.refs_0_.refs_6_ = bf16[384,256]{1,0:T(8,128)(2,1)S(1)} collective-permute-done((bf16[384,256]{1,0:T(8,128)(2,1)S(1)}, bf16[384,256]{1,0:T(8,128)(2,1)S(1)}, u32[]{:S(2)}, u32[]{:S(2)}) %collective-permute-start.8) | collective-permute-done | bytes 196640 | tf_op jit(solution)/shard_map/ppermute | solution.py:396
  30.3 0.0 collective-permute-start.9
  30.3 0.5 collective-permute-start.11
  30.8 0.2 collective-permute-start.15
  31.1 1.1 %collective-permute-start.16 = (bf16[384,256]{1,0:T(8,128)(2,1)S(1)}, bf16[384,256]{1,0:T(8,128)(2,1)S(1)}, u32[]{:S(2)}, u32[]{:S(2)}) collective-permute-start(bf16[384,256]{1,0:T(8,128)(2,1)S(1)} %collective-permute-done.8.refs_0_.refs_6_), channel_id=1, source_target_pairs={{0,1},{1,0},{2,3},{3,2},{4,7},{5,6},{6,5},{7,4},{8,9},{9,8},{10,11... | collective-permute-start | bytes 589832 | tf_op jit(solution)/shard_map/ppermute | solution.py:393
  32.2 0.0 collective-permute-done.9.refs_1_.refs_7_
  32.2 0.0 collective-permute-done.11.refs_1_.refs_9_
  32.2 3.0 %attend_last.2 = (bf16[96,1024]{1,0:T(8,128)(2,1)S(1)}, bf16[96,1024]{1,0:T(8,128)(2,1)S(1)}, bf16[96,1024]{1,0:T(8,128)(2,1)S(1)}, bf16[96,1024]{1,0:T(8,128)(2,1)S(1)}) custom-call(bf16[128,3072]{1,0:T(8,128)(2,1)S(1)} %get-tuple-element.48.queries_ref, f32[1,3072]{1,0:T(1,128)S(1)} %get-tuple-element.49.shift_ref, ...), custom_call_target="tpu_custom_call" | custom-call | flops 2415919104 | tf_op jit(solution)/shard_map/attend_last/pallas_call | solution.py:314
  35.1 1.6 %collective-permute-start.12 = (bf16[96,1024]{1,0:T(8,128)(2,1)S(1)}, bf16[96,1024]{1,0:T(8,128)(2,1)S(1)}, u32[]{:S(2)}, u32[]{:S(2)}) collective-permute-start(bf16[96,1024]{1,0:T(8,128)(2,1)S(1)} %get-tuple-element.71), channel_id=1, source_target_pairs={{0,8},{8,0},{16,24},{24,16},{1,9},{9,1},{17,25},{25,17},{2,10},{10... | collective-permute-start | bytes 589832 | tf_op jit(solution)/shard_map/ppermute | solution.py:444
  36.7 1.5 %collective-permute-start.13 = (bf16[96,1024]{1,0:T(8,128)(2,1)S(1)}, bf16[96,1024]{1,0:T(8,128)(2,1)S(1)}, u32[]{:S(2)}, u32[]{:S(2)}) collective-permute-start(bf16[96,1024]{1,0:T(8,128)(2,1)S(1)} %get-tuple-element.72), channel_id=1, source_target_pairs={{0,16},{8,24},{16,0},{24,8},{1,17},{9,25},{17,1},{25,9},{2,18},{10... | collective-permute-start | bytes 589832 | tf_op jit(solution)/shard_map/ppermute | solution.py:444
  38.2 0.5 collective-permute-start.14
  38.7 2.3 %attend_next.7 = (f32[1,3072]{1,0:T(1,128)S(1)}, f32[128,3072]{1,0:T(8,128)S(1)}) custom-call(bf16[128,3072]{1,0:T(8,128)(2,1)S(1)} %get-tuple-element.60.queries_ref, f32[1,3072]{1,0:T(1,128)S(1)} %get-tuple-element.61.shift_ref, f32[1,3072]{1,0:T(1,128)S(1)} %get-tuple-element.74.total_in, ...), custom_call_target="tpu_custom_call", output_to_operand_aliasing={{0}: (2, {}), {1}: (3, {})} | custom-call | flops 2415919104 | tf_op jit(solution)/shard_map/attend_next/pallas_call | solution.py:220
  41.0 0.0 collective-permute-done.15.refs_0_.refs_8_
  41.1 0.0 collective-permute-done.16.refs_1_.refs_9_
  41.1 3.0 %attend_last.3 = (bf16[96,1024]{1,0:T(8,128)(2,1)S(1)}, bf16[96,1024]{1,0:T(8,128)(2,1)S(1)}, bf16[96,1024]{1,0:T(8,128)(2,1)S(1)}, bf16[96,1024]{1,0:T(8,128)(2,1)S(1)}) custom-call(bf16[128,3072]{1,0:T(8,128)(2,1)S(1)} %get-tuple-element.60.queries_ref, f32[1,3072]{1,0:T(1,128)S(1)} %get-tuple-element.61.shift_ref, ...), custom_call_target="tpu_custom_call" | custom-call | flops 2415919104 | tf_op jit(solution)/shard_map/attend_last/pallas_call | solution.py:314
  44.1 0.0 collective-permute-done.12.refs_1_
  44.1 1.6 %collective-permute-start.17 = (bf16[96,1024]{1,0:T(8,128)(2,1)S(1)}, bf16[96,1024]{1,0:T(8,128)(2,1)S(1)}, u32[]{:S(2)}, u32[]{:S(2)}) collective-permute-start(bf16[96,1024]{1,0:T(8,128)(2,1)S(1)} %get-tuple-element.80), channel_id=1, source_target_pairs={{0,8},{8,0},{16,24},{24,16},{1,9},{9,1},{17,25},{25,17},{2,10},{10... | collective-permute-start | bytes 589832 | tf_op jit(solution)/shard_map/ppermute | solution.py:444
  45.6 1.5 %collective-permute-start.18 = (bf16[96,1024]{1,0:T(8,128)(2,1)S(1)}, bf16[96,1024]{1,0:T(8,128)(2,1)S(1)}, u32[]{:S(2)}, u32[]{:S(2)}) collective-permute-start(bf16[96,1024]{1,0:T(8,128)(2,1)S(1)} %get-tuple-element.82), channel_id=1, source_target_pairs={{0,16},{8,24},{16,0},{24,8},{1,17},{9,25},{17,1},{25,9},{2,18},{10... | collective-permute-start | bytes 589832 | tf_op jit(solution)/shard_map/ppermute | solution.py:444
  47.1 0.5 collective-permute-start.19
  47.6 0.6 %collective-permute-done.13.refs_2_ = bf16[96,1024]{1,0:T(8,128)(2,1)S(1)} collective-permute-done((bf16[96,1024]{1,0:T(8,128)(2,1)S(1)}, bf16[96,1024]{1,0:T(8,128)(2,1)S(1)}, u32[]{:S(2)}, u32[]{:S(2)}) %collective-permute-start.13) | collective-permute-done | bytes 196640 | tf_op jit(solution)/shard_map/ppermute | solution.py:444
  48.2 0.0 collective-permute-done.14.refs_3_
  48.2 3.7 %collective-permute-done.17.refs_5_ = bf16[96,1024]{1,0:T(8,128)(2,1)S(1)} collective-permute-done((bf16[96,1024]{1,0:T(8,128)(2,1)S(1)}, bf16[96,1024]{1,0:T(8,128)(2,1)S(1)}, u32[]{:S(2)}, u32[]{:S(2)}) %collective-permute-start.17) | collective-permute-done | bytes 196640 | tf_op jit(solution)/shard_map/ppermute | solution.py:444
  51.9 5.3 %collective-permute-done.18.refs_6_ = bf16[96,1024]{1,0:T(8,128)(2,1)S(1)} collective-permute-done((bf16[96,1024]{1,0:T(8,128)(2,1)S(1)}, bf16[96,1024]{1,0:T(8,128)(2,1)S(1)}, u32[]{:S(2)}, u32[]{:S(2)}) %collective-permute-start.18) | collective-permute-done | bytes 196640 | tf_op jit(solution)/shard_map/ppermute | solution.py:444
  57.3 0.0 collective-permute-done.19.refs_7_
  57.3 1.2 %place.1 = bf16[96,8192]{1,0:T(8,128)(2,1)} custom-call(bf16[96,1024]{1,0:T(8,128)(2,1)S(1)} %get-tuple-element.70.refs_0_, bf16[96,1024]{1,0:T(8,128)(2,1)S(1)} %collective-permute-done.12.refs_1_, bf16[96,1024]{1,0:T(8,128)(2,1)S(1)} %collective-permute-done.13.refs_2_, bf16[96,1024]{1,0:T(8,128)(2,1)S(1)} %collective-permute-done.14.refs_3_, ...), custom_call_target="tpu_custom_call" | custom-call | tf_op jit(solution)/shard_map/place/pallas_call | solution.py:352
Async XLA Ops:
  0.0 0.9 %copy-start.1 = (bf16[384,256]{1,0:T(8,128)(2,1)S(1)}, bf16[384,256]{1,0:T(8,128)(2,1)}, u32[]{:S(2)}) copy-start(bf16[384,256]{1,0:T(8,128)(2,1)} %k_hbm.1) | copy-start | bytes 589828
  0.9 0.9 %copy-start.2 = (bf16[384,256]{1,0:T(8,128)(2,1)S(1)}, bf16[384,256]{1,0:T(8,128)(2,1)}, u32[]{:S(2)}) copy-start(bf16[384,256]{1,0:T(8,128)(2,1)} %v_hbm.1) | copy-start | bytes 589828
  1.9 0.7 %copy-start.3 = (s32[384]{0:T(512)S(1)}, s32[384]{0:T(512)}, u32[]{:S(2)}) copy-start(s32[384]{0:T(512)} %pos_hbm.1) | copy-start | bytes 4612
  2.5 3.4 %copy-start = (bf16[384,2048]{1,0:T(8,128)(2,1)S(1)}, bf16[384,2048]{1,0:T(8,128)(2,1)}, u32[]{:S(2)}) copy-start(bf16[384,2048]{1,0:T(8,128)(2,1)} %q_ref.1) | copy-start | bytes 4718596
  3.6 7.8 %collective-permute-start = (bf16[384,256]{1,0:T(8,128)(2,1)S(1)}, bf16[384,256]{1,0:T(8,128)(2,1)S(1)}, u32[]{:S(2)}, u32[]{:S(2)}) collective-permute-start(bf16[384,256]{1,0:T(8,128)(2,1)S(1)} %get-tuple-element.46.refs_0_.refs_2_), channel_id=1, source_target_pairs={{0,2},{1,3},{2,4},{3,5},{4,6},{5,7},{6,0},{7,1},{8,10},{9,11},{10,... | collective-permute-start | bytes 589832 | tf_op jit(solution)/shard_map/ppermute | solution.py:382
  3.7 7.8 %collective-permute-start.1 = (bf16[384,256]{1,0:T(8,128)(2,1)S(1)}, bf16[384,256]{1,0:T(8,128)(2,1)S(1)}, u32[]{:S(2)}, u32[]{:S(2)}) collective-permute-start(bf16[384,256]{1,0:T(8,128)(2,1)S(1)} %get-tuple-element.46.refs_0_.refs_2_), channel_id=1, source_target_pairs={{0,1},{1,0},{2,3},{3,2},{4,5},{5,4},{6,7},{7,6},{8,9},{9,8},{10,11... | collective-permute-start | bytes 589832 | tf_op jit(solution)/shard_map/ppermute | solution.py:383
  3.8 7.7 %collective-permute-start.2 = (bf16[384,256]{1,0:T(8,128)(2,1)S(1)}, bf16[384,256]{1,0:T(8,128)(2,1)S(1)}, u32[]{:S(2)}, u32[]{:S(2)}) collective-permute-start(bf16[384,256]{1,0:T(8,128)(2,1)S(1)} %get-tuple-element.47.refs_1_.refs_2_), channel_id=1, source_target_pairs={{0,1},{1,0},{2,3},{3,2},{4,5},{5,4},{6,7},{7,6},{8,9},{9,8},{10,11... | collective-permute-start | bytes 589832 | tf_op jit(solution)/shard_map/ppermute | solution.py:383
  4.3 10.3 %collective-permute-start.3 = (bf16[384,256]{1,0:T(8,128)(2,1)S(1)}, bf16[384,256]{1,0:T(8,128)(2,1)S(1)}, u32[]{:S(2)}, u32[]{:S(2)}) collective-permute-start(bf16[384,256]{1,0:T(8,128)(2,1)S(1)} %get-tuple-element.47.refs_1_.refs_2_), channel_id=1, source_target_pairs={{0,2},{1,3},{2,4},{3,5},{4,6},{5,7},{6,0},{7,1},{8,10},{9,11},{10,... | collective-permute-start | bytes 589832 | tf_op jit(solution)/shard_map/ppermute | solution.py:382
  11.5 3.1 %collective-permute-start.4 = (bf16[384,256]{1,0:T(8,128)(2,1)S(1)}, bf16[384,256]{1,0:T(8,128)(2,1)S(1)}, u32[]{:S(2)}, u32[]{:S(2)}) collective-permute-start(bf16[384,256]{1,0:T(8,128)(2,1)S(1)} %collective-permute-done.refs_1_.refs_4_), channel_id=1, source_target_pairs={{0,1},{1,0},{2,3},{3,2},{4,5},{5,4},{6,7},{7,6},{8,9},{9,8},{10,11... | collective-permute-start | bytes 589832 | tf_op jit(solution)/shard_map/ppermute | solution.py:398
  11.5 7.3 %collective-permute-start.5 = (bf16[384,256]{1,0:T(8,128)(2,1)S(1)}, bf16[384,256]{1,0:T(8,128)(2,1)S(1)}, u32[]{:S(2)}, u32[]{:S(2)}) collective-permute-start(bf16[384,256]{1,0:T(8,128)(2,1)S(1)} %collective-permute-done.refs_1_.refs_4_), channel_id=1, source_target_pairs={{0,1},{1,0},{2,4},{3,5},{4,6},{5,7},{6,2},{7,3},{8,9},{9,8},{10,12... | collective-permute-start | bytes 589832 | tf_op jit(solution)/shard_map/ppermute | solution.py:396
  18.8 1.4 %collective-permute-start.6 = (bf16[384,256]{1,0:T(8,128)(2,1)S(1)}, bf16[384,256]{1,0:T(8,128)(2,1)S(1)}, u32[]{:S(2)}, u32[]{:S(2)}) collective-permute-start(bf16[384,256]{1,0:T(8,128)(2,1)S(1)} %collective-permute-done.5.refs_0_.refs_6_), channel_id=1, source_target_pairs={{0,1},{1,0},{2,3},{3,2},{4,5},{5,4},{6,7},{7,6},{8,9},{9,8},{10,11... | collective-permute-start | bytes 589832 | tf_op jit(solution)/shard_map/ppermute | solution.py:398
  18.8 7.6 %collective-permute-start.10 = (bf16[384,256]{1,0:T(8,128)(2,1)S(1)}, bf16[384,256]{1,0:T(8,128)(2,1)S(1)}, u32[]{:S(2)}, u32[]{:S(2)}) collective-permute-start(bf16[384,256]{1,0:T(8,128)(2,1)S(1)} %collective-permute-done.5.refs_0_.refs_6_), channel_id=1, source_target_pairs={{0,1},{1,0},{2,3},{3,2},{4,6},{5,7},{6,4},{7,5},{8,9},{9,8},{10,11... | collective-permute-start | bytes 589832 | tf_op jit(solution)/shard_map/ppermute | solution.py:396
  22.6 3.8 %collective-permute-start.7 = (bf16[384,256]{1,0:T(8,128)(2,1)S(1)}, bf16[384,256]{1,0:T(8,128)(2,1)S(1)}, u32[]{:S(2)}, u32[]{:S(2)}) collective-permute-start(bf16[384,256]{1,0:T(8,128)(2,1)S(1)} %collective-permute-done.3.refs_1_.refs_4_), channel_id=1, source_target_pairs={{0,1},{1,0},{2,3},{3,2},{4,5},{5,4},{6,7},{7,6},{8,9},{9,8},{10,11... | collective-permute-start | bytes 589832 | tf_op jit(solution)/shard_map/ppermute | solution.py:398
  22.8 7.5 %collective-permute-start.8 = (bf16[384,256]{1,0:T(8,128)(2,1)S(1)}, bf16[384,256]{1,0:T(8,128)(2,1)S(1)}, u32[]{:S(2)}, u32[]{:S(2)}) collective-permute-start(bf16[384,256]{1,0:T(8,128)(2,1)S(1)} %collective-permute-done.3.refs_1_.refs_4_), channel_id=1, source_target_pairs={{0,1},{1,0},{2,4},{3,5},{4,6},{5,7},{6,2},{7,3},{8,9},{9,8},{10,12... | collective-permute-start | bytes 589832 | tf_op jit(solution)/shard_map/ppermute | solution.py:396
  30.3 1.9 %collective-permute-start.9 = (bf16[384,256]{1,0:T(8,128)(2,1)S(1)}, bf16[384,256]{1,0:T(8,128)(2,1)S(1)}, u32[]{:S(2)}, u32[]{:S(2)}) collective-permute-start(bf16[384,256]{1,0:T(8,128)(2,1)S(1)} %collective-permute-done.8.refs_0_.refs_6_), channel_id=1, source_target_pairs={{0,1},{1,0},{2,3},{3,2},{4,5},{5,4},{6,7},{7,6},{8,9},{9,8},{10,11... | collective-permute-start | bytes 589832 | tf_op jit(solution)/shard_map/ppermute | solution.py:392
  30.3 1.9 %collective-permute-start.11 = (bf16[384,256]{1,0:T(8,128)(2,1)S(1)}, bf16[384,256]{1,0:T(8,128)(2,1)S(1)}, u32[]{:S(2)}, u32[]{:S(2)}) collective-permute-start(bf16[384,256]{1,0:T(8,128)(2,1)S(1)} %collective-permute-done.10.refs_0_.refs_8_), channel_id=1, source_target_pairs={{0,1},{1,0},{2,3},{3,2},{4,5},{5,4},{6,7},{7,6},{8,9},{9,8},{10,11... | collective-permute-start | bytes 589832 | tf_op jit(solution)/shard_map/ppermute | solution.py:398
  30.8 10.2 %collective-permute-start.15 = (bf16[384,256]{1,0:T(8,128)(2,1)S(1)}, bf16[384,256]{1,0:T(8,128)(2,1)S(1)}, u32[]{:S(2)}, u32[]{:S(2)}) collective-permute-start(bf16[384,256]{1,0:T(8,128)(2,1)S(1)} %collective-permute-done.8.refs_0_.refs_6_), channel_id=1, source_target_pairs={{0,1},{1,0},{2,3},{3,2},{4,6},{5,7},{6,4},{7,5},{8,9},{9,8},{10,11... | collective-permute-start | bytes 589832 | tf_op jit(solution)/shard_map/ppermute | solution.py:391
  31.1 10.0 %collective-permute-start.16 = (bf16[384,256]{1,0:T(8,128)(2,1)S(1)}, bf16[384,256]{1,0:T(8,128)(2,1)S(1)}, u32[]{:S(2)}, u32[]{:S(2)}) collective-permute-start(bf16[384,256]{1,0:T(8,128)(2,1)S(1)} %collective-permute-done.8.refs_0_.refs_6_), channel_id=1, source_target_pairs={{0,1},{1,0},{2,3},{3,2},{4,7},{5,6},{6,5},{7,4},{8,9},{9,8},{10,11... | collective-permute-start | bytes 589832 | tf_op jit(solution)/shard_map/ppermute | solution.py:393
  35.1 8.9 %collective-permute-start.12 = (bf16[96,1024]{1,0:T(8,128)(2,1)S(1)}, bf16[96,1024]{1,0:T(8,128)(2,1)S(1)}, u32[]{:S(2)}, u32[]{:S(2)}) collective-permute-start(bf16[96,1024]{1,0:T(8,128)(2,1)S(1)} %get-tuple-element.71), channel_id=1, source_target_pairs={{0,8},{8,0},{16,24},{24,16},{1,9},{9,1},{17,25},{25,17},{2,10},{10... | collective-permute-start | bytes 589832 | tf_op jit(solution)/shard_map/ppermute | solution.py:444
  36.7 11.5 %collective-permute-start.13 = (bf16[96,1024]{1,0:T(8,128)(2,1)S(1)}, bf16[96,1024]{1,0:T(8,128)(2,1)S(1)}, u32[]{:S(2)}, u32[]{:S(2)}) collective-permute-start(bf16[96,1024]{1,0:T(8,128)(2,1)S(1)} %get-tuple-element.72), channel_id=1, source_target_pairs={{0,16},{8,24},{16,0},{24,8},{1,17},{9,25},{17,1},{25,9},{2,18},{10... | collective-permute-start | bytes 589832 | tf_op jit(solution)/shard_map/ppermute | solution.py:444
  38.2 10.0 %collective-permute-start.14 = (bf16[96,1024]{1,0:T(8,128)(2,1)S(1)}, bf16[96,1024]{1,0:T(8,128)(2,1)S(1)}, u32[]{:S(2)}, u32[]{:S(2)}) collective-permute-start(bf16[96,1024]{1,0:T(8,128)(2,1)S(1)} %get-tuple-element.73), channel_id=1, source_target_pairs={{0,24},{8,16},{16,8},{24,0},{1,25},{9,17},{17,9},{25,1},{2,26},{10... | collective-permute-start | bytes 589832 | tf_op jit(solution)/shard_map/ppermute | solution.py:444
  44.1 7.8 %collective-permute-start.17 = (bf16[96,1024]{1,0:T(8,128)(2,1)S(1)}, bf16[96,1024]{1,0:T(8,128)(2,1)S(1)}, u32[]{:S(2)}, u32[]{:S(2)}) collective-permute-start(bf16[96,1024]{1,0:T(8,128)(2,1)S(1)} %get-tuple-element.80), channel_id=1, source_target_pairs={{0,8},{8,0},{16,24},{24,16},{1,9},{9,1},{17,25},{25,17},{2,10},{10... | collective-permute-start | bytes 589832 | tf_op jit(solution)/shard_map/ppermute | solution.py:444
  45.6 11.6 %collective-permute-start.18 = (bf16[96,1024]{1,0:T(8,128)(2,1)S(1)}, bf16[96,1024]{1,0:T(8,128)(2,1)S(1)}, u32[]{:S(2)}, u32[]{:S(2)}) collective-permute-start(bf16[96,1024]{1,0:T(8,128)(2,1)S(1)} %get-tuple-element.82), channel_id=1, source_target_pairs={{0,16},{8,24},{16,0},{24,8},{1,17},{9,25},{17,1},{25,9},{2,18},{10... | collective-permute-start | bytes 589832 | tf_op jit(solution)/shard_map/ppermute | solution.py:444
  47.1 10.1 %collective-permute-start.19 = (bf16[96,1024]{1,0:T(8,128)(2,1)S(1)}, bf16[96,1024]{1,0:T(8,128)(2,1)S(1)}, u32[]{:S(2)}, u32[]{:S(2)}) collective-permute-start(bf16[96,1024]{1,0:T(8,128)(2,1)S(1)} %get-tuple-element.84), channel_id=1, source_target_pairs={{0,24},{8,16},{16,8},{24,0},{1,25},{9,17},{17,9},{25,1},{2,26},{10... | collective-permute-start | bytes 589832 | tf_op jit(solution)/shard_map/ppermute | solution.py:444

commit v3 on v2

--- a/solution.py
+++ b/solution.py
@@ -60,31 +60,24 @@
     return x * cosine + pltpu.roll(x, HALF, 1) * sine
 
 
-def prep_kernel(heads, pos_hbm, k_hbm, v_hbm, table_ref, *refs):
-    pack_refs, (pos_ref, k_ref, v_ref, sems) = refs[:heads], refs[heads:]
-    pairs = [(pos_hbm, pos_ref), (k_hbm, k_ref), (v_hbm, v_ref)]
-    loads = [pltpu.make_async_copy(src, dst, sems.at[i]) for i, (src, dst) in enumerate(pairs)]
-    for load in loads:
-        load.start()
+def table_kernel(pos_ref, table_ref):
+    sign = jnp.where(lax.broadcasted_iota(jnp.int32, (HD, HD), 1) < HALF, -1.0, 1.0)
     freq = frequency_row()
-    loads[0].wait()
-    tiles = [slice(t * HD, (t + 1) * HD) for t in range(k_ref.shape[0] // HD)]
-    sign = jnp.where(lax.broadcasted_iota(jnp.int32, (HD, HD), 1) < HALF, -1.0, 1.0)
-    tables = []
-    for rows in tiles:
+    for at in range(0, pos_ref.shape[0], HD):
+        rows = slice(at, at + HD)
         pos = pos_ref[rows].reshape(1, HD).astype(jnp.float32)
         pos = jnp.broadcast_to(pos, (HD, HD)).T
         cosine, sine = cos_sin(pos * freq)
-        sine = sine * sign
         table_ref[rows, :HD] = cosine
-        table_ref[rows, HD:] = sine
-        tables.append((cosine, sine))
-    for load in loads[1:]:
-        load.wait()
-    for rows, (cosine, sine) in zip(tiles, tables, strict=True):
+        table_ref[rows, HD:] = sine * sign
+
+
+def pack_kernel(heads, table_ref, k_ref, v_ref, *pack_refs):
+    for at in range(0, k_ref.shape[0], HD):
+        rows = slice(at, at + HD)
         for head in range(heads):
             cols = slice(head * HD, (head + 1) * HD)
-            key = rotate(k_ref[rows, cols].astype(jnp.float32), cosine, sine)
+            key = rotate(k_ref[rows, cols].astype(jnp.float32), table_ref[rows, :HD], table_ref[rows, HD:])
             pack_refs[head][rows, :HD] = key.astype(jnp.bfloat16)
             pack_refs[head][rows, HD:] = v_ref[rows, cols].T
 
@@ -92,23 +85,26 @@
 def prep(keys, values, positions):
     rows, cols = keys.shape
     heads = cols // HD
-    vmem, hbm = pl.BlockSpec(memory_space=pltpu.VMEM), pl.BlockSpec(memory_space=pltpu.HBM)
-    return pl.pallas_call(
-        functools.partial(prep_kernel, heads),
-        in_specs=[hbm] * 3,
-        out_specs=[vmem] * (1 + heads),
-        out_shape=[jax.ShapeDtypeStruct((rows, 2 * HD), jnp.float32)]
-        + [jax.ShapeDtypeStruct((rows, 2 * HD), jnp.bfloat16)] * heads,
-        scratch_shapes=[
-            pltpu.VMEM(positions.shape, positions.dtype),
-            pltpu.VMEM(keys.shape, keys.dtype),
-            pltpu.VMEM(values.shape, values.dtype),
-            pltpu.SemaphoreType.DMA((3,)),
-        ],
-        compiler_params=pltpu.CompilerParams(vmem_limit_bytes=16 << 20),
-        cost_estimate=pl.CostEstimate(flops=10**10, bytes_accessed=10**7, transcendentals=0),
-        name="prep",
-    )(positions, keys, values)
+    vmem = pl.BlockSpec(memory_space=pltpu.VMEM)
+    params = pltpu.CompilerParams(vmem_limit_bytes=16 << 20)
+    table = pl.pallas_call(
+        table_kernel,
+        in_specs=[vmem],
+        out_specs=vmem,
+        out_shape=jax.ShapeDtypeStruct((rows, 2 * HD), jnp.float32),
+        compiler_params=params,
+        cost_estimate=pl.CostEstimate(flops=10**10, bytes_accessed=0, transcendentals=0),
+        name="table",
+    )(positions)
+    packs = pl.pallas_call(
+        functools.partial(pack_kernel, heads),
+        in_specs=[vmem] * 3,
+        out_specs=[vmem] * heads,
+        out_shape=[jax.ShapeDtypeStruct((rows, 2 * HD), jnp.bfloat16)] * heads,
+        compiler_params=params,
+        name="pack",
+    )(table, keys, values)
+    return table, *packs
 
 
 def piece_starts(rows, parts):
@@ -298,7 +294,7 @@
     def finish(g, carry):
         cols = pl.ds(pl.multiple_of(g * rows, rows), rows)
         out = pl.ds(pl.multiple_of(g * HD, HD), HD)
-        result = (acc_ref[:, cols] * (1.0 / total_ref[:, cols])).T.astype(jnp.bfloat16)
+        result = (acc_ref[:, cols] * (1.0 / total_ref[:, cols])).astype(jnp.bfloat16).T
         for k in range(parts):
             out_refs[k][:, out] = result[k * piece : (k + 1) * piece]
         return carry

time: 58.8 us -> 56.4 us (0.959)
  local copies, waits for them, and re-layouts: 2.54 us -> 0.74 us
  Pallas kernels: 22.3 us -> 21.7 us
    unnamed x8, local copies, waits for them, and re-layouts: 2.54 us -> 0.74 us
  transfers between devices with their start and end apart: 20 -> 20, of which waited for: 9 -> 9; matrix products, arithmetic and copies ran while one was open for 0% -> 0% of each run, Pallas kernels for 34% -> 36%
where the time goes in v3:
time: 56.4 us; the launch traced here: 56.3 us
  Pallas kernels  21.7 us (38%)
  waiting for transfers between devices  20.3 us (36%)
  starting transfers between devices  13.2 us (23%)
  local copies, waits for them, and re-layouts  0.74 us (1%)
    ppermute x6, waiting for transfers between devices, local(): lax.ppermute(out[k], 'heads', [(i, i ^ k) for i in range(parts)])  9.66 us
    pallas_call x4, Pallas kernels, attend_next(): pl.pallas_call(functools.partial(next_kernel, groups), in_specs=[vmem] *...  9.27 us
    ppermute x4, waiting for transfers between devices, pass_on(): near[head].append(lax.ppermute(block, 'ctx', upward(step + 1)))  7.18 us
    ppermute x6, starting transfers between devices, local(): lax.ppermute(out[k], 'heads', [(i, i ^ k) for i in range(parts)])  7.11 us
    pallas_call x2, Pallas kernels, attend_last(): pl.pallas_call(functools.partial(last_kernel, groups, len(blocks), len(ev...  5.89 us
    pallas_call x1, Pallas kernels, attend_first(): pl.pallas_call(functools.partial(first_kernel, len(owns), group, parts),...  4.88 us
    ppermute x2, waiting for transfers between devices, local(): near = [[pack, lax.ppermute(pack, 'ctx', upward(1))] for pack in packs]  2.41 us
    ppermute x4, starting transfers between devices, pass_on(): near[head].append(lax.ppermute(block, 'ctx', upward(step + 1)))  1.91 us
  transfers between devices with their start and end apart: 20, of which 9 were waited for; matrix products, arithmetic and copies ran while one was open for 0% of the time, Pallas kernels for 36%

profile of v3, /device:TPU:24, one launch (start us, length us, event | category | flops | bytes accessed | tf_op | source)
XLA Modules:
  0.0 56.3 jit_solution(3065603306523856404)
XLA Ops:
  0.0 0.0 copy-start
  0.0 0.0 copy-start.1
  0.0 0.0 copy-start.3
  0.0 0.7 %copy-done.3 = s32[384]{0:T(512)S(1)} copy-done((s32[384]{0:T(512)S(1)}, s32[384]{0:T(512)}, u32[]{:S(2)}) %copy-start.3) | copy-done | bytes 1560
  0.7 0.0 copy-start.2
  0.7 0.3 table.1.table_ref
  1.1 0.0 copy-done
  1.1 0.0 copy-done.1
  1.1 0.2 pack.1
  1.3 0.1 collective-permute-start
  1.4 0.1 collective-permute-start.1
  1.4 0.5 collective-permute-start.2
  1.9 1.7 %collective-permute-start.3 = (bf16[384,256]{1,0:T(8,128)(2,1)S(1)}, bf16[384,256]{1,0:T(8,128)(2,1)S(1)}, u32[]{:S(2)}, u32[]{:S(2)}) collective-permute-start(bf16[384,256]{1,0:T(8,128)(2,1)S(1)} %get-tuple-element.45.refs_1_.refs_2_), channel_id=1, source_target_pairs={{0,2},{1,3},{2,4},{3,5},{4,6},{5,7},{6,0},{7,1},{8,10},{9,11},{10,... | collective-permute-start | bytes 589832 | tf_op jit(solution)/shard_map/ppermute | solution.py:378
  3.6 0.0 copy-done.2
  3.6 4.9 %attend_first.1 = (bf16[128,3072]{1,0:T(8,128)(2,1)S(1)}, f32[1,3072]{1,0:T(1,128)S(1)}, f32[1,3072]{1,0:T(1,128)S(1)}, f32[128,3072]{1,0:T(8,128)S(1)}, bf16[12...) custom-call(bf16[384,2048]{1,0:T(8,128)(2,1)S(1)} %copy-done.2, ...), custom_call_target="tpu_custom_call" | custom-call | flops 2415919104 | tf_op jit(solution)/shard_map/attend_first/pallas_call | solution.py:176
  8.5 0.6 %collective-permute-done.refs_1_.refs_4_ = bf16[384,256]{1,0:T(8,128)(2,1)S(1)} collective-permute-done((bf16[384,256]{1,0:T(8,128)(2,1)S(1)}, bf16[384,256]{1,0:T(8,128)(2,1)S(1)}, u32[]{:S(2)}, u32[]{:S(2)}) %collective-permute-start) | collective-permute-done | bytes 196640 | tf_op jit(solution)/shard_map/ppermute | solution.py:378
  9.1 0.0 collective-permute-done.1.refs_0_.refs_3_
  9.1 0.0 collective-permute-done.2.refs_0_.refs_3_
  9.1 0.0 collective-permute-start.4
  9.1 1.2 %collective-permute-start.5 = (bf16[384,256]{1,0:T(8,128)(2,1)S(1)}, bf16[384,256]{1,0:T(8,128)(2,1)S(1)}, u32[]{:S(2)}, u32[]{:S(2)}) collective-permute-start(bf16[384,256]{1,0:T(8,128)(2,1)S(1)} %collective-permute-done.refs_1_.refs_4_), channel_id=1, source_target_pairs={{0,1},{1,0},{2,4},{3,5},{4,6},{5,7},{6,2},{7,3},{8,9},{9,8},{10,12... | collective-permute-start | bytes 589832 | tf_op jit(solution)/shard_map/ppermute | solution.py:392
  10.4 1.8 %collective-permute-done.3.refs_1_.refs_4_ = bf16[384,256]{1,0:T(8,128)(2,1)S(1)} collective-permute-done((bf16[384,256]{1,0:T(8,128)(2,1)S(1)}, bf16[384,256]{1,0:T(8,128)(2,1)S(1)}, u32[]{:S(2)}, u32[]{:S(2)}) %collective-permute-start.3) | collective-permute-done | bytes 196640 | tf_op jit(solution)/shard_map/ppermute | solution.py:378
  12.2 0.0 collective-permute-done.4.refs_2_.refs_5_
  12.2 2.3 %attend_next.4 = (f32[1,3072]{1,0:T(1,128)S(1)}, f32[128,3072]{1,0:T(8,128)S(1)}) custom-call(bf16[128,3072]{1,0:T(8,128)(2,1)S(1)} %get-tuple-element.46.queries_ref, f32[1,3072]{1,0:T(1,128)S(1)} %get-tuple-element.47.shift_ref, f32[1,3072]{1,0:T(1,128)S(1)} %get-tuple-element.51.total_in, ...), custom_call_target="tpu_custom_call", output_to_operand_aliasing={{0}: (2, {}), {1}: (3, {})} | custom-call | flops 3623878656 | tf_op jit(solution)/shard_map/attend_next/pallas_call | solution.py:216
  14.5 1.9 %collective-permute-done.5.refs_0_.refs_6_ = bf16[384,256]{1,0:T(8,128)(2,1)S(1)} collective-permute-done((bf16[384,256]{1,0:T(8,128)(2,1)S(1)}, bf16[384,256]{1,0:T(8,128)(2,1)S(1)}, u32[]{:S(2)}, u32[]{:S(2)}) %collective-permute-start.5) | collective-permute-done | bytes 196640 | tf_op jit(solution)/shard_map/ppermute | solution.py:392
  16.5 0.0 collective-permute-start.6
  16.5 0.5 collective-permute-start.10
  16.9 1.0 %collective-permute-done.6.refs_1_.refs_7_ = bf16[384,256]{1,0:T(8,128)(2,1)S(1)} collective-permute-done((bf16[384,256]{1,0:T(8,128)(2,1)S(1)}, bf16[384,256]{1,0:T(8,128)(2,1)S(1)}, u32[]{:S(2)}, u32[]{:S(2)}) %collective-permute-start.6) | collective-permute-done | bytes 196640 | tf_op jit(solution)/shard_map/ppermute | solution.py:394
  17.9 2.3 %attend_next.5 = (f32[1,3072]{1,0:T(1,128)S(1)}, f32[128,3072]{1,0:T(8,128)S(1)}) custom-call(bf16[128,3072]{1,0:T(8,128)(2,1)S(1)} %get-tuple-element.46.queries_ref, f32[1,3072]{1,0:T(1,128)S(1)} %get-tuple-element.47.shift_ref, f32[1,3072]{1,0:T(1,128)S(1)} %get-tuple-element.55.total_in, ...), custom_call_target="tpu_custom_call", output_to_operand_aliasing={{0}: (2, {}), {1}: (3, {})} | custom-call | flops 2415919104 | tf_op jit(solution)/shard_map/attend_next/pallas_call | solution.py:216
  20.2 0.2 collective-permute-start.7
  20.4 0.0 collective-permute-start.8
  20.4 3.6 %collective-permute-done.10.refs_0_.refs_8_ = bf16[384,256]{1,0:T(8,128)(2,1)S(1)} collective-permute-done((bf16[384,256]{1,0:T(8,128)(2,1)S(1)}, bf16[384,256]{1,0:T(8,128)(2,1)S(1)}, u32[]{:S(2)}, u32[]{:S(2)}) %collective-permute-start.10) | collective-permute-done | bytes 196640 | tf_op jit(solution)/shard_map/ppermute | solution.py:392
  24.1 0.0 collective-permute-done.7.refs_2_.refs_5_
  24.1 2.3 %attend_next.6 = (f32[1,3072]{1,0:T(1,128)S(1)}, f32[128,3072]{1,0:T(8,128)S(1)}) custom-call(bf16[128,3072]{1,0:T(8,128)(2,1)S(1)} %get-tuple-element.58.queries_ref, f32[1,3072]{1,0:T(1,128)S(1)} %get-tuple-element.59.shift_ref, f32[1,3072]{1,0:T(1,128)S(1)} %get-tuple-element.61.total_in, ...), custom_call_target="tpu_custom_call", output_to_operand_aliasing={{0}: (2, {}), {1}: (3, {})} | custom-call | flops 3623878656 | tf_op jit(solution)/shard_map/attend_next/pallas_call | solution.py:216
  26.4 1.6 %collective-permute-done.8.refs_0_.refs_6_ = bf16[384,256]{1,0:T(8,128)(2,1)S(1)} collective-permute-done((bf16[384,256]{1,0:T(8,128)(2,1)S(1)}, bf16[384,256]{1,0:T(8,128)(2,1)S(1)}, u32[]{:S(2)}, u32[]{:S(2)}) %collective-permute-start.8) | collective-permute-done | bytes 196640 | tf_op jit(solution)/shard_map/ppermute | solution.py:392
  28.0 0.0 collective-permute-start.9
  28.0 0.5 collective-permute-start.11
  28.5 0.2 collective-permute-start.15
  28.7 1.1 %collective-permute-start.16 = (bf16[384,256]{1,0:T(8,128)(2,1)S(1)}, bf16[384,256]{1,0:T(8,128)(2,1)S(1)}, u32[]{:S(2)}, u32[]{:S(2)}) collective-permute-start(bf16[384,256]{1,0:T(8,128)(2,1)S(1)} %collective-permute-done.8.refs_0_.refs_6_), channel_id=1, source_target_pairs={{0,1},{1,0},{2,3},{3,2},{4,7},{5,6},{6,5},{7,4},{8,9},{9,8},{10,11... | collective-permute-start | bytes 589832 | tf_op jit(solution)/shard_map/ppermute | solution.py:389
  29.8 0.0 collective-permute-done.9.refs_1_.refs_7_
  29.9 0.0 collective-permute-done.11.refs_1_.refs_9_
  29.9 2.9 %attend_last.2 = (bf16[96,1024]{1,0:T(8,128)(2,1)S(1)}, bf16[96,1024]{1,0:T(8,128)(2,1)S(1)}, bf16[96,1024]{1,0:T(8,128)(2,1)S(1)}, bf16[96,1024]{1,0:T(8,128)(2,1)S(1)}) custom-call(bf16[128,3072]{1,0:T(8,128)(2,1)S(1)} %get-tuple-element.46.queries_ref, f32[1,3072]{1,0:T(1,128)S(1)} %get-tuple-element.47.shift_ref, ...), custom_call_target="tpu_custom_call" | custom-call | flops 2415919104 | tf_op jit(solution)/shard_map/attend_last/pallas_call | solution.py:310
  32.8 1.6 %collective-permute-start.12 = (bf16[96,1024]{1,0:T(8,128)(2,1)S(1)}, bf16[96,1024]{1,0:T(8,128)(2,1)S(1)}, u32[]{:S(2)}, u32[]{:S(2)}) collective-permute-start(bf16[96,1024]{1,0:T(8,128)(2,1)S(1)} %get-tuple-element.69), channel_id=1, source_target_pairs={{0,8},{8,0},{16,24},{24,16},{1,9},{9,1},{17,25},{25,17},{2,10},{10... | collective-permute-start | bytes 589832 | tf_op jit(solution)/shard_map/ppermute | solution.py:440
  34.3 1.5 %collective-permute-start.13 = (bf16[96,1024]{1,0:T(8,128)(2,1)S(1)}, bf16[96,1024]{1,0:T(8,128)(2,1)S(1)}, u32[]{:S(2)}, u32[]{:S(2)}) collective-permute-start(bf16[96,1024]{1,0:T(8,128)(2,1)S(1)} %get-tuple-element.70), channel_id=1, source_target_pairs={{0,16},{8,24},{16,0},{24,8},{1,17},{9,25},{17,1},{25,9},{2,18},{10... | collective-permute-start | bytes 589832 | tf_op jit(solution)/shard_map/ppermute | solution.py:440
  35.9 0.5 collective-permute-start.14
  36.3 2.3 %attend_next.7 = (f32[1,3072]{1,0:T(1,128)S(1)}, f32[128,3072]{1,0:T(8,128)S(1)}) custom-call(bf16[128,3072]{1,0:T(8,128)(2,1)S(1)} %get-tuple-element.58.queries_ref, f32[1,3072]{1,0:T(1,128)S(1)} %get-tuple-element.59.shift_ref, f32[1,3072]{1,0:T(1,128)S(1)} %get-tuple-element.72.total_in, ...), custom_call_target="tpu_custom_call", output_to_operand_aliasing={{0}: (2, {}), {1}: (3, {})} | custom-call | flops 2415919104 | tf_op jit(solution)/shard_map/attend_next/pallas_call | solution.py:216
  38.7 0.0 collective-permute-done.15.refs_0_.refs_8_
  38.7 0.0 collective-permute-done.16.refs_1_.refs_9_
  38.7 3.0 %attend_last.3 = (bf16[96,1024]{1,0:T(8,128)(2,1)S(1)}, bf16[96,1024]{1,0:T(8,128)(2,1)S(1)}, bf16[96,1024]{1,0:T(8,128)(2,1)S(1)}, bf16[96,1024]{1,0:T(8,128)(2,1)S(1)}) custom-call(bf16[128,3072]{1,0:T(8,128)(2,1)S(1)} %get-tuple-element.58.queries_ref, f32[1,3072]{1,0:T(1,128)S(1)} %get-tuple-element.59.shift_ref, ...), custom_call_target="tpu_custom_call" | custom-call | flops 2415919104 | tf_op jit(solution)/shard_map/attend_last/pallas_call | solution.py:310
  41.7 0.0 collective-permute-done.12.refs_1_
  41.7 1.6 %collective-permute-start.17 = (bf16[96,1024]{1,0:T(8,128)(2,1)S(1)}, bf16[96,1024]{1,0:T(8,128)(2,1)S(1)}, u32[]{:S(2)}, u32[]{:S(2)}) collective-permute-start(bf16[96,1024]{1,0:T(8,128)(2,1)S(1)} %get-tuple-element.78), channel_id=1, source_target_pairs={{0,8},{8,0},{16,24},{24,16},{1,9},{9,1},{17,25},{25,17},{2,10},{10... | collective-permute-start | bytes 589832 | tf_op jit(solution)/shard_map/ppermute | solution.py:440
  43.2 1.5 %collective-permute-start.18 = (bf16[96,1024]{1,0:T(8,128)(2,1)S(1)}, bf16[96,1024]{1,0:T(8,128)(2,1)S(1)}, u32[]{:S(2)}, u32[]{:S(2)}) collective-permute-start(bf16[96,1024]{1,0:T(8,128)(2,1)S(1)} %get-tuple-element.80), channel_id=1, source_target_pairs={{0,16},{8,24},{16,0},{24,8},{1,17},{9,25},{17,1},{25,9},{2,18},{10... | collective-permute-start | bytes 589832 | tf_op jit(solution)/shard_map/ppermute | solution.py:440
  44.8 0.5 collective-permute-start.19
  45.2 0.6 %collective-permute-done.13.refs_2_ = bf16[96,1024]{1,0:T(8,128)(2,1)S(1)} collective-permute-done((bf16[96,1024]{1,0:T(8,128)(2,1)S(1)}, bf16[96,1024]{1,0:T(8,128)(2,1)S(1)}, u32[]{:S(2)}, u32[]{:S(2)}) %collective-permute-start.13) | collective-permute-done | bytes 196640 | tf_op jit(solution)/shard_map/ppermute | solution.py:440
  45.9 0.0 collective-permute-done.14.refs_3_
  45.9 3.7 %collective-permute-done.17.refs_5_ = bf16[96,1024]{1,0:T(8,128)(2,1)S(1)} collective-permute-done((bf16[96,1024]{1,0:T(8,128)(2,1)S(1)}, bf16[96,1024]{1,0:T(8,128)(2,1)S(1)}, u32[]{:S(2)}, u32[]{:S(2)}) %collective-permute-start.17) | collective-permute-done | bytes 196640 | tf_op jit(solution)/shard_map/ppermute | solution.py:440
  49.5 5.4 %collective-permute-done.18.refs_6_ = bf16[96,1024]{1,0:T(8,128)(2,1)S(1)} collective-permute-done((bf16[96,1024]{1,0:T(8,128)(2,1)S(1)}, bf16[96,1024]{1,0:T(8,128)(2,1)S(1)}, u32[]{:S(2)}, u32[]{:S(2)}) %collective-permute-start.18) | collective-permute-done | bytes 196640 | tf_op jit(solution)/shard_map/ppermute | solution.py:440
  54.9 0.0 collective-permute-done.19.refs_7_
  54.9 1.2 %place.1 = bf16[96,8192]{1,0:T(8,128)(2,1)} custom-call(bf16[96,1024]{1,0:T(8,128)(2,1)S(1)} %get-tuple-element.68.refs_0_, bf16[96,1024]{1,0:T(8,128)(2,1)S(1)} %collective-permute-done.12.refs_1_, bf16[96,1024]{1,0:T(8,128)(2,1)S(1)} %collective-permute-done.13.refs_2_, bf16[96,1024]{1,0:T(8,128)(2,1)S(1)} %collective-permute-done.14.refs_3_, ...), custom_call_target="tpu_custom_call" | custom-call | tf_op jit(solution)/shard_map/place/pallas_call | solution.py:348
Async XLA Ops:
  0.0 1.1 %copy-start = (bf16[384,256]{1,0:T(8,128)(2,1)S(1)}, bf16[384,256]{1,0:T(8,128)(2,1)}, u32[]{:S(2)}) copy-start(bf16[384,256]{1,0:T(8,128)(2,1)} %k_ref.1) | copy-start | bytes 589828
  0.0 1.1 %copy-start.1 = (bf16[384,256]{1,0:T(8,128)(2,1)S(1)}, bf16[384,256]{1,0:T(8,128)(2,1)}, u32[]{:S(2)}) copy-start(bf16[384,256]{1,0:T(8,128)(2,1)} %v_ref.1) | copy-start | bytes 589828
  0.0 0.7 %copy-start.3 = (s32[384]{0:T(512)S(1)}, s32[384]{0:T(512)}, u32[]{:S(2)}) copy-start(s32[384]{0:T(512)} %pos_ref.1) | copy-start | bytes 4612
  0.7 2.9 %copy-start.2 = (bf16[384,2048]{1,0:T(8,128)(2,1)S(1)}, bf16[384,2048]{1,0:T(8,128)(2,1)}, u32[]{:S(2)}) copy-start(bf16[384,2048]{1,0:T(8,128)(2,1)} %q_ref.1) | copy-start | bytes 4718596
  1.3 7.8 %collective-permute-start = (bf16[384,256]{1,0:T(8,128)(2,1)S(1)}, bf16[384,256]{1,0:T(8,128)(2,1)S(1)}, u32[]{:S(2)}, u32[]{:S(2)}) collective-permute-start(bf16[384,256]{1,0:T(8,128)(2,1)S(1)} %get-tuple-element.44.refs_0_.refs_2_), channel_id=1, source_target_pairs={{0,2},{1,3},{2,4},{3,5},{4,6},{5,7},{6,0},{7,1},{8,10},{9,11},{10,... | collective-permute-start | bytes 589832 | tf_op jit(solution)/shard_map/ppermute | solution.py:378
  1.4 7.8 %collective-permute-start.1 = (bf16[384,256]{1,0:T(8,128)(2,1)S(1)}, bf16[384,256]{1,0:T(8,128)(2,1)S(1)}, u32[]{:S(2)}, u32[]{:S(2)}) collective-permute-start(bf16[384,256]{1,0:T(8,128)(2,1)S(1)} %get-tuple-element.44.refs_0_.refs_2_), channel_id=1, source_target_pairs={{0,1},{1,0},{2,3},{3,2},{4,5},{5,4},{6,7},{7,6},{8,9},{9,8},{10,11... | collective-permute-start | bytes 589832 | tf_op jit(solution)/shard_map/ppermute | solution.py:379
  1.4 7.7 %collective-permute-start.2 = (bf16[384,256]{1,0:T(8,128)(2,1)S(1)}, bf16[384,256]{1,0:T(8,128)(2,1)S(1)}, u32[]{:S(2)}, u32[]{:S(2)}) collective-permute-start(bf16[384,256]{1,0:T(8,128)(2,1)S(1)} %get-tuple-element.45.refs_1_.refs_2_), channel_id=1, source_target_pairs={{0,1},{1,0},{2,3},{3,2},{4,5},{5,4},{6,7},{7,6},{8,9},{9,8},{10,11... | collective-permute-start | bytes 589832 | tf_op jit(solution)/shard_map/ppermute | solution.py:379
  1.9 10.3 %collective-permute-start.3 = (bf16[384,256]{1,0:T(8,128)(2,1)S(1)}, bf16[384,256]{1,0:T(8,128)(2,1)S(1)}, u32[]{:S(2)}, u32[]{:S(2)}) collective-permute-start(bf16[384,256]{1,0:T(8,128)(2,1)S(1)} %get-tuple-element.45.refs_1_.refs_2_), channel_id=1, source_target_pairs={{0,2},{1,3},{2,4},{3,5},{4,6},{5,7},{6,0},{7,1},{8,10},{9,11},{10,... | collective-permute-start | bytes 589832 | tf_op jit(solution)/shard_map/ppermute | solution.py:378
  9.1 3.1 %collective-permute-start.4 = (bf16[384,256]{1,0:T(8,128)(2,1)S(1)}, bf16[384,256]{1,0:T(8,128)(2,1)S(1)}, u32[]{:S(2)}, u32[]{:S(2)}) collective-permute-start(bf16[384,256]{1,0:T(8,128)(2,1)S(1)} %collective-permute-done.refs_1_.refs_4_), channel_id=1, source_target_pairs={{0,1},{1,0},{2,3},{3,2},{4,5},{5,4},{6,7},{7,6},{8,9},{9,8},{10,11... | collective-permute-start | bytes 589832 | tf_op jit(solution)/shard_map/ppermute | solution.py:394
  9.1 7.3 %collective-permute-start.5 = (bf16[384,256]{1,0:T(8,128)(2,1)S(1)}, bf16[384,256]{1,0:T(8,128)(2,1)S(1)}, u32[]{:S(2)}, u32[]{:S(2)}) collective-permute-start(bf16[384,256]{1,0:T(8,128)(2,1)S(1)} %collective-permute-done.refs_1_.refs_4_), channel_id=1, source_target_pairs={{0,1},{1,0},{2,4},{3,5},{4,6},{5,7},{6,2},{7,3},{8,9},{9,8},{10,12... | collective-permute-start | bytes 589832 | tf_op jit(solution)/shard_map/ppermute | solution.py:392
  16.5 1.4 %collective-permute-start.6 = (bf16[384,256]{1,0:T(8,128)(2,1)S(1)}, bf16[384,256]{1,0:T(8,128)(2,1)S(1)}, u32[]{:S(2)}, u32[]{:S(2)}) collective-permute-start(bf16[384,256]{1,0:T(8,128)(2,1)S(1)} %collective-permute-done.5.refs_0_.refs_6_), channel_id=1, source_target_pairs={{0,1},{1,0},{2,3},{3,2},{4,5},{5,4},{6,7},{7,6},{8,9},{9,8},{10,11... | collective-permute-start | bytes 589832 | tf_op jit(solution)/shard_map/ppermute | solution.py:394
  16.5 7.6 %collective-permute-start.10 = (bf16[384,256]{1,0:T(8,128)(2,1)S(1)}, bf16[384,256]{1,0:T(8,128)(2,1)S(1)}, u32[]{:S(2)}, u32[]{:S(2)}) collective-permute-start(bf16[384,256]{1,0:T(8,128)(2,1)S(1)} %collective-permute-done.5.refs_0_.refs_6_), channel_id=1, source_target_pairs={{0,1},{1,0},{2,3},{3,2},{4,6},{5,7},{6,4},{7,5},{8,9},{9,8},{10,11... | collective-permute-start | bytes 589832 | tf_op jit(solution)/shard_map/ppermute | solution.py:392
  20.2 3.8 %collective-permute-start.7 = (bf16[384,256]{1,0:T(8,128)(2,1)S(1)}, bf16[384,256]{1,0:T(8,128)(2,1)S(1)}, u32[]{:S(2)}, u32[]{:S(2)}) collective-permute-start(bf16[384,256]{1,0:T(8,128)(2,1)S(1)} %collective-permute-done.3.refs_1_.refs_4_), channel_id=1, source_target_pairs={{0,1},{1,0},{2,3},{3,2},{4,5},{5,4},{6,7},{7,6},{8,9},{9,8},{10,11... | collective-permute-start | bytes 589832 | tf_op jit(solution)/shard_map/ppermute | solution.py:394
  20.4 7.5 %collective-permute-start.8 = (bf16[384,256]{1,0:T(8,128)(2,1)S(1)}, bf16[384,256]{1,0:T(8,128)(2,1)S(1)}, u32[]{:S(2)}, u32[]{:S(2)}) collective-permute-start(bf16[384,256]{1,0:T(8,128)(2,1)S(1)} %collective-permute-done.3.refs_1_.refs_4_), channel_id=1, source_target_pairs={{0,1},{1,0},{2,4},{3,5},{4,6},{5,7},{6,2},{7,3},{8,9},{9,8},{10,12... | collective-permute-start | bytes 589832 | tf_op jit(solution)/shard_map/ppermute | solution.py:392
  28.0 1.9 %collective-permute-start.9 = (bf16[384,256]{1,0:T(8,128)(2,1)S(1)}, bf16[384,256]{1,0:T(8,128)(2,1)S(1)}, u32[]{:S(2)}, u32[]{:S(2)}) collective-permute-start(bf16[384,256]{1,0:T(8,128)(2,1)S(1)} %collective-permute-done.8.refs_0_.refs_6_), channel_id=1, source_target_pairs={{0,1},{1,0},{2,3},{3,2},{4,5},{5,4},{6,7},{7,6},{8,9},{9,8},{10,11... | collective-permute-start | bytes 589832 | tf_op jit(solution)/shard_map/ppermute | solution.py:388
  28.0 1.9 %collective-permute-start.11 = (bf16[384,256]{1,0:T(8,128)(2,1)S(1)}, bf16[384,256]{1,0:T(8,128)(2,1)S(1)}, u32[]{:S(2)}, u32[]{:S(2)}) collective-permute-start(bf16[384,256]{1,0:T(8,128)(2,1)S(1)} %collective-permute-done.10.refs_0_.refs_8_), channel_id=1, source_target_pairs={{0,1},{1,0},{2,3},{3,2},{4,5},{5,4},{6,7},{7,6},{8,9},{9,8},{10,11... | collective-permute-start | bytes 589832 | tf_op jit(solution)/shard_map/ppermute | solution.py:394
  28.5 10.2 %collective-permute-start.15 = (bf16[384,256]{1,0:T(8,128)(2,1)S(1)}, bf16[384,256]{1,0:T(8,128)(2,1)S(1)}, u32[]{:S(2)}, u32[]{:S(2)}) collective-permute-start(bf16[384,256]{1,0:T(8,128)(2,1)S(1)} %collective-permute-done.8.refs_0_.refs_6_), channel_id=1, source_target_pairs={{0,1},{1,0},{2,3},{3,2},{4,6},{5,7},{6,4},{7,5},{8,9},{9,8},{10,11... | collective-permute-start | bytes 589832 | tf_op jit(solution)/shard_map/ppermute | solution.py:387
  28.7 10.0 %collective-permute-start.16 = (bf16[384,256]{1,0:T(8,128)(2,1)S(1)}, bf16[384,256]{1,0:T(8,128)(2,1)S(1)}, u32[]{:S(2)}, u32[]{:S(2)}) collective-permute-start(bf16[384,256]{1,0:T(8,128)(2,1)S(1)} %collective-permute-done.8.refs_0_.refs_6_), channel_id=1, source_target_pairs={{0,1},{1,0},{2,3},{3,2},{4,7},{5,6},{6,5},{7,4},{8,9},{9,8},{10,11... | collective-permute-start | bytes 589832 | tf_op jit(solution)/shard_map/ppermute | solution.py:389
  32.8 8.9 %collective-permute-start.12 = (bf16[96,1024]{1,0:T(8,128)(2,1)S(1)}, bf16[96,1024]{1,0:T(8,128)(2,1)S(1)}, u32[]{:S(2)}, u32[]{:S(2)}) collective-permute-start(bf16[96,1024]{1,0:T(8,128)(2,1)S(1)} %get-tuple-element.69), channel_id=1, source_target_pairs={{0,8},{8,0},{16,24},{24,16},{1,9},{9,1},{17,25},{25,17},{2,10},{10... | collective-permute-start | bytes 589832 | tf_op jit(solution)/shard_map/ppermute | solution.py:440
  34.3 11.5 %collective-permute-start.13 = (bf16[96,1024]{1,0:T(8,128)(2,1)S(1)}, bf16[96,1024]{1,0:T(8,128)(2,1)S(1)}, u32[]{:S(2)}, u32[]{:S(2)}) collective-permute-start(bf16[96,1024]{1,0:T(8,128)(2,1)S(1)} %get-tuple-element.70), channel_id=1, source_target_pairs={{0,16},{8,24},{16,0},{24,8},{1,17},{9,25},{17,1},{25,9},{2,18},{10... | collective-permute-start | bytes 589832 | tf_op jit(solution)/shard_map/ppermute | solution.py:440
  35.9 10.0 %collective-permute-start.14 = (bf16[96,1024]{1,0:T(8,128)(2,1)S(1)}, bf16[96,1024]{1,0:T(8,128)(2,1)S(1)}, u32[]{:S(2)}, u32[]{:S(2)}) collective-permute-start(bf16[96,1024]{1,0:T(8,128)(2,1)S(1)} %get-tuple-element.71), channel_id=1, source_target_pairs={{0,24},{8,16},{16,8},{24,0},{1,25},{9,17},{17,9},{25,1},{2,26},{10... | collective-permute-start | bytes 589832 | tf_op jit(solution)/shard_map/ppermute | solution.py:440
  41.7 7.8 %collective-permute-start.17 = (bf16[96,1024]{1,0:T(8,128)(2,1)S(1)}, bf16[96,1024]{1,0:T(8,128)(2,1)S(1)}, u32[]{:S(2)}, u32[]{:S(2)}) collective-permute-start(bf16[96,1024]{1,0:T(8,128)(2,1)S(1)} %get-tuple-element.78), channel_id=1, source_target_pairs={{0,8},{8,0},{16,24},{24,16},{1,9},{9,1},{17,25},{25,17},{2,10},{10... | collective-permute-start | bytes 589832 | tf_op jit(solution)/shard_map/ppermute | solution.py:440
  43.2 11.7 %collective-permute-start.18 = (bf16[96,1024]{1,0:T(8,128)(2,1)S(1)}, bf16[96,1024]{1,0:T(8,128)(2,1)S(1)}, u32[]{:S(2)}, u32[]{:S(2)}) collective-permute-start(bf16[96,1024]{1,0:T(8,128)(2,1)S(1)} %get-tuple-element.80), channel_id=1, source_target_pairs={{0,16},{8,24},{16,0},{24,8},{1,17},{9,25},{17,1},{25,9},{2,18},{10... | collective-permute-start | bytes 589832 | tf_op jit(solution)/shard_map/ppermute | solution.py:440
  44.8 10.1 %collective-permute-start.19 = (bf16[96,1024]{1,0:T(8,128)(2,1)S(1)}, bf16[96,1024]{1,0:T(8,128)(2,1)S(1)}, u32[]{:S(2)}, u32[]{:S(2)}) collective-permute-start(bf16[96,1024]{1,0:T(8,128)(2,1)S(1)} %get-tuple-element.82), channel_id=1, source_target_pairs={{0,24},{8,16},{16,8},{24,0},{1,25},{9,17},{17,9},{25,1},{2,26},{10... | collective-permute-start | bytes 589832 | tf_op jit(solution)/shard_map/ppermute | solution.py:440

commit v4 on v3

--- a/solution.py
+++ b/solution.py
@@ -17,6 +17,7 @@
 TILE = 1536
 ONES = 16
 LIMIT = 24 << 20
+MORE = 16
 
 
 def inverse_frequencies():
@@ -80,9 +81,13 @@
             key = rotate(k_ref[rows, cols].astype(jnp.float32), table_ref[rows, :HD], table_ref[rows, HD:])
             pack_refs[head][rows, :HD] = key.astype(jnp.bfloat16)
             pack_refs[head][rows, HD:] = v_ref[rows, cols].T
-
-
-def prep(keys, values, positions):
+    for pack_ref in pack_refs:
+        if pack_ref.shape[0] > k_ref.shape[0]:
+            more = slice(k_ref.shape[0], pack_ref.shape[0])
+            pack_ref[more, :] = jnp.zeros((more.stop - more.start, 2 * HD), jnp.bfloat16)
+
+
+def prep(keys, values, positions, extra):
     rows, cols = keys.shape
     heads = cols // HD
     vmem = pl.BlockSpec(memory_space=pltpu.VMEM)
@@ -100,7 +105,7 @@
         functools.partial(pack_kernel, heads),
         in_specs=[vmem] * 3,
         out_specs=[vmem] * heads,
-        out_shape=[jax.ShapeDtypeStruct((rows, 2 * HD), jnp.bfloat16)] * heads,
+        out_shape=[jax.ShapeDtypeStruct((rows + more, 2 * HD), jnp.bfloat16) for more in extra],
         compiler_params=params,
         name="pack",
     )(table, keys, values)
@@ -111,6 +116,10 @@
     piece = rows // parts
     me = lax.axis_index("heads")
     return piece, [pl.multiple_of((me ^ k) * piece, piece) for k in range(parts)]
+
+
+def trim(refs, rows):
+    return [ref.at[pl.ds(0, rows)] if ref.shape[0] > rows else ref for ref in refs]
 
 
 def values_of(blocks):
@@ -145,8 +154,8 @@
 
 
 def first_kernel(heads, group, parts, q_ref, table_ref, *refs):
-    own_refs, out_refs = refs[:heads], refs[heads:]
     rows = q_ref.shape[0]
+    own_refs, out_refs = trim(refs[:heads], rows), refs[heads:]
     piece, starts = piece_starts(rows, parts)
     table = jnp.concatenate([table_ref[pl.ds(s, piece), :] for s in starts], axis=0)
     lane = lax.broadcasted_iota(jnp.int32, (1, piece), 1)
@@ -191,36 +200,36 @@
     return [tuple(flat[4 * h : 4 * h + 4]) for h in range(len(owns))]
 
 
-def cost(width, keys):
-    return pl.CostEstimate(flops=8 * width * keys * HD, bytes_accessed=0, transcendentals=0)
-
-
-def attend_groups(groups, refs, state):
+def cost(width, keys, share=1):
+    return pl.CostEstimate(flops=share * 8 * width * keys * HD, bytes_accessed=0, transcendentals=0)
+
+
+def attend_groups(groups, refs, state, rows):
     rank = lax.axis_index("ctx")
     chip, core = rank // 2, rank % 2
-    refs = list(refs)
+    refs = trim(refs, rows)
     for step in groups:
         blocks = [refs.pop(0) for _ in range(1 if step == 0 else 2)]
         there = core == 1 if step == 0 else chip >= step
         pl.when(there)(functools.partial(attend, state, blocks))
 
 
-def next_kernel(groups, queries_ref, shift_ref, total_in, acc_in, *refs):
+def next_kernel(groups, rows, queries_ref, shift_ref, total_in, acc_in, *refs):
     del total_in, acc_in
-    attend_groups(groups, refs[:-2], (queries_ref, shift_ref, refs[-2], refs[-1]))
-
-
-def attend_next(state, groups, blocks):
+    attend_groups(groups, refs[:-2], (queries_ref, shift_ref, refs[-2], refs[-1]), rows)
+
+
+def attend_next(state, groups, blocks, rows, share=1):
     queries, shift, total, acc = state
     vmem = pl.BlockSpec(memory_space=pltpu.VMEM)
     total, acc = pl.pallas_call(
-        functools.partial(next_kernel, groups),
+        functools.partial(next_kernel, groups, rows),
         in_specs=[vmem] * (4 + len(blocks)),
         out_specs=[vmem] * 2,
         out_shape=[jax.ShapeDtypeStruct(x.shape, x.dtype) for x in (total, acc)],
         input_output_aliases={2: 0, 3: 1},
         compiler_params=pltpu.CompilerParams(vmem_limit_bytes=LIMIT),
-        cost_estimate=cost(queries.shape[1], sum(b.shape[0] for b in blocks)),
+        cost_estimate=cost(queries.shape[1], sum(b.shape[0] for b in blocks), share),
         name="attend_next",
     )(queries, shift, total, acc, *blocks)
     return queries, shift, total, acc
@@ -278,11 +287,11 @@
 def last_kernel(groups, count, every_count, rows, parts, queries_ref, shift_ref, total_in, acc_in, *refs):
     refs = list(refs)
     blocks, refs = refs[:count], refs[count:]
-    every, refs = refs[:every_count], refs[every_count:]
+    every, refs = trim(refs[:every_count], rows), refs[every_count:]
     out_refs, (total_ref, acc_ref, top_ref, blocks_ref, sems) = refs[:parts], refs[parts:]
     total_ref[...] = total_in[...]
     acc_ref[...] = acc_in[...]
-    attend_groups(groups, blocks, (queries_ref, shift_ref, total_ref, acc_ref))
+    attend_groups(groups, blocks, (queries_ref, shift_ref, total_ref, acc_ref), rows)
     in_range = jnp.max(total_ref[...]) <= TOTAL_LIMIT
 
     @pl.when(jnp.logical_not(in_range))
@@ -302,9 +311,8 @@
     lax.fori_loop(0, queries_ref.shape[1] // rows, finish, 0, unroll=True)
 
 
-def attend_last(state, groups, blocks, every, parts):
+def attend_last(state, groups, blocks, every, rows, parts, share=1):
     queries, shift, total, acc = state
-    rows = every[0].shape[0]
     group = queries.shape[1] // rows
     vmem, anywhere = pl.BlockSpec(memory_space=pltpu.VMEM), pl.BlockSpec(memory_space=pl.ANY)
     return pl.pallas_call(
@@ -320,7 +328,7 @@
             pltpu.SemaphoreType.DMA((len(every),)),
         ],
         compiler_params=pltpu.CompilerParams(vmem_limit_bytes=LIMIT),
-        cost_estimate=cost(queries.shape[1], sum(b.shape[0] for b in blocks)),
+        cost_estimate=cost(queries.shape[1], sum(b.shape[0] for b in blocks), share),
         name="attend_last",
     )(queries, shift, total, acc, *blocks, *every)
 
@@ -360,86 +368,95 @@
     return lax.optimization_barrier((value, *earlier))[0]
 
 
+class Exchange:
+    def __init__(self, ctx_size, parts, group, queries, table, packs):
+        self.size, self.parts, self.rows = ctx_size, parts, queries.shape[0]
+        self.chips, self.heads = ctx_size // 2, range(len(packs))
+        self.swap = [(c, c ^ 1) for c in range(ctx_size)]
+        self.near = [[pack, self.up(pack, 1)] for pack in packs]
+        self.far = [[self.across(pack)] for pack in packs]
+        self.states = attend_first(queries, table, packs, group, parts)
+
+    def across(self, block):
+        return lax.ppermute(block, "ctx", self.swap)
+
+    def up(self, block, step, cross=0):
+        low = 2 * (step - 1)
+        top = [(c, (c + 2 if c + 2 < self.size else low + c % 2) ^ cross) for c in range(low, self.size)]
+        return lax.ppermute(block, "ctx", self.swap[:low] + top)
+
+    def pass_on(self, head, step, *earlier):
+        block = after(self.near[head][step], *earlier)
+        self.near[head][step] = block
+        if step + 1 < self.chips:
+            self.near[head].append(self.up(block, step + 1))
+        self.far[head].append(self.across(block))
+
+    def blocks(self, head, steps):
+        out = []
+        for s in steps:
+            out += [self.far[head][0]] if s == 0 else [self.near[head][s], self.far[head][s]]
+        return out
+
+    def state(self, head, earlier):
+        queries_t, shift, total, acc = self.states[head]
+        return queries_t, shift, after(total, *earlier), acc
+
+    def call(self, head, steps, *earlier, share=1):
+        state = self.state(head, earlier)
+        self.states[head] = attend_next(state, steps, self.blocks(head, steps), self.rows, share)
+        return self.states[head][2]
+
+    def last(self, head, *earlier, share=1):
+        every = [b for pair in zip(self.near[head], self.far[head], strict=True) for b in pair]
+        steps = [self.chips - 1]
+        blocks = self.blocks(head, steps)
+        return attend_last(self.state(head, earlier), steps, blocks, every, self.rows, self.parts, share)
+
+    def spread(self, outs, *earlier):
+        out = [after(o, *earlier) if earlier else o for o in outs]
+        perms = [[(i, i ^ k) for i in range(self.parts)] for k in range(self.parts)]
+        return [outs[0]] + [lax.ppermute(out[k], "heads", perms[k]) for k in range(1, self.parts)]
+
+
+def in_turn(ex):
+    began = [ex.states[-1][2], *(far[0] for far in ex.far)]
+    pieces = []
+    for head in ex.heads:
+        ex.pass_on(head, 1, *began)
+        for step in range(1, ex.chips - 1):
+            ex.call(head, [0, 1] if step == 1 else [step])
+            ex.pass_on(head, step + 1, ex.states[head][2])
+        pieces += ex.spread(ex.last(head))
+    return pieces
+
+
+def four_chips(ex):
+    one, two = 0, 1
+    latest = ex.states[two][2]
+    ex.pass_on(one, 1, latest, ex.far[one][0], ex.far[two][0])
+    ex.pass_on(two, 1, latest)
+    latest = ex.call(one, [0, 1], latest, ex.near[one][1])
+    ex.pass_on(one, 2, latest)
+    latest = ex.call(one, [2], latest, share=0)
+    ex.pass_on(two, 2, latest)
+    ex.far[two].append(ex.up(ex.near[two][2], 3, 1))
+    latest = ex.call(two, [0, 1], latest)
+    ex.pass_on(one, 3, latest)
+    outs = ex.last(one, latest, share=0)
+    pieces = ex.spread(outs)
+    latest = ex.call(two, [2], outs[0], share=0)
+    outs = ex.last(two, latest)
+    return pieces + ex.spread(outs, pieces[1])
+
+
 def local(ctx_size, parts, queries, keys, values, positions):
     kv_heads = keys.shape[1] // HD
     group = queries.shape[1] // (kv_heads * HD)
-    chips = ctx_size // 2
-    heads = range(kv_heads)
-    swap = [(c, c ^ 1) for c in range(ctx_size)]
-
-    def upward(step, cross=0):
-        low = 2 * (step - 1)
-        top = [(c, (c + 2 if c + 2 < ctx_size else low + c % 2) ^ cross) for c in range(low, ctx_size)]
-        return swap[:low] + top
-
-    direct = chips > 3 and kv_heads > 1
-
-    table, *packs = prep(keys, values, positions)
-    near = [[pack, lax.ppermute(pack, "ctx", upward(1))] for pack in packs]
-    far = [[lax.ppermute(pack, "ctx", swap)] for pack in packs]
-    states = attend_first(queries, table, packs, group, parts)
-    latest = [states[-1][2], *(far[h][0] for h in heads)]
-
-    def pass_on(head, step, *earlier):
-        block = after(near[head][step], *earlier)
-        near[head][step] = block
-        if step + 1 == chips - 1 and direct and head == kv_heads - 1:
-            near[head].append(lax.ppermute(block, "ctx", upward(step + 1)))
-            far[head].append(lax.ppermute(block, "ctx", swap))
-            far[head].append(lax.ppermute(block, "ctx", upward(step + 1, 1)))
-            return
-        if step + 1 < chips:
-            near[head].append(lax.ppermute(block, "ctx", upward(step + 1)))
-        if len(far[head]) == step:
-            far[head].append(lax.ppermute(block, "ctx", swap))
-
-    def blocks_of(head, steps):
-        out = []
-        for s in steps:
-            out += [far[head][0]] if s == 0 else [near[head][s], far[head][s]]
-        return out
-
-    def state_after(head, earlier):
-        queries_t, shift, total, acc = states[head]
-        return queries_t, shift, after(total, *earlier), acc
-
-    order = [(0, [0, 1])] + [(0, [s]) for s in range(2, chips - 1)]
-    for head in range(1, kv_heads):
-        order += [(head, [0, 1])] + [(head, [s]) for s in range(2, chips - 2)]
-    done = [0] * kv_heads
-    pass_on(0, 1, *latest)
-    latest = latest[:1] + [near[h][1] for h in heads]
-    for i, (head, steps) in enumerate(order):
-        states[head] = attend_next(state_after(head, latest), steps, blocks_of(head, steps))
-        done[head] = steps[-1]
-        latest = [states[head][2]]
-        if done[head] + 1 < chips and (head == kv_heads - 1 or done[head] + 1 < chips - 1):
-            pass_on(head, done[head] + 1, *latest)
-            latest.append(far[head][done[head] + 1])
-        elif head < kv_heads - 1:
-            pass_on(head + 1, 1, *latest)
-            pass_on(head, chips - 1, *latest)
-            latest.append(far[head + 1][1])
-    pieces = []
-    sent = []
-    for head in heads:
-        if chips - done[head] > 2:
-            steps = list(range(done[head] + 1, chips - 1))
-            states[head] = attend_next(state_after(head, latest), steps, blocks_of(head, steps))
-            done[head], latest = chips - 2, [states[head][2]]
-        steps = list(range(done[head] + 1, chips))
-        outs = attend_last(
-            state_after(head, latest),
-            steps,
-            blocks_of(head, steps),
-            [b for pair in zip(near[head], far[head], strict=True) for b in pair],
-            parts,
-        )
-        latest = [outs[0]]
-        out = [after(outs[k], *sent) if k else outs[k] for k in range(parts)]
-        out[1:] = [lax.ppermute(out[k], "heads", [(i, i ^ k) for i in range(parts)]) for k in range(1, parts)]
-        sent = out[1:2]
-        pieces += out
+    four = (ctx_size, kv_heads) == (8, 2)
+    table, *packs = prep(keys, values, positions, (0, MORE) if four else (0,) * kv_heads)
+    ex = Exchange(ctx_size, parts, group, queries, table, packs)
+    pieces = four_chips(ex) if four else in_turn(ex)
     return place(pieces, kv_heads, parts)
 
 

time: 56.4 us -> 53.9 us (0.956)
  waiting for transfers between devices: 20.3 us -> 14.4 us
  starting transfers between devices: 13.2 us -> 16.4 us
    ppermute x20, waiting for transfers between devices: 20.3 us -> 14.4 us  [the longest x6 8.63 us: spread(): lax.ppermute(out[k], 'heads', perms[k])]
    ppermute x20, starting transfers between devices: 13.2 us -> 16.4 us  [the longest x6 7.12 us: spread(): lax.ppermute(out[k], 'heads', perms[k])]
  transfers between devices with their start and end apart: 20 -> 20, of which waited for: 9 -> 9; matrix products, arithmetic and copies ran while one was open for 0% -> 0% of each run, Pallas kernels for 36% -> 38%
where the time goes in v4:
time: 53.9 us; the launch traced here: 53.8 us
  Pallas kernels  22 us (41%)
  starting transfers between devices  16.4 us (30%)
  waiting for transfers between devices  14.4 us (27%)
  local copies, waits for them, and re-layouts  0.74 us (1%)
    pallas_call x4, Pallas kernels, attend_next(): pl.pallas_call(functools.partial(next_kernel, groups, rows), in_specs=[vm...  9.37 us
    ppermute x6, waiting for transfers between devices, spread(): lax.ppermute(out[k], 'heads', perms[k])  8.63 us
    ppermute x6, starting transfers between devices, spread(): lax.ppermute(out[k], 'heads', perms[k])  7.12 us
    ppermute x7, starting transfers between devices, up(): return lax.ppermute(block, 'ctx', self.swap[:low] + top)  6.9 us
    pallas_call x2, Pallas kernels, attend_last(): pl.pallas_call(functools.partial(last_kernel, groups, len(blocks), len(ev...  5.88 us
    pallas_call x1, Pallas kernels, attend_first(): pl.pallas_call(functools.partial(first_kernel, len(owns), group, parts),...  5.02 us
    ppermute x7, waiting for transfers between devices, up(): return lax.ppermute(block, 'ctx', self.swap[:low] + top)  4.65 us
    ppermute x7, starting transfers between devices, across(): return lax.ppermute(block, 'ctx', self.swap)  2.34 us
  transfers between devices with their start and end apart: 20, of which 9 were waited for; matrix products, arithmetic and copies ran while one was open for 0% of the time, Pallas kernels for 38%

profile of v4, /device:TPU:24, one launch (start us, length us, event | category | flops | bytes accessed | tf_op | source)
XLA Modules:
  0.0 53.8 jit_solution(9436239838679973859)
XLA Ops:
  0.0 0.0 copy-start
  0.0 0.0 copy-start.1
  0.0 0.0 copy-start.3
  0.0 0.7 %copy-done.3 = s32[384]{0:T(512)S(1)} copy-done((s32[384]{0:T(512)S(1)}, s32[384]{0:T(512)}, u32[]{:S(2)}) %copy-start.3) | copy-done | bytes 1560
  0.7 0.0 copy-start.2
  0.7 0.3 table.1.table_ref
  1.1 0.0 copy-done
  1.1 0.0 copy-done.1
  1.1 0.2 pack.1
  1.3 0.1 collective-permute-start
  1.4 0.1 collective-permute-start.1
  1.4 0.5 collective-permute-start.2
  1.9 1.7 %collective-permute-start.6 = (bf16[400,256]{1,0:T(8,128)(2,1)S(1)}, bf16[400,256]{1,0:T(8,128)(2,1)S(1)}, u32[]{:S(2)}, u32[]{:S(2)}) collective-permute-start(bf16[400,256]{1,0:T(8,128)(2,1)S(1)} %get-tuple-element.45.refs_1_.refs_2_), channel_id=1, source_target_pairs={{0,2},{1,3},{2,4},{3,5},{4,6},{5,7},{6,0},{7,1},{8,10},{9,11},{10,... | collective-permute-start | bytes 614408 | tf_op jit(solution)/shard_map/ppermute | solution.py:386
  3.6 0.0 copy-done.2
  3.7 5.0 %attend_first.1 = (bf16[128,3072]{1,0:T(8,128)(2,1)S(1)}, f32[1,3072]{1,0:T(1,128)S(1)}, f32[1,3072]{1,0:T(1,128)S(1)}, f32[128,3072]{1,0:T(8,128)S(1)}, bf16[12...) custom-call(bf16[384,2048]{1,0:T(8,128)(2,1)S(1)} %copy-done.2, ...), custom_call_target="tpu_custom_call" | custom-call | flops 2415919104 | tf_op jit(solution)/shard_map/attend_first/pallas_call | solution.py:185
  8.7 0.5 collective-permute-done.refs_1_.refs_4_
  9.1 0.0 collective-permute-done.1.refs_0_.refs_3_
  9.1 0.0 collective-permute-done.2.refs_0_.refs_3_
  9.1 0.0 collective-permute-start.3
  9.1 1.4 %collective-permute-start.4 = (bf16[384,256]{1,0:T(8,128)(2,1)S(1)}, bf16[384,256]{1,0:T(8,128)(2,1)S(1)}, u32[]{:S(2)}, u32[]{:S(2)}) collective-permute-start(bf16[384,256]{1,0:T(8,128)(2,1)S(1)} %collective-permute-done.refs_1_.refs_4_), channel_id=1, source_target_pairs={{0,1},{1,0},{2,4},{3,5},{4,6},{5,7},{6,2},{7,3},{8,9},{9,8},{10,12... | collective-permute-start | bytes 589832 | tf_op jit(solution)/shard_map/ppermute | solution.py:386
  10.5 1.9 %collective-permute-done.6.refs_1_.refs_4_ = bf16[400,256]{1,0:T(8,128)(2,1)S(1)} collective-permute-done((bf16[400,256]{1,0:T(8,128)(2,1)S(1)}, bf16[400,256]{1,0:T(8,128)(2,1)S(1)}, u32[]{:S(2)}, u32[]{:S(2)}) %collective-permute-start.6) | collective-permute-done | bytes 204832 | tf_op jit(solution)/shard_map/ppermute | solution.py:386
  12.4 0.0 collective-permute-start.7
  12.4 0.3 collective-permute-start.13
  12.7 0.0 collective-permute-done.3.refs_2_.refs_5_
  12.7 2.3 %attend_next.4 = (f32[1,3072]{1,0:T(1,128)S(1)}, f32[128,3072]{1,0:T(8,128)S(1)}) custom-call(bf16[128,3072]{1,0:T(8,128)(2,1)S(1)} %get-tuple-element.46.queries_ref, f32[1,3072]{1,0:T(1,128)S(1)} %get-tuple-element.47.shift_ref, f32[1,3072]{1,0:T(1,128)S(1)} %get-tuple-element.51.total_in, ...), custom_call_target="tpu_custom_call", output_to_operand_aliasing={{0}: (2, {}), {1}: (3, {})} | custom-call | flops 3623878656 | tf_op jit(solution)/shard_map/attend_next/pallas_call | solution.py:225
  15.0 1.9 %collective-permute-done.4.refs_0_.refs_6_ = bf16[384,256]{1,0:T(8,128)(2,1)S(1)} collective-permute-done((bf16[384,256]{1,0:T(8,128)(2,1)S(1)}, bf16[384,256]{1,0:T(8,128)(2,1)S(1)}, u32[]{:S(2)}, u32[]{:S(2)}) %collective-permute-start.4) | collective-permute-done | bytes 196640 | tf_op jit(solution)/shard_map/ppermute | solution.py:386
  16.9 0.0 collective-permute-start.5
  16.9 1.6 %collective-permute-start.8 = (bf16[384,256]{1,0:T(8,128)(2,1)S(1)}, bf16[384,256]{1,0:T(8,128)(2,1)S(1)}, u32[]{:S(2)}, u32[]{:S(2)}) collective-permute-start(bf16[384,256]{1,0:T(8,128)(2,1)S(1)} %collective-permute-done.4.refs_0_.refs_6_), channel_id=1, source_target_pairs={{0,1},{1,0},{2,3},{3,2},{4,6},{5,7},{6,4},{7,5},{8,9},{9,8},{10,11... | collective-permute-start | bytes 589832 | tf_op jit(solution)/shard_map/ppermute | solution.py:386
  18.5 0.0 collective-permute-done.5.refs_1_.refs_7_
  18.5 2.4 %attend_next.5 = (f32[1,3072]{1,0:T(1,128)S(1)}, f32[128,3072]{1,0:T(8,128)S(1)}) custom-call(bf16[128,3072]{1,0:T(8,128)(2,1)S(1)} %get-tuple-element.46.queries_ref, f32[1,3072]{1,0:T(1,128)S(1)} %get-tuple-element.47.shift_ref, f32[1,3072]{1,0:T(1,128)S(1)} %get-tuple-element.54.total_in, ...), custom_call_target="tpu_custom_call", output_to_operand_aliasing={{0}: (2, {}), {1}: (3, {})} | custom-call | tf_op jit(solution)/shard_map/attend_next/pallas_call | solution.py:225
  20.9 0.4 collective-permute-done.13.refs_0_.refs_6_
  21.3 0.0 collective-permute-start.14
  21.3 1.1 %collective-permute-start.15 = (bf16[400,256]{1,0:T(8,128)(2,1)S(1)}, bf16[400,256]{1,0:T(8,128)(2,1)S(1)}, u32[]{:S(2)}, u32[]{:S(2)}) collective-permute-start(bf16[400,256]{1,0:T(8,128)(2,1)S(1)} %collective-permute-done.13.refs_0_.refs_6_), channel_id=1, source_target_pairs={{0,1},{1,0},{2,3},{3,2},{4,6},{5,7},{6,4},{7,5},{8,9},{9,8},{10,11... | collective-permute-start | bytes 614408 | tf_op jit(solution)/shard_map/ppermute | solution.py:386
  22.4 0.8 %collective-permute-start.16 = (bf16[400,256]{1,0:T(8,128)(2,1)S(1)}, bf16[400,256]{1,0:T(8,128)(2,1)S(1)}, u32[]{:S(2)}, u32[]{:S(2)}) collective-permute-start(bf16[400,256]{1,0:T(8,128)(2,1)S(1)} %collective-permute-done.13.refs_0_.refs_6_), channel_id=1, source_target_pairs={{0,1},{1,0},{2,3},{3,2},{4,7},{5,6},{6,5},{7,4},{8,9},{9,8},{10,11... | collective-permute-start | bytes 614408 | tf_op jit(solution)/shard_map/ppermute | solution.py:386
  23.2 0.0 collective-permute-done.7.refs_2_.refs_5_
  23.2 2.4 %attend_next.6 = (f32[1,3072]{1,0:T(1,128)S(1)}, f32[128,3072]{1,0:T(8,128)S(1)}) custom-call(bf16[128,3072]{1,0:T(8,128)(2,1)S(1)} %get-tuple-element.58.queries_ref, f32[1,3072]{1,0:T(1,128)S(1)} %get-tuple-element.59.shift_ref, f32[1,3072]{1,0:T(1,128)S(1)} %get-tuple-element.60.total_in, ...), custom_call_target="tpu_custom_call", output_to_operand_aliasing={{0}: (2, {}), {1}: (3, {})} | custom-call | flops 3774873600 | tf_op jit(solution)/shard_map/attend_next/pallas_call | solution.py:225
  25.5 0.0 collective-permute-done.8.refs_0_.refs_8_
  25.5 1.8 %collective-permute-start.9 = (bf16[384,256]{1,0:T(8,128)(2,1)S(1)}, bf16[384,256]{1,0:T(8,128)(2,1)S(1)}, u32[]{:S(2)}, u32[]{:S(2)}) collective-permute-start(bf16[384,256]{1,0:T(8,128)(2,1)S(1)} %collective-permute-done.8.refs_0_.refs_8_), channel_id=1, source_target_pairs={{0,1},{1,0},{2,3},{3,2},{4,5},{5,4},{6,7},{7,6},{8,9},{9,8},{10,11... | collective-permute-start | bytes 589832 | tf_op jit(solution)/shard_map/ppermute | solution.py:381
  27.3 1.1 %collective-permute-done.9.refs_1_.refs_9_ = bf16[384,256]{1,0:T(8,128)(2,1)S(1)} collective-permute-done((bf16[384,256]{1,0:T(8,128)(2,1)S(1)}, bf16[384,256]{1,0:T(8,128)(2,1)S(1)}, u32[]{:S(2)}, u32[]{:S(2)}) %collective-permute-start.9) | collective-permute-done | bytes 196640 | tf_op jit(solution)/shard_map/ppermute | solution.py:381
  28.4 3.0 %attend_last.2 = (bf16[96,1024]{1,0:T(8,128)(2,1)S(1)}, bf16[96,1024]{1,0:T(8,128)(2,1)S(1)}, bf16[96,1024]{1,0:T(8,128)(2,1)S(1)}, bf16[96,1024]{1,0:T(8,128)(2,1)S(1)}) custom-call(bf16[128,3072]{1,0:T(8,128)(2,1)S(1)} %get-tuple-element.46.queries_ref, f32[1,3072]{1,0:T(1,128)S(1)} %get-tuple-element.47.shift_ref, ...), custom_call_target="tpu_custom_call" | custom-call | tf_op jit(solution)/shard_map/attend_last/pallas_call | solution.py:318
  31.3 1.6 %collective-permute-start.10 = (bf16[96,1024]{1,0:T(8,128)(2,1)S(1)}, bf16[96,1024]{1,0:T(8,128)(2,1)S(1)}, u32[]{:S(2)}, u32[]{:S(2)}) collective-permute-start(bf16[96,1024]{1,0:T(8,128)(2,1)S(1)} %get-tuple-element.68), channel_id=1, source_target_pairs={{0,8},{8,0},{16,24},{24,16},{1,9},{9,1},{17,25},{25,17},{2,10},{10... | collective-permute-start | bytes 589832 | tf_op jit(solution)/shard_map/ppermute | solution.py:419
  32.9 1.5 %collective-permute-start.11 = (bf16[96,1024]{1,0:T(8,128)(2,1)S(1)}, bf16[96,1024]{1,0:T(8,128)(2,1)S(1)}, u32[]{:S(2)}, u32[]{:S(2)}) collective-permute-start(bf16[96,1024]{1,0:T(8,128)(2,1)S(1)} %get-tuple-element.69), channel_id=1, source_target_pairs={{0,16},{8,24},{16,0},{24,8},{1,17},{9,25},{17,1},{25,9},{2,18},{10... | collective-permute-start | bytes 589832 | tf_op jit(solution)/shard_map/ppermute | solution.py:419
  34.4 0.0 collective-permute-done.14.refs_1_.refs_7_
  34.4 0.5 collective-permute-start.12
  34.9 2.4 %attend_next.7 = (f32[1,3072]{1,0:T(1,128)S(1)}, f32[128,3072]{1,0:T(8,128)S(1)}) custom-call(bf16[128,3072]{1,0:T(8,128)(2,1)S(1)} %get-tuple-element.58.queries_ref, f32[1,3072]{1,0:T(1,128)S(1)} %get-tuple-element.59.shift_ref, f32[1,3072]{1,0:T(1,128)S(1)} %get-tuple-element.71.total_in, ...), custom_call_target="tpu_custom_call", output_to_operand_aliasing={{0}: (2, {}), {1}: (3, {})} | custom-call | tf_op jit(solution)/shard_map/attend_next/pallas_call | solution.py:225
  37.3 0.0 collective-permute-done.15.refs_0_.refs_8_
  37.3 0.0 collective-permute-done.16.refs_1_.refs_9_
  37.3 2.9 %attend_last.3 = (bf16[96,1024]{1,0:T(8,128)(2,1)S(1)}, bf16[96,1024]{1,0:T(8,128)(2,1)S(1)}, bf16[96,1024]{1,0:T(8,128)(2,1)S(1)}, bf16[96,1024]{1,0:T(8,128)(2,1)S(1)}) custom-call(bf16[128,3072]{1,0:T(8,128)(2,1)S(1)} %get-tuple-element.58.queries_ref, f32[1,3072]{1,0:T(1,128)S(1)} %get-tuple-element.59.shift_ref, ...), custom_call_target="tpu_custom_call" | custom-call | flops 2516582400 | tf_op jit(solution)/shard_map/attend_last/pallas_call | solution.py:318
  40.2 0.0 collective-permute-done.10.refs_1_
  40.2 1.5 %collective-permute-start.17 = (bf16[96,1024]{1,0:T(8,128)(2,1)S(1)}, bf16[96,1024]{1,0:T(8,128)(2,1)S(1)}, u32[]{:S(2)}, u32[]{:S(2)}) collective-permute-start(bf16[96,1024]{1,0:T(8,128)(2,1)S(1)} %get-tuple-element.78), channel_id=1, source_target_pairs={{0,8},{8,0},{16,24},{24,16},{1,9},{9,1},{17,25},{25,17},{2,10},{10... | collective-permute-start | bytes 589832 | tf_op jit(solution)/shard_map/ppermute | solution.py:419
  41.8 1.5 %collective-permute-start.18 = (bf16[96,1024]{1,0:T(8,128)(2,1)S(1)}, bf16[96,1024]{1,0:T(8,128)(2,1)S(1)}, u32[]{:S(2)}, u32[]{:S(2)}) collective-permute-start(bf16[96,1024]{1,0:T(8,128)(2,1)S(1)} %get-tuple-element.80), channel_id=1, source_target_pairs={{0,16},{8,24},{16,0},{24,8},{1,17},{9,25},{17,1},{25,9},{2,18},{10... | collective-permute-start | bytes 589832 | tf_op jit(solution)/shard_map/ppermute | solution.py:419
  43.3 0.5 collective-permute-start.19
  43.8 0.1 collective-permute-done.11.refs_2_
  43.9 0.2 collective-permute-done.12.refs_3_
  44.1 4.0 %collective-permute-done.17.refs_5_ = bf16[96,1024]{1,0:T(8,128)(2,1)S(1)} collective-permute-done((bf16[96,1024]{1,0:T(8,128)(2,1)S(1)}, bf16[96,1024]{1,0:T(8,128)(2,1)S(1)}, u32[]{:S(2)}, u32[]{:S(2)}) %collective-permute-start.17) | collective-permute-done | bytes 196640 | tf_op jit(solution)/shard_map/ppermute | solution.py:419
  48.1 4.3 %collective-permute-done.18.refs_6_ = bf16[96,1024]{1,0:T(8,128)(2,1)S(1)} collective-permute-done((bf16[96,1024]{1,0:T(8,128)(2,1)S(1)}, bf16[96,1024]{1,0:T(8,128)(2,1)S(1)}, u32[]{:S(2)}, u32[]{:S(2)}) %collective-permute-start.18) | collective-permute-done | bytes 196640 | tf_op jit(solution)/shard_map/ppermute | solution.py:419
  52.4 0.0 collective-permute-done.19.refs_7_
  52.4 1.2 %place.1 = bf16[96,8192]{1,0:T(8,128)(2,1)} custom-call(bf16[96,1024]{1,0:T(8,128)(2,1)S(1)} %get-tuple-element.67.refs_0_, bf16[96,1024]{1,0:T(8,128)(2,1)S(1)} %collective-permute-done.10.refs_1_, bf16[96,1024]{1,0:T(8,128)(2,1)S(1)} %collective-permute-done.11.refs_2_, bf16[96,1024]{1,0:T(8,128)(2,1)S(1)} %collective-permute-done.12.refs_3_, ...), custom_call_target="tpu_custom_call" | custom-call | tf_op jit(solution)/shard_map/place/pallas_call | solution.py:356
Async XLA Ops:
  0.0 1.1 %copy-start = (bf16[384,256]{1,0:T(8,128)(2,1)S(1)}, bf16[384,256]{1,0:T(8,128)(2,1)}, u32[]{:S(2)}) copy-start(bf16[384,256]{1,0:T(8,128)(2,1)} %k_ref.1) | copy-start | bytes 589828
  0.0 1.1 %copy-start.1 = (bf16[384,256]{1,0:T(8,128)(2,1)S(1)}, bf16[384,256]{1,0:T(8,128)(2,1)}, u32[]{:S(2)}) copy-start(bf16[384,256]{1,0:T(8,128)(2,1)} %v_ref.1) | copy-start | bytes 589828
  0.0 0.7 %copy-start.3 = (s32[384]{0:T(512)S(1)}, s32[384]{0:T(512)}, u32[]{:S(2)}) copy-start(s32[384]{0:T(512)} %pos_ref.1) | copy-start | bytes 4612
  0.7 2.9 %copy-start.2 = (bf16[384,2048]{1,0:T(8,128)(2,1)S(1)}, bf16[384,2048]{1,0:T(8,128)(2,1)}, u32[]{:S(2)}) copy-start(bf16[384,2048]{1,0:T(8,128)(2,1)} %q_ref.1) | copy-start | bytes 4718596
  1.3 7.8 %collective-permute-start = (bf16[384,256]{1,0:T(8,128)(2,1)S(1)}, bf16[384,256]{1,0:T(8,128)(2,1)S(1)}, u32[]{:S(2)}, u32[]{:S(2)}) collective-permute-start(bf16[384,256]{1,0:T(8,128)(2,1)S(1)} %get-tuple-element.44.refs_0_.refs_2_), channel_id=1, source_target_pairs={{0,2},{1,3},{2,4},{3,5},{4,6},{5,7},{6,0},{7,1},{8,10},{9,11},{10,... | collective-permute-start | bytes 589832 | tf_op jit(solution)/shard_map/ppermute | solution.py:386
  1.4 7.8 %collective-permute-start.1 = (bf16[384,256]{1,0:T(8,128)(2,1)S(1)}, bf16[384,256]{1,0:T(8,128)(2,1)S(1)}, u32[]{:S(2)}, u32[]{:S(2)}) collective-permute-start(bf16[384,256]{1,0:T(8,128)(2,1)S(1)} %get-tuple-element.44.refs_0_.refs_2_), channel_id=1, source_target_pairs={{0,1},{1,0},{2,3},{3,2},{4,5},{5,4},{6,7},{7,6},{8,9},{9,8},{10,11... | collective-permute-start | bytes 589832 | tf_op jit(solution)/shard_map/ppermute | solution.py:381
  1.4 7.7 %collective-permute-start.2 = (bf16[400,256]{1,0:T(8,128)(2,1)S(1)}, bf16[400,256]{1,0:T(8,128)(2,1)S(1)}, u32[]{:S(2)}, u32[]{:S(2)}) collective-permute-start(bf16[400,256]{1,0:T(8,128)(2,1)S(1)} %get-tuple-element.45.refs_1_.refs_2_), channel_id=1, source_target_pairs={{0,1},{1,0},{2,3},{3,2},{4,5},{5,4},{6,7},{7,6},{8,9},{9,8},{10,11... | collective-permute-start | bytes 614408 | tf_op jit(solution)/shard_map/ppermute | solution.py:381
  1.9 10.5 %collective-permute-start.6 = (bf16[400,256]{1,0:T(8,128)(2,1)S(1)}, bf16[400,256]{1,0:T(8,128)(2,1)S(1)}, u32[]{:S(2)}, u32[]{:S(2)}) collective-permute-start(bf16[400,256]{1,0:T(8,128)(2,1)S(1)} %get-tuple-element.45.refs_1_.refs_2_), channel_id=1, source_target_pairs={{0,2},{1,3},{2,4},{3,5},{4,6},{5,7},{6,0},{7,1},{8,10},{9,11},{10,... | collective-permute-start | bytes 614408 | tf_op jit(solution)/shard_map/ppermute | solution.py:386
  9.1 3.6 %collective-permute-start.3 = (bf16[384,256]{1,0:T(8,128)(2,1)S(1)}, bf16[384,256]{1,0:T(8,128)(2,1)S(1)}, u32[]{:S(2)}, u32[]{:S(2)}) collective-permute-start(bf16[384,256]{1,0:T(8,128)(2,1)S(1)} %collective-permute-done.refs_1_.refs_4_), channel_id=1, source_target_pairs={{0,1},{1,0},{2,3},{3,2},{4,5},{5,4},{6,7},{7,6},{8,9},{9,8},{10,11... | collective-permute-start | bytes 589832 | tf_op jit(solution)/shard_map/ppermute | solution.py:381
  9.1 7.8 %collective-permute-start.4 = (bf16[384,256]{1,0:T(8,128)(2,1)S(1)}, bf16[384,256]{1,0:T(8,128)(2,1)S(1)}, u32[]{:S(2)}, u32[]{:S(2)}) collective-permute-start(bf16[384,256]{1,0:T(8,128)(2,1)S(1)} %collective-permute-done.refs_1_.refs_4_), channel_id=1, source_target_pairs={{0,1},{1,0},{2,4},{3,5},{4,6},{5,7},{6,2},{7,3},{8,9},{9,8},{10,12... | collective-permute-start | bytes 589832 | tf_op jit(solution)/shard_map/ppermute | solution.py:386
  12.4 10.7 %collective-permute-start.7 = (bf16[400,256]{1,0:T(8,128)(2,1)S(1)}, bf16[400,256]{1,0:T(8,128)(2,1)S(1)}, u32[]{:S(2)}, u32[]{:S(2)}) collective-permute-start(bf16[400,256]{1,0:T(8,128)(2,1)S(1)} %collective-permute-done.6.refs_1_.refs_4_), channel_id=1, source_target_pairs={{0,1},{1,0},{2,3},{3,2},{4,5},{5,4},{6,7},{7,6},{8,9},{9,8},{10,11... | collective-permute-start | bytes 614408 | tf_op jit(solution)/shard_map/ppermute | solution.py:381
  12.4 8.9 %collective-permute-start.13 = (bf16[400,256]{1,0:T(8,128)(2,1)S(1)}, bf16[400,256]{1,0:T(8,128)(2,1)S(1)}, u32[]{:S(2)}, u32[]{:S(2)}) collective-permute-start(bf16[400,256]{1,0:T(8,128)(2,1)S(1)} %collective-permute-done.6.refs_1_.refs_4_), channel_id=1, source_target_pairs={{0,1},{1,0},{2,4},{3,5},{4,6},{5,7},{6,2},{7,3},{8,9},{9,8},{10,12... | collective-permute-start | bytes 614408 | tf_op jit(solution)/shard_map/ppermute | solution.py:386
  16.9 1.6 %collective-permute-start.5 = (bf16[384,256]{1,0:T(8,128)(2,1)S(1)}, bf16[384,256]{1,0:T(8,128)(2,1)S(1)}, u32[]{:S(2)}, u32[]{:S(2)}) collective-permute-start(bf16[384,256]{1,0:T(8,128)(2,1)S(1)} %collective-permute-done.4.refs_0_.refs_6_), channel_id=1, source_target_pairs={{0,1},{1,0},{2,3},{3,2},{4,5},{5,4},{6,7},{7,6},{8,9},{9,8},{10,11... | collective-permute-start | bytes 589832 | tf_op jit(solution)/shard_map/ppermute | solution.py:381
  16.9 8.6 %collective-permute-start.8 = (bf16[384,256]{1,0:T(8,128)(2,1)S(1)}, bf16[384,256]{1,0:T(8,128)(2,1)S(1)}, u32[]{:S(2)}, u32[]{:S(2)}) collective-permute-start(bf16[384,256]{1,0:T(8,128)(2,1)S(1)} %collective-permute-done.4.refs_0_.refs_6_), channel_id=1, source_target_pairs={{0,1},{1,0},{2,3},{3,2},{4,6},{5,7},{6,4},{7,5},{8,9},{9,8},{10,11... | collective-permute-start | bytes 589832 | tf_op jit(solution)/shard_map/ppermute | solution.py:386
  21.3 13.1 %collective-permute-start.14 = (bf16[400,256]{1,0:T(8,128)(2,1)S(1)}, bf16[400,256]{1,0:T(8,128)(2,1)S(1)}, u32[]{:S(2)}, u32[]{:S(2)}) collective-permute-start(bf16[400,256]{1,0:T(8,128)(2,1)S(1)} %collective-permute-done.13.refs_0_.refs_6_), channel_id=1, source_target_pairs={{0,1},{1,0},{2,3},{3,2},{4,5},{5,4},{6,7},{7,6},{8,9},{9,8},{10,11... | collective-permute-start | bytes 614408 | tf_op jit(solution)/shard_map/ppermute | solution.py:381
  21.3 16.0 %collective-permute-start.15 = (bf16[400,256]{1,0:T(8,128)(2,1)S(1)}, bf16[400,256]{1,0:T(8,128)(2,1)S(1)}, u32[]{:S(2)}, u32[]{:S(2)}) collective-permute-start(bf16[400,256]{1,0:T(8,128)(2,1)S(1)} %collective-permute-done.13.refs_0_.refs_6_), channel_id=1, source_target_pairs={{0,1},{1,0},{2,3},{3,2},{4,6},{5,7},{6,4},{7,5},{8,9},{9,8},{10,11... | collective-permute-start | bytes 614408 | tf_op jit(solution)/shard_map/ppermute | solution.py:386
  22.4 14.9 %collective-permute-start.16 = (bf16[400,256]{1,0:T(8,128)(2,1)S(1)}, bf16[400,256]{1,0:T(8,128)(2,1)S(1)}, u32[]{:S(2)}, u32[]{:S(2)}) collective-permute-start(bf16[400,256]{1,0:T(8,128)(2,1)S(1)} %collective-permute-done.13.refs_0_.refs_6_), channel_id=1, source_target_pairs={{0,1},{1,0},{2,3},{3,2},{4,7},{5,6},{6,5},{7,4},{8,9},{9,8},{10,11... | collective-permute-start | bytes 614408 | tf_op jit(solution)/shard_map/ppermute | solution.py:386
  25.5 2.8 %collective-permute-start.9 = (bf16[384,256]{1,0:T(8,128)(2,1)S(1)}, bf16[384,256]{1,0:T(8,128)(2,1)S(1)}, u32[]{:S(2)}, u32[]{:S(2)}) collective-permute-start(bf16[384,256]{1,0:T(8,128)(2,1)S(1)} %collective-permute-done.8.refs_0_.refs_8_), channel_id=1, source_target_pairs={{0,1},{1,0},{2,3},{3,2},{4,5},{5,4},{6,7},{7,6},{8,9},{9,8},{10,11... | collective-permute-start | bytes 589832 | tf_op jit(solution)/shard_map/ppermute | solution.py:381
  31.3 8.9 %collective-permute-start.10 = (bf16[96,1024]{1,0:T(8,128)(2,1)S(1)}, bf16[96,1024]{1,0:T(8,128)(2,1)S(1)}, u32[]{:S(2)}, u32[]{:S(2)}) collective-permute-start(bf16[96,1024]{1,0:T(8,128)(2,1)S(1)} %get-tuple-element.68), channel_id=1, source_target_pairs={{0,8},{8,0},{16,24},{24,16},{1,9},{9,1},{17,25},{25,17},{2,10},{10... | collective-permute-start | bytes 589832 | tf_op jit(solution)/shard_map/ppermute | solution.py:419
  32.9 11.0 %collective-permute-start.11 = (bf16[96,1024]{1,0:T(8,128)(2,1)S(1)}, bf16[96,1024]{1,0:T(8,128)(2,1)S(1)}, u32[]{:S(2)}, u32[]{:S(2)}) collective-permute-start(bf16[96,1024]{1,0:T(8,128)(2,1)S(1)} %get-tuple-element.69), channel_id=1, source_target_pairs={{0,16},{8,24},{16,0},{24,8},{1,17},{9,25},{17,1},{25,9},{2,18},{10... | collective-permute-start | bytes 589832 | tf_op jit(solution)/shard_map/ppermute | solution.py:419
  34.4 9.7 %collective-permute-start.12 = (bf16[96,1024]{1,0:T(8,128)(2,1)S(1)}, bf16[96,1024]{1,0:T(8,128)(2,1)S(1)}, u32[]{:S(2)}, u32[]{:S(2)}) collective-permute-start(bf16[96,1024]{1,0:T(8,128)(2,1)S(1)} %get-tuple-element.70), channel_id=1, source_target_pairs={{0,24},{8,16},{16,8},{24,0},{1,25},{9,17},{17,9},{25,1},{2,26},{10... | collective-permute-start | bytes 589832 | tf_op jit(solution)/shard_map/ppermute | solution.py:419
  40.2 7.9 %collective-permute-start.17 = (bf16[96,1024]{1,0:T(8,128)(2,1)S(1)}, bf16[96,1024]{1,0:T(8,128)(2,1)S(1)}, u32[]{:S(2)}, u32[]{:S(2)}) collective-permute-start(bf16[96,1024]{1,0:T(8,128)(2,1)S(1)} %get-tuple-element.78), channel_id=1, source_target_pairs={{0,8},{8,0},{16,24},{24,16},{1,9},{9,1},{17,25},{25,17},{2,10},{10... | collective-permute-start | bytes 589832 | tf_op jit(solution)/shard_map/ppermute | solution.py:419
  41.8 10.6 %collective-permute-start.18 = (bf16[96,1024]{1,0:T(8,128)(2,1)S(1)}, bf16[96,1024]{1,0:T(8,128)(2,1)S(1)}, u32[]{:S(2)}, u32[]{:S(2)}) collective-permute-start(bf16[96,1024]{1,0:T(8,128)(2,1)S(1)} %get-tuple-element.80), channel_id=1, source_target_pairs={{0,16},{8,24},{16,0},{24,8},{1,17},{9,25},{17,1},{25,9},{2,18},{10... | collective-permute-start | bytes 589832 | tf_op jit(solution)/shard_map/ppermute | solution.py:419
  43.3 9.1 %collective-permute-start.19 = (bf16[96,1024]{1,0:T(8,128)(2,1)S(1)}, bf16[96,1024]{1,0:T(8,128)(2,1)S(1)}, u32[]{:S(2)}, u32[]{:S(2)}) collective-permute-start(bf16[96,1024]{1,0:T(8,128)(2,1)S(1)} %get-tuple-element.82), channel_id=1, source_target_pairs={{0,24},{8,16},{16,8},{24,0},{1,25},{9,17},{17,9},{25,1},{2,26},{10... | collective-permute-start | bytes 589832 | tf_op jit(solution)/shard_map/ppermute | solution.py:419

commit v5 on v4

--- a/solution.py
+++ b/solution.py
@@ -333,13 +333,17 @@
     )(queries, shift, total, acc, *blocks, *every)
 
 
+def turns(parts):
+    return [0] + sorted(range(1, parts), key=lambda k: (-bin(k).count("1"), k))
+
+
 def place_kernel(heads, parts, *refs):
     pieces, out_ref, sems = refs[: heads * parts], refs[-2], refs[-1]
     me = lax.axis_index("heads")
     copies = []
     for head in range(heads):
-        for k in range(parts):
-            src = pieces[head * parts + k]
+        for i, k in enumerate(turns(parts)):
+            src = pieces[head * parts + i]
             cols = src.shape[1]
             start = pl.multiple_of(((me ^ k) * heads + head) * cols, cols)
             copies.append(
@@ -416,7 +420,7 @@
     def spread(self, outs, *earlier):
         out = [after(o, *earlier) if earlier else o for o in outs]
         perms = [[(i, i ^ k) for i in range(self.parts)] for k in range(self.parts)]
-        return [outs[0]] + [lax.ppermute(out[k], "heads", perms[k]) for k in range(1, self.parts)]
+        return [lax.ppermute(out[k], "heads", perms[k]) if k else outs[0] for k in turns(self.parts)]
 
 
 def in_turn(ex):
@@ -441,8 +445,9 @@
     latest = ex.call(one, [2], latest, share=0)
     ex.pass_on(two, 2, latest)
     ex.far[two].append(ex.up(ex.near[two][2], 3, 1))
-    latest = ex.call(two, [0, 1], latest)
+    latest = ex.call(two, [1], latest)
     ex.pass_on(one, 3, latest)
+    latest = ex.call(two, [0], latest, share=0)
     outs = ex.last(one, latest, share=0)
     pieces = ex.spread(outs)
     latest = ex.call(two, [2], outs[0], share=0)

time: 53.9 us -> 52.6 us (0.976)
  starting transfers between devices: 16.4 us -> 14.9 us
    ppermute x7, starting transfers between devices: 2.34 us -> 0.93 us  [across(): return lax.ppermute(block, 'ctx', self.swap)]
    pallas_call x4 -> x5, Pallas kernels: 9.37 us -> 9.32 us  [attend_next(): pl.pallas_call(functools.partial(next_kernel, groups, rows), in_specs=[vm...]
  transfers between devices with their start and end apart: 20 -> 20, of which waited for: 9 -> 8; matrix products, arithmetic and copies ran while one was open for 0% -> 0% of each run, Pallas kernels for 38% -> 38%
where the time goes in v5:
time: 52.6 us; the launch traced here: 52.4 us
  Pallas kernels  21.8 us (41%)
  starting transfers between devices  14.9 us (28%)
  waiting for transfers between devices  14.6 us (28%)
  local copies, waits for them, and re-layouts  0.74 us (1%)
    pallas_call x5, Pallas kernels, attend_next(): pl.pallas_call(functools.partial(next_kernel, groups, rows), in_specs=[vm...  9.32 us
    ppermute x6, waiting for transfers between devices, spread(): lax.ppermute(out[k], 'heads', perms[k])  8.68 us
    ppermute x6, starting transfers between devices, spread(): lax.ppermute(out[k], 'heads', perms[k])  7.11 us
    ppermute x7, starting transfers between devices, up(): return lax.ppermute(block, 'ctx', self.swap[:low] + top)  6.82 us
    pallas_call x2, Pallas kernels, attend_last(): pl.pallas_call(functools.partial(last_kernel, groups, len(blocks), len(ev...  5.83 us
    pallas_call x1, Pallas kernels, attend_first(): pl.pallas_call(functools.partial(first_kernel, len(owns), group, parts),...  4.96 us
    ppermute x7, waiting for transfers between devices, up(): return lax.ppermute(block, 'ctx', self.swap[:low] + top)  4.79 us
    pallas_call x1, Pallas kernels, place(): pl.pallas_call(functools.partial(place_kernel, heads, parts), in_specs=[p...  1.2 us
  transfers between devices with their start and end apart: 20, of which 8 were waited for; matrix products, arithmetic and copies ran while one was open for 0% of the time, Pallas kernels for 38%

profile of v5, /device:TPU:24, one launch (start us, length us, event | category | flops | bytes accessed | tf_op | source)
XLA Modules:
  0.0 52.4 jit_solution(16351196989295323923)
XLA Ops:
  0.0 0.0 copy-start
  0.0 0.0 copy-start.1
  0.0 0.0 copy-start.3
  0.0 0.7 %copy-done.3 = s32[384]{0:T(512)S(1)} copy-done((s32[384]{0:T(512)S(1)}, s32[384]{0:T(512)}, u32[]{:S(2)}) %copy-start.3) | copy-done | bytes 1560
  0.7 0.0 copy-start.2
  0.7 0.3 table.1.table_ref
  1.1 0.0 copy-done
  1.1 0.0 copy-done.1
  1.1 0.2 pack.1
  1.3 0.1 collective-permute-start
  1.4 0.1 collective-permute-start.1
  1.4 0.5 collective-permute-start.2
  1.9 1.7 %collective-permute-start.6 = (bf16[400,256]{1,0:T(8,128)(2,1)S(1)}, bf16[400,256]{1,0:T(8,128)(2,1)S(1)}, u32[]{:S(2)}, u32[]{:S(2)}) collective-permute-start(bf16[400,256]{1,0:T(8,128)(2,1)S(1)} %get-tuple-element.48.refs_1_.refs_2_), channel_id=1, source_target_pairs={{0,2},{1,3},{2,4},{3,5},{4,6},{5,7},{6,0},{7,1},{8,10},{9,11},{10,... | collective-permute-start | bytes 614408 | tf_op jit(solution)/shard_map/ppermute | solution.py:390
  3.6 0.0 copy-done.2
  3.7 5.0 %attend_first.1 = (bf16[128,3072]{1,0:T(8,128)(2,1)S(1)}, f32[1,3072]{1,0:T(1,128)S(1)}, f32[1,3072]{1,0:T(1,128)S(1)}, f32[128,3072]{1,0:T(8,128)S(1)}, bf16[12...) custom-call(bf16[384,2048]{1,0:T(8,128)(2,1)S(1)} %copy-done.2, ...), custom_call_target="tpu_custom_call" | custom-call | flops 2415919104 | tf_op jit(solution)/shard_map/attend_first/pallas_call | solution.py:185
  8.6 0.5 collective-permute-done.refs_1_.refs_4_
  9.1 0.0 collective-permute-done.1.refs_0_.refs_3_
  9.1 0.0 collective-permute-done.2.refs_0_.refs_3_
  9.1 0.0 collective-permute-start.3
  9.1 1.3 %collective-permute-start.4 = (bf16[384,256]{1,0:T(8,128)(2,1)S(1)}, bf16[384,256]{1,0:T(8,128)(2,1)S(1)}, u32[]{:S(2)}, u32[]{:S(2)}) collective-permute-start(bf16[384,256]{1,0:T(8,128)(2,1)S(1)} %collective-permute-done.refs_1_.refs_4_), channel_id=1, source_target_pairs={{0,1},{1,0},{2,4},{3,5},{4,6},{5,7},{6,2},{7,3},{8,9},{9,8},{10,12... | collective-permute-start | bytes 589832 | tf_op jit(solution)/shard_map/ppermute | solution.py:390
  10.5 2.0 %collective-permute-done.6.refs_0_.refs_4_ = bf16[400,256]{1,0:T(8,128)(2,1)S(1)} collective-permute-done((bf16[400,256]{1,0:T(8,128)(2,1)S(1)}, bf16[400,256]{1,0:T(8,128)(2,1)S(1)}, u32[]{:S(2)}, u32[]{:S(2)}) %collective-permute-start.6) | collective-permute-done | bytes 204832 | tf_op jit(solution)/shard_map/ppermute | solution.py:390
  12.4 0.0 collective-permute-start.7
  12.4 0.3 collective-permute-start.13
  12.7 0.0 collective-permute-done.3.refs_2_.refs_5_
  12.7 2.3 %attend_next.5 = (f32[1,3072]{1,0:T(1,128)S(1)}, f32[128,3072]{1,0:T(8,128)S(1)}) custom-call(bf16[128,3072]{1,0:T(8,128)(2,1)S(1)} %get-tuple-element.49.queries_ref, f32[1,3072]{1,0:T(1,128)S(1)} %get-tuple-element.50.shift_ref, f32[1,3072]{1,0:T(1,128)S(1)} %get-tuple-element.54.total_in, ...), custom_call_target="tpu_custom_call", output_to_operand_aliasing={{0}: (2, {}), {1}: (3, {})} | custom-call | flops 3623878656 | tf_op jit(solution)/shard_map/attend_next/pallas_call | solution.py:225
  15.0 1.9 %collective-permute-done.4.refs_0_.refs_6_ = bf16[384,256]{1,0:T(8,128)(2,1)S(1)} collective-permute-done((bf16[384,256]{1,0:T(8,128)(2,1)S(1)}, bf16[384,256]{1,0:T(8,128)(2,1)S(1)}, u32[]{:S(2)}, u32[]{:S(2)}) %collective-permute-start.4) | collective-permute-done | bytes 196640 | tf_op jit(solution)/shard_map/ppermute | solution.py:390
  16.9 0.0 collective-permute-start.5
  16.9 1.6 %collective-permute-start.8 = (bf16[384,256]{1,0:T(8,128)(2,1)S(1)}, bf16[384,256]{1,0:T(8,128)(2,1)S(1)}, u32[]{:S(2)}, u32[]{:S(2)}) collective-permute-start(bf16[384,256]{1,0:T(8,128)(2,1)S(1)} %collective-permute-done.4.refs_0_.refs_6_), channel_id=1, source_target_pairs={{0,1},{1,0},{2,3},{3,2},{4,6},{5,7},{6,4},{7,5},{8,9},{9,8},{10,11... | collective-permute-start | bytes 589832 | tf_op jit(solution)/shard_map/ppermute | solution.py:390
  18.5 0.0 collective-permute-done.5.refs_1_.refs_7_
  18.5 2.3 %attend_next.6 = (f32[1,3072]{1,0:T(1,128)S(1)}, f32[128,3072]{1,0:T(8,128)S(1)}) custom-call(bf16[128,3072]{1,0:T(8,128)(2,1)S(1)} %get-tuple-element.49.queries_ref, f32[1,3072]{1,0:T(1,128)S(1)} %get-tuple-element.50.shift_ref, f32[1,3072]{1,0:T(1,128)S(1)} %get-tuple-element.57.total_in, ...), custom_call_target="tpu_custom_call", output_to_operand_aliasing={{0}: (2, {}), {1}: (3, {})} | custom-call | tf_op jit(solution)/shard_map/attend_next/pallas_call | solution.py:225
  20.9 0.4 collective-permute-done.13.refs_0_.refs_6_
  21.3 0.0 collective-permute-start.14
  21.3 1.1 %collective-permute-start.15 = (bf16[400,256]{1,0:T(8,128)(2,1)S(1)}, bf16[400,256]{1,0:T(8,128)(2,1)S(1)}, u32[]{:S(2)}, u32[]{:S(2)}) collective-permute-start(bf16[400,256]{1,0:T(8,128)(2,1)S(1)} %collective-permute-done.13.refs_0_.refs_6_), channel_id=1, source_target_pairs={{0,1},{1,0},{2,3},{3,2},{4,6},{5,7},{6,4},{7,5},{8,9},{9,8},{10,11... | collective-permute-start | bytes 614408 | tf_op jit(solution)/shard_map/ppermute | solution.py:390
  22.4 0.8 %collective-permute-start.16 = (bf16[400,256]{1,0:T(8,128)(2,1)S(1)}, bf16[400,256]{1,0:T(8,128)(2,1)S(1)}, u32[]{:S(2)}, u32[]{:S(2)}) collective-permute-start(bf16[400,256]{1,0:T(8,128)(2,1)S(1)} %collective-permute-done.13.refs_0_.refs_6_), channel_id=1, source_target_pairs={{0,1},{1,0},{2,3},{3,2},{4,7},{5,6},{6,5},{7,4},{8,9},{9,8},{10,11... | collective-permute-start | bytes 614408 | tf_op jit(solution)/shard_map/ppermute | solution.py:390
  23.2 0.0 collective-permute-done.7.refs_1_.refs_5_
  23.2 2.4 %attend_next.7 = (f32[1,3072]{1,0:T(1,128)S(1)}, f32[128,3072]{1,0:T(8,128)S(1)}) custom-call(bf16[128,3072]{1,0:T(8,128)(2,1)S(1)} %get-tuple-element.61.queries_ref, f32[1,3072]{1,0:T(1,128)S(1)} %get-tuple-element.62.shift_ref, f32[1,3072]{1,0:T(1,128)S(1)} %get-tuple-element.63.total_in, ...), custom_call_target="tpu_custom_call", output_to_operand_aliasing={{0}: (2, {}), {1}: (3, {})} | custom-call | flops 2516582400 | tf_op jit(solution)/shard_map/attend_next/pallas_call | solution.py:225
  25.5 0.0 collective-permute-done.8.refs_0_.refs_8_
  25.5 0.3 collective-permute-start.9
  25.9 1.2 %collective-permute-done.9.refs_1_.refs_9_ = bf16[384,256]{1,0:T(8,128)(2,1)S(1)} collective-permute-done((bf16[384,256]{1,0:T(8,128)(2,1)S(1)}, bf16[384,256]{1,0:T(8,128)(2,1)S(1)}, u32[]{:S(2)}, u32[]{:S(2)}) %collective-permute-start.9) | collective-permute-done | bytes 196640 | tf_op jit(solution)/shard_map/ppermute | solution.py:385
  27.0 2.9 %attend_last.2 = (bf16[96,1024]{1,0:T(8,128)(2,1)S(1)}, bf16[96,1024]{1,0:T(8,128)(2,1)S(1)}, bf16[96,1024]{1,0:T(8,128)(2,1)S(1)}, bf16[96,1024]{1,0:T(8,128)(2,1)S(1)}) custom-call(bf16[128,3072]{1,0:T(8,128)(2,1)S(1)} %get-tuple-element.49.queries_ref, f32[1,3072]{1,0:T(1,128)S(1)} %get-tuple-element.50.shift_ref, ...), custom_call_target="tpu_custom_call" | custom-call | tf_op jit(solution)/shard_map/attend_last/pallas_call | solution.py:318
  30.0 2.5 %collective-permute-start.10 = (bf16[96,1024]{1,0:T(8,128)(2,1)S(1)}, bf16[96,1024]{1,0:T(8,128)(2,1)S(1)}, u32[]{:S(2)}, u32[]{:S(2)}) collective-permute-start(bf16[96,1024]{1,0:T(8,128)(2,1)S(1)} %get-tuple-element.74), channel_id=1, source_target_pairs={{0,24},{8,16},{16,8},{24,0},{1,25},{9,17},{17,9},{25,1},{2,26},{10... | collective-permute-start | bytes 589832 | tf_op jit(solution)/shard_map/ppermute | solution.py:423
  32.5 0.5 %collective-permute-start.11 = (bf16[96,1024]{1,0:T(8,128)(2,1)S(1)}, bf16[96,1024]{1,0:T(8,128)(2,1)S(1)}, u32[]{:S(2)}, u32[]{:S(2)}) collective-permute-start(bf16[96,1024]{1,0:T(8,128)(2,1)S(1)} %get-tuple-element.75), channel_id=1, source_target_pairs={{0,8},{8,0},{16,24},{24,16},{1,9},{9,1},{17,25},{25,17},{2,10},{10... | collective-permute-start | bytes 589832 | tf_op jit(solution)/shard_map/ppermute | solution.py:423
  33.0 0.0 collective-permute-done.14.refs_1_.refs_7_
  33.0 0.5 collective-permute-start.12
  33.5 2.3 %attend_next.9 = (f32[1,3072]{1,0:T(1,128)S(1)}, f32[128,3072]{1,0:T(8,128)S(1)}) custom-call(bf16[128,3072]{1,0:T(8,128)(2,1)S(1)} %get-tuple-element.61.queries_ref, f32[1,3072]{1,0:T(1,128)S(1)} %get-tuple-element.62.shift_ref, f32[1,3072]{1,0:T(1,128)S(1)} %get-tuple-element.77.total_in, ...), custom_call_target="tpu_custom_call", output_to_operand_aliasing={{0}: (2, {}), {1}: (3, {})} | custom-call | tf_op jit(solution)/shard_map/attend_next/pallas_call | solution.py:225
  35.8 0.0 collective-permute-done.15.refs_0_.refs_8_
  35.8 0.0 collective-permute-done.16.refs_1_.refs_9_
  35.8 2.9 %attend_last.3 = (bf16[96,1024]{1,0:T(8,128)(2,1)S(1)}, bf16[96,1024]{1,0:T(8,128)(2,1)S(1)}, bf16[96,1024]{1,0:T(8,128)(2,1)S(1)}, bf16[96,1024]{1,0:T(8,128)(2,1)S(1)}) custom-call(bf16[128,3072]{1,0:T(8,128)(2,1)S(1)} %get-tuple-element.61.queries_ref, f32[1,3072]{1,0:T(1,128)S(1)} %get-tuple-element.62.shift_ref, ...), custom_call_target="tpu_custom_call" | custom-call | flops 2516582400 | tf_op jit(solution)/shard_map/attend_last/pallas_call | solution.py:318
  38.8 0.0 collective-permute-done.10.refs_1_
  38.8 2.5 %collective-permute-start.17 = (bf16[96,1024]{1,0:T(8,128)(2,1)S(1)}, bf16[96,1024]{1,0:T(8,128)(2,1)S(1)}, u32[]{:S(2)}, u32[]{:S(2)}) collective-permute-start(bf16[96,1024]{1,0:T(8,128)(2,1)S(1)} %get-tuple-element.84), channel_id=1, source_target_pairs={{0,24},{8,16},{16,8},{24,0},{1,25},{9,17},{17,9},{25,1},{2,26},{10... | collective-permute-start | bytes 589832 | tf_op jit(solution)/shard_map/ppermute | solution.py:423
  41.3 0.5 %collective-permute-start.18 = (bf16[96,1024]{1,0:T(8,128)(2,1)S(1)}, bf16[96,1024]{1,0:T(8,128)(2,1)S(1)}, u32[]{:S(2)}, u32[]{:S(2)}) collective-permute-start(bf16[96,1024]{1,0:T(8,128)(2,1)S(1)} %get-tuple-element.86), channel_id=1, source_target_pairs={{0,8},{8,0},{16,24},{24,16},{1,9},{9,1},{17,25},{25,17},{2,10},{10... | collective-permute-start | bytes 589832 | tf_op jit(solution)/shard_map/ppermute | solution.py:423
  41.8 0.5 collective-permute-start.19
  42.3 0.6 %collective-permute-done.11.refs_2_ = bf16[96,1024]{1,0:T(8,128)(2,1)S(1)} collective-permute-done((bf16[96,1024]{1,0:T(8,128)(2,1)S(1)}, bf16[96,1024]{1,0:T(8,128)(2,1)S(1)}, u32[]{:S(2)}, u32[]{:S(2)}) %collective-permute-start.11) | collective-permute-done | bytes 196640 | tf_op jit(solution)/shard_map/ppermute | solution.py:423
  42.9 0.0 collective-permute-done.12.refs_3_
  42.9 4.7 %collective-permute-done.17.refs_5_ = bf16[96,1024]{1,0:T(8,128)(2,1)S(1)} collective-permute-done((bf16[96,1024]{1,0:T(8,128)(2,1)S(1)}, bf16[96,1024]{1,0:T(8,128)(2,1)S(1)}, u32[]{:S(2)}, u32[]{:S(2)}) %collective-permute-start.17) | collective-permute-done | bytes 196640 | tf_op jit(solution)/shard_map/ppermute | solution.py:423
  47.6 3.4 %collective-permute-done.18.refs_6_ = bf16[96,1024]{1,0:T(8,128)(2,1)S(1)} collective-permute-done((bf16[96,1024]{1,0:T(8,128)(2,1)S(1)}, bf16[96,1024]{1,0:T(8,128)(2,1)S(1)}, u32[]{:S(2)}, u32[]{:S(2)}) %collective-permute-start.18) | collective-permute-done | bytes 196640 | tf_op jit(solution)/shard_map/ppermute | solution.py:423
  51.0 0.0 collective-permute-done.19.refs_7_
  51.0 1.2 %place.1 = bf16[96,8192]{1,0:T(8,128)(2,1)} custom-call(bf16[96,1024]{1,0:T(8,128)(2,1)S(1)} %get-tuple-element.73.refs_0_, bf16[96,1024]{1,0:T(8,128)(2,1)S(1)} %collective-permute-done.10.refs_1_, bf16[96,1024]{1,0:T(8,128)(2,1)S(1)} %collective-permute-done.11.refs_2_, bf16[96,1024]{1,0:T(8,128)(2,1)S(1)} %collective-permute-done.12.refs_3_, ...), custom_call_target="tpu_custom_call" | custom-call | tf_op jit(solution)/shard_map/place/pallas_call | solution.py:360
  (1 shorter events, 0.0 us)
Async XLA Ops:
  0.0 1.1 %copy-start = (bf16[384,256]{1,0:T(8,128)(2,1)S(1)}, bf16[384,256]{1,0:T(8,128)(2,1)}, u32[]{:S(2)}) copy-start(bf16[384,256]{1,0:T(8,128)(2,1)} %k_ref.1) | copy-start | bytes 589828
  0.0 1.1 %copy-start.1 = (bf16[384,256]{1,0:T(8,128)(2,1)S(1)}, bf16[384,256]{1,0:T(8,128)(2,1)}, u32[]{:S(2)}) copy-start(bf16[384,256]{1,0:T(8,128)(2,1)} %v_ref.1) | copy-start | bytes 589828
  0.0 0.7 %copy-start.3 = (s32[384]{0:T(512)S(1)}, s32[384]{0:T(512)}, u32[]{:S(2)}) copy-start(s32[384]{0:T(512)} %pos_ref.1) | copy-start | bytes 4612
  0.7 2.9 %copy-start.2 = (bf16[384,2048]{1,0:T(8,128)(2,1)S(1)}, bf16[384,2048]{1,0:T(8,128)(2,1)}, u32[]{:S(2)}) copy-start(bf16[384,2048]{1,0:T(8,128)(2,1)} %q_ref.1) | copy-start | bytes 4718596
  1.3 7.8 %collective-permute-start = (bf16[384,256]{1,0:T(8,128)(2,1)S(1)}, bf16[384,256]{1,0:T(8,128)(2,1)S(1)}, u32[]{:S(2)}, u32[]{:S(2)}) collective-permute-start(bf16[384,256]{1,0:T(8,128)(2,1)S(1)} %get-tuple-element.47.refs_0_.refs_2_), channel_id=1, source_target_pairs={{0,2},{1,3},{2,4},{3,5},{4,6},{5,7},{6,0},{7,1},{8,10},{9,11},{10,... | collective-permute-start | bytes 589832 | tf_op jit(solution)/shard_map/ppermute | solution.py:390
  1.4 7.8 %collective-permute-start.1 = (bf16[384,256]{1,0:T(8,128)(2,1)S(1)}, bf16[384,256]{1,0:T(8,128)(2,1)S(1)}, u32[]{:S(2)}, u32[]{:S(2)}) collective-permute-start(bf16[384,256]{1,0:T(8,128)(2,1)S(1)} %get-tuple-element.47.refs_0_.refs_2_), channel_id=1, source_target_pairs={{0,1},{1,0},{2,3},{3,2},{4,5},{5,4},{6,7},{7,6},{8,9},{9,8},{10,11... | collective-permute-start | bytes 589832 | tf_op jit(solution)/shard_map/ppermute | solution.py:385
  1.4 7.7 %collective-permute-start.2 = (bf16[400,256]{1,0:T(8,128)(2,1)S(1)}, bf16[400,256]{1,0:T(8,128)(2,1)S(1)}, u32[]{:S(2)}, u32[]{:S(2)}) collective-permute-start(bf16[400,256]{1,0:T(8,128)(2,1)S(1)} %get-tuple-element.48.refs_1_.refs_2_), channel_id=1, source_target_pairs={{0,1},{1,0},{2,3},{3,2},{4,5},{5,4},{6,7},{7,6},{8,9},{9,8},{10,11... | collective-permute-start | bytes 614408 | tf_op jit(solution)/shard_map/ppermute | solution.py:385
  1.9 10.5 %collective-permute-start.6 = (bf16[400,256]{1,0:T(8,128)(2,1)S(1)}, bf16[400,256]{1,0:T(8,128)(2,1)S(1)}, u32[]{:S(2)}, u32[]{:S(2)}) collective-permute-start(bf16[400,256]{1,0:T(8,128)(2,1)S(1)} %get-tuple-element.48.refs_1_.refs_2_), channel_id=1, source_target_pairs={{0,2},{1,3},{2,4},{3,5},{4,6},{5,7},{6,0},{7,1},{8,10},{9,11},{10,... | collective-permute-start | bytes 614408 | tf_op jit(solution)/shard_map/ppermute | solution.py:390
  9.1 3.6 %collective-permute-start.3 = (bf16[384,256]{1,0:T(8,128)(2,1)S(1)}, bf16[384,256]{1,0:T(8,128)(2,1)S(1)}, u32[]{:S(2)}, u32[]{:S(2)}) collective-permute-start(bf16[384,256]{1,0:T(8,128)(2,1)S(1)} %collective-permute-done.refs_1_.refs_4_), channel_id=1, source_target_pairs={{0,1},{1,0},{2,3},{3,2},{4,5},{5,4},{6,7},{7,6},{8,9},{9,8},{10,11... | collective-permute-start | bytes 589832 | tf_op jit(solution)/shard_map/ppermute | solution.py:385
  9.1 7.8 %collective-permute-start.4 = (bf16[384,256]{1,0:T(8,128)(2,1)S(1)}, bf16[384,256]{1,0:T(8,128)(2,1)S(1)}, u32[]{:S(2)}, u32[]{:S(2)}) collective-permute-start(bf16[384,256]{1,0:T(8,128)(2,1)S(1)} %collective-permute-done.refs_1_.refs_4_), channel_id=1, source_target_pairs={{0,1},{1,0},{2,4},{3,5},{4,6},{5,7},{6,2},{7,3},{8,9},{9,8},{10,12... | collective-permute-start | bytes 589832 | tf_op jit(solution)/shard_map/ppermute | solution.py:390
  12.4 10.7 %collective-permute-start.7 = (bf16[400,256]{1,0:T(8,128)(2,1)S(1)}, bf16[400,256]{1,0:T(8,128)(2,1)S(1)}, u32[]{:S(2)}, u32[]{:S(2)}) collective-permute-start(bf16[400,256]{1,0:T(8,128)(2,1)S(1)} %collective-permute-done.6.refs_0_.refs_4_), channel_id=1, source_target_pairs={{0,1},{1,0},{2,3},{3,2},{4,5},{5,4},{6,7},{7,6},{8,9},{9,8},{10,11... | collective-permute-start | bytes 614408 | tf_op jit(solution)/shard_map/ppermute | solution.py:385
  12.4 8.9 %collective-permute-start.13 = (bf16[400,256]{1,0:T(8,128)(2,1)S(1)}, bf16[400,256]{1,0:T(8,128)(2,1)S(1)}, u32[]{:S(2)}, u32[]{:S(2)}) collective-permute-start(bf16[400,256]{1,0:T(8,128)(2,1)S(1)} %collective-permute-done.6.refs_0_.refs_4_), channel_id=1, source_target_pairs={{0,1},{1,0},{2,4},{3,5},{4,6},{5,7},{6,2},{7,3},{8,9},{9,8},{10,12... | collective-permute-start | bytes 614408 | tf_op jit(solution)/shard_map/ppermute | solution.py:390
  16.9 1.6 %collective-permute-start.5 = (bf16[384,256]{1,0:T(8,128)(2,1)S(1)}, bf16[384,256]{1,0:T(8,128)(2,1)S(1)}, u32[]{:S(2)}, u32[]{:S(2)}) collective-permute-start(bf16[384,256]{1,0:T(8,128)(2,1)S(1)} %collective-permute-done.4.refs_0_.refs_6_), channel_id=1, source_target_pairs={{0,1},{1,0},{2,3},{3,2},{4,5},{5,4},{6,7},{7,6},{8,9},{9,8},{10,11... | collective-permute-start | bytes 589832 | tf_op jit(solution)/shard_map/ppermute | solution.py:385
  16.9 8.6 %collective-permute-start.8 = (bf16[384,256]{1,0:T(8,128)(2,1)S(1)}, bf16[384,256]{1,0:T(8,128)(2,1)S(1)}, u32[]{:S(2)}, u32[]{:S(2)}) collective-permute-start(bf16[384,256]{1,0:T(8,128)(2,1)S(1)} %collective-permute-done.4.refs_0_.refs_6_), channel_id=1, source_target_pairs={{0,1},{1,0},{2,3},{3,2},{4,6},{5,7},{6,4},{7,5},{8,9},{9,8},{10,11... | collective-permute-start | bytes 589832 | tf_op jit(solution)/shard_map/ppermute | solution.py:390
  21.3 11.7 %collective-permute-start.14 = (bf16[400,256]{1,0:T(8,128)(2,1)S(1)}, bf16[400,256]{1,0:T(8,128)(2,1)S(1)}, u32[]{:S(2)}, u32[]{:S(2)}) collective-permute-start(bf16[400,256]{1,0:T(8,128)(2,1)S(1)} %collective-permute-done.13.refs_0_.refs_6_), channel_id=1, source_target_pairs={{0,1},{1,0},{2,3},{3,2},{4,5},{5,4},{6,7},{7,6},{8,9},{9,8},{10,11... | collective-permute-start | bytes 614408 | tf_op jit(solution)/shard_map/ppermute | solution.py:385
  21.3 14.5 %collective-permute-start.15 = (bf16[400,256]{1,0:T(8,128)(2,1)S(1)}, bf16[400,256]{1,0:T(8,128)(2,1)S(1)}, u32[]{:S(2)}, u32[]{:S(2)}) collective-permute-start(bf16[400,256]{1,0:T(8,128)(2,1)S(1)} %collective-permute-done.13.refs_0_.refs_6_), channel_id=1, source_target_pairs={{0,1},{1,0},{2,3},{3,2},{4,6},{5,7},{6,4},{7,5},{8,9},{9,8},{10,11... | collective-permute-start | bytes 614408 | tf_op jit(solution)/shard_map/ppermute | solution.py:390
  22.4 13.5 %collective-permute-start.16 = (bf16[400,256]{1,0:T(8,128)(2,1)S(1)}, bf16[400,256]{1,0:T(8,128)(2,1)S(1)}, u32[]{:S(2)}, u32[]{:S(2)}) collective-permute-start(bf16[400,256]{1,0:T(8,128)(2,1)S(1)} %collective-permute-done.13.refs_0_.refs_6_), channel_id=1, source_target_pairs={{0,1},{1,0},{2,3},{3,2},{4,7},{5,6},{6,5},{7,4},{8,9},{9,8},{10,11... | collective-permute-start | bytes 614408 | tf_op jit(solution)/shard_map/ppermute | solution.py:390
  25.5 1.5 %collective-permute-start.9 = (bf16[384,256]{1,0:T(8,128)(2,1)S(1)}, bf16[384,256]{1,0:T(8,128)(2,1)S(1)}, u32[]{:S(2)}, u32[]{:S(2)}) collective-permute-start(bf16[384,256]{1,0:T(8,128)(2,1)S(1)} %collective-permute-done.8.refs_0_.refs_8_), channel_id=1, source_target_pairs={{0,1},{1,0},{2,3},{3,2},{4,5},{5,4},{6,7},{7,6},{8,9},{9,8},{10,11... | collective-permute-start | bytes 589832 | tf_op jit(solution)/shard_map/ppermute | solution.py:385
  30.0 8.8 %collective-permute-start.10 = (bf16[96,1024]{1,0:T(8,128)(2,1)S(1)}, bf16[96,1024]{1,0:T(8,128)(2,1)S(1)}, u32[]{:S(2)}, u32[]{:S(2)}) collective-permute-start(bf16[96,1024]{1,0:T(8,128)(2,1)S(1)} %get-tuple-element.74), channel_id=1, source_target_pairs={{0,24},{8,16},{16,8},{24,0},{1,25},{9,17},{17,9},{25,1},{2,26},{10... | collective-permute-start | bytes 589832 | tf_op jit(solution)/shard_map/ppermute | solution.py:423
  32.5 10.5 %collective-permute-start.11 = (bf16[96,1024]{1,0:T(8,128)(2,1)S(1)}, bf16[96,1024]{1,0:T(8,128)(2,1)S(1)}, u32[]{:S(2)}, u32[]{:S(2)}) collective-permute-start(bf16[96,1024]{1,0:T(8,128)(2,1)S(1)} %get-tuple-element.75), channel_id=1, source_target_pairs={{0,8},{8,0},{16,24},{24,16},{1,9},{9,1},{17,25},{25,17},{2,10},{10... | collective-permute-start | bytes 589832 | tf_op jit(solution)/shard_map/ppermute | solution.py:423
  33.0 9.9 %collective-permute-start.12 = (bf16[96,1024]{1,0:T(8,128)(2,1)S(1)}, bf16[96,1024]{1,0:T(8,128)(2,1)S(1)}, u32[]{:S(2)}, u32[]{:S(2)}) collective-permute-start(bf16[96,1024]{1,0:T(8,128)(2,1)S(1)} %get-tuple-element.76), channel_id=1, source_target_pairs={{0,16},{8,24},{16,0},{24,8},{1,17},{9,25},{17,1},{25,9},{2,18},{10... | collective-permute-start | bytes 589832 | tf_op jit(solution)/shard_map/ppermute | solution.py:423
  38.8 8.8 %collective-permute-start.17 = (bf16[96,1024]{1,0:T(8,128)(2,1)S(1)}, bf16[96,1024]{1,0:T(8,128)(2,1)S(1)}, u32[]{:S(2)}, u32[]{:S(2)}) collective-permute-start(bf16[96,1024]{1,0:T(8,128)(2,1)S(1)} %get-tuple-element.84), channel_id=1, source_target_pairs={{0,24},{8,16},{16,8},{24,0},{1,25},{9,17},{17,9},{25,1},{2,26},{10... | collective-permute-start | bytes 589832 | tf_op jit(solution)/shard_map/ppermute | solution.py:423
  41.3 9.7 %collective-permute-start.18 = (bf16[96,1024]{1,0:T(8,128)(2,1)S(1)}, bf16[96,1024]{1,0:T(8,128)(2,1)S(1)}, u32[]{:S(2)}, u32[]{:S(2)}) collective-permute-start(bf16[96,1024]{1,0:T(8,128)(2,1)S(1)} %get-tuple-element.86), channel_id=1, source_target_pairs={{0,8},{8,0},{16,24},{24,16},{1,9},{9,1},{17,25},{25,17},{2,10},{10... | collective-permute-start | bytes 589832 | tf_op jit(solution)/shard_map/ppermute | solution.py:423
  41.8 9.2 %collective-permute-start.19 = (bf16[96,1024]{1,0:T(8,128)(2,1)S(1)}, bf16[96,1024]{1,0:T(8,128)(2,1)S(1)}, u32[]{:S(2)}, u32[]{:S(2)}) collective-permute-start(bf16[96,1024]{1,0:T(8,128)(2,1)S(1)} %get-tuple-element.88), channel_id=1, source_target_pairs={{0,16},{8,24},{16,0},{24,8},{1,17},{9,25},{17,1},{25,9},{2,18},{10... | collective-permute-start | bytes 589832 | tf_op jit(solution)/shard_map/ppermute | solution.py:423

commit v6 on v5

--- a/solution.py
+++ b/solution.py
@@ -150,7 +150,7 @@
             acc_ref[:, cols] = mixed[:HD]
         return carry
 
-    lax.fori_loop(0, width // tile, step, 0)
+    lax.fori_loop(0, width // tile, step, 0, unroll=True)
 
 
 def first_kernel(heads, group, parts, q_ref, table_ref, *refs):
@@ -337,18 +337,14 @@
     return [0] + sorted(range(1, parts), key=lambda k: (-bin(k).count("1"), k))
 
 
-def place_kernel(heads, parts, *refs):
-    pieces, out_ref, sems = refs[: heads * parts], refs[-2], refs[-1]
+def place_kernel(heads, parts, head, *refs):
+    pieces, out_ref, sems = refs[-2 - parts : -2], refs[-2], refs[-1]
     me = lax.axis_index("heads")
     copies = []
-    for head in range(heads):
-        for i, k in enumerate(turns(parts)):
-            src = pieces[head * parts + i]
-            cols = src.shape[1]
-            start = pl.multiple_of(((me ^ k) * heads + head) * cols, cols)
-            copies.append(
-                pltpu.make_async_copy(src, out_ref.at[:, pl.ds(start, cols)], sems.at[len(copies)])
-            )
+    for i, k in enumerate(turns(parts)):
+        cols = pieces[i].shape[1]
+        start = pl.multiple_of(((me ^ k) * heads + head) * cols, cols)
+        copies.append(pltpu.make_async_copy(pieces[i], out_ref.at[:, pl.ds(start, cols)], sems.at[i]))
     for c in copies:
         c.start()
     for c in copies:
@@ -357,15 +353,22 @@
 
 def place(pieces, heads, parts):
     rows, cols = pieces[0].shape
-    return pl.pallas_call(
-        functools.partial(place_kernel, heads, parts),
-        in_specs=[pl.BlockSpec(memory_space=pltpu.VMEM)] * len(pieces),
-        out_specs=pl.BlockSpec(memory_space=pl.ANY),
-        out_shape=jax.ShapeDtypeStruct((rows, cols * len(pieces)), jnp.bfloat16),
-        compiler_params=pltpu.CompilerParams(vmem_limit_bytes=16 << 20),
-        scratch_shapes=[pltpu.SemaphoreType.DMA((len(pieces),))],
-        name="place",
-    )(*pieces)
+    vmem, anywhere = pl.BlockSpec(memory_space=pltpu.VMEM), pl.BlockSpec(memory_space=pl.ANY)
+    out = ()
+    for head in range(heads):
+        out = (
+            pl.pallas_call(
+                functools.partial(place_kernel, heads, parts, head),
+                in_specs=[anywhere] * len(out) + [vmem] * parts,
+                out_specs=anywhere,
+                out_shape=jax.ShapeDtypeStruct((rows, cols * heads * parts), jnp.bfloat16),
+                input_output_aliases={0: 0} if out else {},
+                compiler_params=pltpu.CompilerParams(vmem_limit_bytes=16 << 20),
+                scratch_shapes=[pltpu.SemaphoreType.DMA((parts,))],
+                name="place",
+            )(*out, *pieces[head * parts : (head + 1) * parts]),
+        )
+    return out[0]
 
 
 def after(value, *earlier):

time: 52.6 us -> 51.9 us (0.987)
  starting transfers between devices: 14.9 us -> 14 us
  waiting for transfers between devices: 14.6 us -> 15.4 us
  Pallas kernels: 21.8 us -> 21.2 us
    ppermute x7, waiting for transfers between devices: 4.79 us -> 6.04 us  [up(): return lax.ppermute(block, 'ctx', self.swap[:low] + top)]
    ppermute x6, waiting for transfers between devices: 8.68 us -> 8 us  [spread(): lax.ppermute(out[k], 'heads', perms[k])]
    ppermute x7, starting transfers between devices: 6.82 us -> 6.18 us  [up(): return lax.ppermute(block, 'ctx', self.swap[:low] + top)]
    pallas_call x1 -> x2, Pallas kernels: 1.2 us -> 1.81 us  [place(): pl.pallas_call(functools.partial(place_kernel, heads, parts, head), in_sp...]
  transfers between devices with their start and end apart: 20 -> 20, of which waited for: 8 -> 11; matrix products, arithmetic and copies ran while one was open for 0% -> 0% of each run, Pallas kernels for 38% -> 38%
where the time goes in v6:
time: 51.9 us; the launch traced here: 51.7 us
  Pallas kernels  21.2 us (41%)
  waiting for transfers between devices  15.4 us (30%)
  starting transfers between devices  14 us (27%)
  local copies, waits for them, and re-layouts  0.74 us (1%)
    pallas_call x5, Pallas kernels, attend_next(): pl.pallas_call(functools.partial(next_kernel, groups, rows), in_specs=[vm...  8.81 us
    ppermute x6, waiting for transfers between devices, spread(): lax.ppermute(out[k], 'heads', perms[k])  8 us
    ppermute x6, starting transfers between devices, spread(): lax.ppermute(out[k], 'heads', perms[k])  7.04 us
    ppermute x7, starting transfers between devices, up(): return lax.ppermute(block, 'ctx', self.swap[:low] + top)  6.18 us
    ppermute x7, waiting for transfers between devices, up(): return lax.ppermute(block, 'ctx', self.swap[:low] + top)  6.04 us
    pallas_call x2, Pallas kernels, attend_last(): pl.pallas_call(functools.partial(last_kernel, groups, len(blocks), len(ev...  5.51 us
    pallas_call x1, Pallas kernels, attend_first(): pl.pallas_call(functools.partial(first_kernel, len(owns), group, parts),...  4.59 us
    pallas_call x2, Pallas kernels, place(): pl.pallas_call(functools.partial(place_kernel, heads, parts, head), in_sp...  1.81 us
  transfers between devices with their start and end apart: 20, of which 11 were waited for; matrix products, arithmetic and copies ran while one was open for 0% of the time, Pallas kernels for 38%

profile of v6, /device:TPU:24, one launch (start us, length us, event | category | flops | bytes accessed | tf_op | source)
XLA Modules:
  0.0 51.7 jit_solution(5593807949629548140)
XLA Ops:
  0.0 0.0 copy-start
  0.0 0.0 copy-start.1
  0.0 0.0 copy-start.3
  0.0 0.7 %copy-done.3 = s32[384]{0:T(512)S(1)} copy-done((s32[384]{0:T(512)S(1)}, s32[384]{0:T(512)}, u32[]{:S(2)}) %copy-start.3) | copy-done | bytes 1560
  0.7 0.0 copy-start.2
  0.7 0.3 table.1.table_ref
  1.1 0.0 copy-done
  1.1 0.0 copy-done.1
  1.1 0.2 pack.1
  1.3 0.1 collective-permute-start
  1.4 0.1 collective-permute-start.1
  1.4 0.5 collective-permute-start.2
  1.9 1.7 %collective-permute-start.6 = (bf16[400,256]{1,0:T(8,128)(2,1)S(1)}, bf16[400,256]{1,0:T(8,128)(2,1)S(1)}, u32[]{:S(2)}, u32[]{:S(2)}) collective-permute-start(bf16[400,256]{1,0:T(8,128)(2,1)S(1)} %get-tuple-element.48.refs_1_.refs_2_), channel_id=1, source_target_pairs={{0,2},{1,3},{2,4},{3,5},{4,6},{5,7},{6,0},{7,1},{8,10},{9,11},{10,... | collective-permute-start | bytes 614408 | tf_op jit(solution)/shard_map/ppermute | solution.py:393
  3.6 0.0 copy-done.2
  3.7 4.6 %attend_first.1 = (bf16[128,3072]{1,0:T(8,128)(2,1)S(1)}, f32[1,3072]{1,0:T(1,128)S(1)}, f32[1,3072]{1,0:T(1,128)S(1)}, f32[128,3072]{1,0:T(8,128)S(1)}, bf16[12...) custom-call(bf16[384,2048]{1,0:T(8,128)(2,1)S(1)} %copy-done.2, ...), custom_call_target="tpu_custom_call" | custom-call | flops 2415919104 | tf_op jit(solution)/shard_map/attend_first/pallas_call | solution.py:185
  8.2 0.9 %collective-permute-done.refs_1_.refs_4_ = bf16[384,256]{1,0:T(8,128)(2,1)S(1)} collective-permute-done((bf16[384,256]{1,0:T(8,128)(2,1)S(1)}, bf16[384,256]{1,0:T(8,128)(2,1)S(1)}, u32[]{:S(2)}, u32[]{:S(2)}) %collective-permute-start) | collective-permute-done | bytes 196640 | tf_op jit(solution)/shard_map/ppermute | solution.py:393
  9.1 0.0 collective-permute-done.1.refs_0_.refs_3_
  9.1 0.0 collective-permute-done.2.refs_0_.refs_3_
  9.1 0.0 collective-permute-start.3
  9.1 0.9 %collective-permute-start.4 = (bf16[384,256]{1,0:T(8,128)(2,1)S(1)}, bf16[384,256]{1,0:T(8,128)(2,1)S(1)}, u32[]{:S(2)}, u32[]{:S(2)}) collective-permute-start(bf16[384,256]{1,0:T(8,128)(2,1)S(1)} %collective-permute-done.refs_1_.refs_4_), channel_id=1, source_target_pairs={{0,1},{1,0},{2,4},{3,5},{4,6},{5,7},{6,2},{7,3},{8,9},{9,8},{10,12... | collective-permute-start | bytes 589832 | tf_op jit(solution)/shard_map/ppermute | solution.py:393
  10.1 2.3 %collective-permute-done.6.refs_0_.refs_4_ = bf16[400,256]{1,0:T(8,128)(2,1)S(1)} collective-permute-done((bf16[400,256]{1,0:T(8,128)(2,1)S(1)}, bf16[400,256]{1,0:T(8,128)(2,1)S(1)}, u32[]{:S(2)}, u32[]{:S(2)}) %collective-permute-start.6) | collective-permute-done | bytes 204832 | tf_op jit(solution)/shard_map/ppermute | solution.py:393
  12.4 0.0 collective-permute-start.7
  12.4 0.3 collective-permute-start.13
  12.7 0.0 collective-permute-done.3.refs_2_.refs_5_
  12.7 2.2 %attend_next.5 = (f32[1,3072]{1,0:T(1,128)S(1)}, f32[128,3072]{1,0:T(8,128)S(1)}) custom-call(bf16[128,3072]{1,0:T(8,128)(2,1)S(1)} %get-tuple-element.49.queries_ref, f32[1,3072]{1,0:T(1,128)S(1)} %get-tuple-element.50.shift_ref, f32[1,3072]{1,0:T(1,128)S(1)} %get-tuple-element.54.total_in, ...), custom_call_target="tpu_custom_call", output_to_operand_aliasing={{0}: (2, {}), {1}: (3, {})} | custom-call | flops 3623878656 | tf_op jit(solution)/shard_map/attend_next/pallas_call | solution.py:225
  14.9 2.0 %collective-permute-done.4.refs_0_.refs_6_ = bf16[384,256]{1,0:T(8,128)(2,1)S(1)} collective-permute-done((bf16[384,256]{1,0:T(8,128)(2,1)S(1)}, bf16[384,256]{1,0:T(8,128)(2,1)S(1)}, u32[]{:S(2)}, u32[]{:S(2)}) %collective-permute-start.4) | collective-permute-done | bytes 196640 | tf_op jit(solution)/shard_map/ppermute | solution.py:393
  16.9 0.0 collective-permute-start.5
  16.9 1.3 %collective-permute-start.8 = (bf16[384,256]{1,0:T(8,128)(2,1)S(1)}, bf16[384,256]{1,0:T(8,128)(2,1)S(1)}, u32[]{:S(2)}, u32[]{:S(2)}) collective-permute-start(bf16[384,256]{1,0:T(8,128)(2,1)S(1)} %collective-permute-done.4.refs_0_.refs_6_), channel_id=1, source_target_pairs={{0,1},{1,0},{2,3},{3,2},{4,6},{5,7},{6,4},{7,5},{8,9},{9,8},{10,11... | collective-permute-start | bytes 589832 | tf_op jit(solution)/shard_map/ppermute | solution.py:393
  18.2 0.1 collective-permute-done.5.refs_1_.refs_7_
  18.3 2.2 %attend_next.6 = (f32[1,3072]{1,0:T(1,128)S(1)}, f32[128,3072]{1,0:T(8,128)S(1)}) custom-call(bf16[128,3072]{1,0:T(8,128)(2,1)S(1)} %get-tuple-element.49.queries_ref, f32[1,3072]{1,0:T(1,128)S(1)} %get-tuple-element.50.shift_ref, f32[1,3072]{1,0:T(1,128)S(1)} %get-tuple-element.57.total_in, ...), custom_call_target="tpu_custom_call", output_to_operand_aliasing={{0}: (2, {}), {1}: (3, {})} | custom-call | tf_op jit(solution)/shard_map/attend_next/pallas_call | solution.py:225
  20.6 0.7 %collective-permute-done.13.refs_0_.refs_6_ = bf16[400,256]{1,0:T(8,128)(2,1)S(1)} collective-permute-done((bf16[400,256]{1,0:T(8,128)(2,1)S(1)}, bf16[400,256]{1,0:T(8,128)(2,1)S(1)}, u32[]{:S(2)}, u32[]{:S(2)}) %collective-permute-start.13) | collective-permute-done | bytes 204832 | tf_op jit(solution)/shard_map/ppermute | solution.py:393
  21.3 0.0 collective-permute-start.14
  21.3 0.7 %collective-permute-start.15 = (bf16[400,256]{1,0:T(8,128)(2,1)S(1)}, bf16[400,256]{1,0:T(8,128)(2,1)S(1)}, u32[]{:S(2)}, u32[]{:S(2)}) collective-permute-start(bf16[400,256]{1,0:T(8,128)(2,1)S(1)} %collective-permute-done.13.refs_0_.refs_6_), channel_id=1, source_target_pairs={{0,1},{1,0},{2,3},{3,2},{4,6},{5,7},{6,4},{7,5},{8,9},{9,8},{10,11... | collective-permute-start | bytes 614408 | tf_op jit(solution)/shard_map/ppermute | solution.py:393
  22.0 1.2 %collective-permute-start.16 = (bf16[400,256]{1,0:T(8,128)(2,1)S(1)}, bf16[400,256]{1,0:T(8,128)(2,1)S(1)}, u32[]{:S(2)}, u32[]{:S(2)}) collective-permute-start(bf16[400,256]{1,0:T(8,128)(2,1)S(1)} %collective-permute-done.13.refs_0_.refs_6_), channel_id=1, source_target_pairs={{0,1},{1,0},{2,3},{3,2},{4,7},{5,6},{6,5},{7,4},{8,9},{9,8},{10,11... | collective-permute-start | bytes 614408 | tf_op jit(solution)/shard_map/ppermute | solution.py:393
  23.2 0.0 collective-permute-done.7.refs_1_.refs_5_
  23.2 2.2 %attend_next.7 = (f32[1,3072]{1,0:T(1,128)S(1)}, f32[128,3072]{1,0:T(8,128)S(1)}) custom-call(bf16[128,3072]{1,0:T(8,128)(2,1)S(1)} %get-tuple-element.61.queries_ref, f32[1,3072]{1,0:T(1,128)S(1)} %get-tuple-element.62.shift_ref, f32[1,3072]{1,0:T(1,128)S(1)} %get-tuple-element.63.total_in, ...), custom_call_target="tpu_custom_call", output_to_operand_aliasing={{0}: (2, {}), {1}: (3, {})} | custom-call | flops 2516582400 | tf_op jit(solution)/shard_map/attend_next/pallas_call | solution.py:225
  25.4 0.1 collective-permute-done.8.refs_0_.refs_8_
  25.5 0.3 collective-permute-start.9
  25.8 1.2 %collective-permute-done.9.refs_1_.refs_9_ = bf16[384,256]{1,0:T(8,128)(2,1)S(1)} collective-permute-done((bf16[384,256]{1,0:T(8,128)(2,1)S(1)}, bf16[384,256]{1,0:T(8,128)(2,1)S(1)}, u32[]{:S(2)}, u32[]{:S(2)}) %collective-permute-start.9) | collective-permute-done | bytes 196640 | tf_op jit(solution)/shard_map/ppermute | solution.py:388
  26.9 2.7 %attend_last.2 = (bf16[96,1024]{1,0:T(8,128)(2,1)S(1)}, bf16[96,1024]{1,0:T(8,128)(2,1)S(1)}, bf16[96,1024]{1,0:T(8,128)(2,1)S(1)}, bf16[96,1024]{1,0:T(8,128)(2,1)S(1)}) custom-call(bf16[128,3072]{1,0:T(8,128)(2,1)S(1)} %get-tuple-element.49.queries_ref, f32[1,3072]{1,0:T(1,128)S(1)} %get-tuple-element.50.shift_ref, ...), custom_call_target="tpu_custom_call" | custom-call | tf_op jit(solution)/shard_map/attend_last/pallas_call | solution.py:318
  29.7 2.5 %collective-permute-start.10 = (bf16[96,1024]{1,0:T(8,128)(2,1)S(1)}, bf16[96,1024]{1,0:T(8,128)(2,1)S(1)}, u32[]{:S(2)}, u32[]{:S(2)}) collective-permute-start(bf16[96,1024]{1,0:T(8,128)(2,1)S(1)} %get-tuple-element.74), channel_id=1, source_target_pairs={{0,24},{8,16},{16,8},{24,0},{1,25},{9,17},{17,9},{25,1},{2,26},{10... | collective-permute-start | bytes 589832 | tf_op jit(solution)/shard_map/ppermute | solution.py:426
  32.2 0.5 %collective-permute-start.11 = (bf16[96,1024]{1,0:T(8,128)(2,1)S(1)}, bf16[96,1024]{1,0:T(8,128)(2,1)S(1)}, u32[]{:S(2)}, u32[]{:S(2)}) collective-permute-start(bf16[96,1024]{1,0:T(8,128)(2,1)S(1)} %get-tuple-element.75), channel_id=1, source_target_pairs={{0,8},{8,0},{16,24},{24,16},{1,9},{9,1},{17,25},{25,17},{2,10},{10... | collective-permute-start | bytes 589832 | tf_op jit(solution)/shard_map/ppermute | solution.py:426
  32.8 0.0 collective-permute-done.14.refs_1_.refs_7_
  32.8 0.5 collective-permute-start.12
  33.3 2.2 %attend_next.9 = (f32[1,3072]{1,0:T(1,128)S(1)}, f32[128,3072]{1,0:T(8,128)S(1)}) custom-call(bf16[128,3072]{1,0:T(8,128)(2,1)S(1)} %get-tuple-element.61.queries_ref, f32[1,3072]{1,0:T(1,128)S(1)} %get-tuple-element.62.shift_ref, f32[1,3072]{1,0:T(1,128)S(1)} %get-tuple-element.77.total_in, ...), custom_call_target="tpu_custom_call", output_to_operand_aliasing={{0}: (2, {}), {1}: (3, {})} | custom-call | tf_op jit(solution)/shard_map/attend_next/pallas_call | solution.py:225
  35.4 0.0 collective-permute-done.15.refs_0_.refs_8_
  35.4 0.0 collective-permute-done.16.refs_1_.refs_9_
  35.4 2.8 %attend_last.3 = (bf16[96,1024]{1,0:T(8,128)(2,1)S(1)}, bf16[96,1024]{1,0:T(8,128)(2,1)S(1)}, bf16[96,1024]{1,0:T(8,128)(2,1)S(1)}, bf16[96,1024]{1,0:T(8,128)(2,1)S(1)}) custom-call(bf16[128,3072]{1,0:T(8,128)(2,1)S(1)} %get-tuple-element.61.queries_ref, f32[1,3072]{1,0:T(1,128)S(1)} %get-tuple-element.62.shift_ref, ...), custom_call_target="tpu_custom_call" | custom-call | flops 2516582400 | tf_op jit(solution)/shard_map/attend_last/pallas_call | solution.py:318
  38.2 0.2 collective-permute-done.10.refs_1_
  38.4 2.5 %collective-permute-start.17 = (bf16[96,1024]{1,0:T(8,128)(2,1)S(1)}, bf16[96,1024]{1,0:T(8,128)(2,1)S(1)}, u32[]{:S(2)}, u32[]{:S(2)}) collective-permute-start(bf16[96,1024]{1,0:T(8,128)(2,1)S(1)} %get-tuple-element.84), channel_id=1, source_target_pairs={{0,24},{8,16},{16,8},{24,0},{1,25},{9,17},{17,9},{25,1},{2,26},{10... | collective-permute-start | bytes 589832 | tf_op jit(solution)/shard_map/ppermute | solution.py:426
  40.9 0.5 %collective-permute-start.18 = (bf16[96,1024]{1,0:T(8,128)(2,1)S(1)}, bf16[96,1024]{1,0:T(8,128)(2,1)S(1)}, u32[]{:S(2)}, u32[]{:S(2)}) collective-permute-start(bf16[96,1024]{1,0:T(8,128)(2,1)S(1)} %get-tuple-element.86), channel_id=1, source_target_pairs={{0,8},{8,0},{16,24},{24,16},{1,9},{9,1},{17,25},{25,17},{2,10},{10... | collective-permute-start | bytes 589832 | tf_op jit(solution)/shard_map/ppermute | solution.py:426
  41.4 0.5 collective-permute-start.19
  41.9 0.8 %collective-permute-done.11.refs_2_ = bf16[96,1024]{1,0:T(8,128)(2,1)S(1)} collective-permute-done((bf16[96,1024]{1,0:T(8,128)(2,1)S(1)}, bf16[96,1024]{1,0:T(8,128)(2,1)S(1)}, u32[]{:S(2)}, u32[]{:S(2)}) %collective-permute-start.11) | collective-permute-done | bytes 196640 | tf_op jit(solution)/shard_map/ppermute | solution.py:426
  42.7 0.0 collective-permute-done.12.refs_3_
  42.7 0.9 %place.2.refs_0_ = bf16[96,8192]{1,0:T(8,128)(2,1)} custom-call(bf16[96,1024]{1,0:T(8,128)(2,1)S(1)} %get-tuple-element.73.refs_0_, bf16[96,1024]{1,0:T(8,128)(2,1)S(1)} %collective-permute-done.10.refs_1_, bf16[96,1024]{1,0:T(8,128)(2,1)S(1)} %collective-permute-done.11.refs_2_, bf16[96,1024]{1,0:T(8,128)(2,1)S(1)} %collective-permute-done.12.refs_3_), custom_call_target="tpu_custom_call" | custom-call | tf_op jit(solution)/shard_map/place/pallas_call | solution.py:360
  43.6 3.6 %collective-permute-done.17.refs_2_ = bf16[96,1024]{1,0:T(8,128)(2,1)S(1)} collective-permute-done((bf16[96,1024]{1,0:T(8,128)(2,1)S(1)}, bf16[96,1024]{1,0:T(8,128)(2,1)S(1)}, u32[]{:S(2)}, u32[]{:S(2)}) %collective-permute-start.17) | collective-permute-done | bytes 196640 | tf_op jit(solution)/shard_map/ppermute | solution.py:426
  47.2 3.4 %collective-permute-done.18.refs_3_ = bf16[96,1024]{1,0:T(8,128)(2,1)S(1)} collective-permute-done((bf16[96,1024]{1,0:T(8,128)(2,1)S(1)}, bf16[96,1024]{1,0:T(8,128)(2,1)S(1)}, u32[]{:S(2)}, u32[]{:S(2)}) %collective-permute-start.18) | collective-permute-done | bytes 196640 | tf_op jit(solution)/shard_map/ppermute | solution.py:426
  50.6 0.0 collective-permute-done.19.refs_4_
  50.6 0.9 %place.3 = bf16[96,8192]{1,0:T(8,128)(2,1)} custom-call(bf16[96,8192]{1,0:T(8,128)(2,1)} %place.2.refs_0_, bf16[96,1024]{1,0:T(8,128)(2,1)S(1)} %get-tuple-element.82.refs_1_, bf16[96,1024]{1,0:T(8,128)(2,1)S(1)} %collective-permute-done.17.refs_2_, bf16[96,1024]{1,0:T(8,128)(2,1)S(1)} %collective-permute-done.18.refs_3_, ...), custom_call_target="tpu_custom_call", output_to_operand_aliasing={{}: (0, {})} | custom-call | tf_op jit(solution)/shard_map/place/pallas_call | solution.py:360
  (1 shorter events, 0.0 us)
Async XLA Ops:
  0.0 1.1 %copy-start = (bf16[384,256]{1,0:T(8,128)(2,1)S(1)}, bf16[384,256]{1,0:T(8,128)(2,1)}, u32[]{:S(2)}) copy-start(bf16[384,256]{1,0:T(8,128)(2,1)} %k_ref.1) | copy-start | bytes 589828
  0.0 1.1 %copy-start.1 = (bf16[384,256]{1,0:T(8,128)(2,1)S(1)}, bf16[384,256]{1,0:T(8,128)(2,1)}, u32[]{:S(2)}) copy-start(bf16[384,256]{1,0:T(8,128)(2,1)} %v_ref.1) | copy-start | bytes 589828
  0.0 0.7 %copy-start.3 = (s32[384]{0:T(512)S(1)}, s32[384]{0:T(512)}, u32[]{:S(2)}) copy-start(s32[384]{0:T(512)} %pos_ref.1) | copy-start | bytes 4612
  0.7 2.9 %copy-start.2 = (bf16[384,2048]{1,0:T(8,128)(2,1)S(1)}, bf16[384,2048]{1,0:T(8,128)(2,1)}, u32[]{:S(2)}) copy-start(bf16[384,2048]{1,0:T(8,128)(2,1)} %q_ref.1) | copy-start | bytes 4718596
  1.3 7.8 %collective-permute-start = (bf16[384,256]{1,0:T(8,128)(2,1)S(1)}, bf16[384,256]{1,0:T(8,128)(2,1)S(1)}, u32[]{:S(2)}, u32[]{:S(2)}) collective-permute-start(bf16[384,256]{1,0:T(8,128)(2,1)S(1)} %get-tuple-element.47.refs_0_.refs_2_), channel_id=1, source_target_pairs={{0,2},{1,3},{2,4},{3,5},{4,6},{5,7},{6,0},{7,1},{8,10},{9,11},{10,... | collective-permute-start | bytes 589832 | tf_op jit(solution)/shard_map/ppermute | solution.py:393
  1.4 7.8 %collective-permute-start.1 = (bf16[384,256]{1,0:T(8,128)(2,1)S(1)}, bf16[384,256]{1,0:T(8,128)(2,1)S(1)}, u32[]{:S(2)}, u32[]{:S(2)}) collective-permute-start(bf16[384,256]{1,0:T(8,128)(2,1)S(1)} %get-tuple-element.47.refs_0_.refs_2_), channel_id=1, source_target_pairs={{0,1},{1,0},{2,3},{3,2},{4,5},{5,4},{6,7},{7,6},{8,9},{9,8},{10,11... | collective-permute-start | bytes 589832 | tf_op jit(solution)/shard_map/ppermute | solution.py:388
  1.4 7.7 %collective-permute-start.2 = (bf16[400,256]{1,0:T(8,128)(2,1)S(1)}, bf16[400,256]{1,0:T(8,128)(2,1)S(1)}, u32[]{:S(2)}, u32[]{:S(2)}) collective-permute-start(bf16[400,256]{1,0:T(8,128)(2,1)S(1)} %get-tuple-element.48.refs_1_.refs_2_), channel_id=1, source_target_pairs={{0,1},{1,0},{2,3},{3,2},{4,5},{5,4},{6,7},{7,6},{8,9},{9,8},{10,11... | collective-permute-start | bytes 614408 | tf_op jit(solution)/shard_map/ppermute | solution.py:388
  1.9 10.5 %collective-permute-start.6 = (bf16[400,256]{1,0:T(8,128)(2,1)S(1)}, bf16[400,256]{1,0:T(8,128)(2,1)S(1)}, u32[]{:S(2)}, u32[]{:S(2)}) collective-permute-start(bf16[400,256]{1,0:T(8,128)(2,1)S(1)} %get-tuple-element.48.refs_1_.refs_2_), channel_id=1, source_target_pairs={{0,2},{1,3},{2,4},{3,5},{4,6},{5,7},{6,0},{7,1},{8,10},{9,11},{10,... | collective-permute-start | bytes 614408 | tf_op jit(solution)/shard_map/ppermute | solution.py:393
  9.1 3.6 %collective-permute-start.3 = (bf16[384,256]{1,0:T(8,128)(2,1)S(1)}, bf16[384,256]{1,0:T(8,128)(2,1)S(1)}, u32[]{:S(2)}, u32[]{:S(2)}) collective-permute-start(bf16[384,256]{1,0:T(8,128)(2,1)S(1)} %collective-permute-done.refs_1_.refs_4_), channel_id=1, source_target_pairs={{0,1},{1,0},{2,3},{3,2},{4,5},{5,4},{6,7},{7,6},{8,9},{9,8},{10,11... | collective-permute-start | bytes 589832 | tf_op jit(solution)/shard_map/ppermute | solution.py:388
  9.1 7.8 %collective-permute-start.4 = (bf16[384,256]{1,0:T(8,128)(2,1)S(1)}, bf16[384,256]{1,0:T(8,128)(2,1)S(1)}, u32[]{:S(2)}, u32[]{:S(2)}) collective-permute-start(bf16[384,256]{1,0:T(8,128)(2,1)S(1)} %collective-permute-done.refs_1_.refs_4_), channel_id=1, source_target_pairs={{0,1},{1,0},{2,4},{3,5},{4,6},{5,7},{6,2},{7,3},{8,9},{9,8},{10,12... | collective-permute-start | bytes 589832 | tf_op jit(solution)/shard_map/ppermute | solution.py:393
  12.4 10.7 %collective-permute-start.7 = (bf16[400,256]{1,0:T(8,128)(2,1)S(1)}, bf16[400,256]{1,0:T(8,128)(2,1)S(1)}, u32[]{:S(2)}, u32[]{:S(2)}) collective-permute-start(bf16[400,256]{1,0:T(8,128)(2,1)S(1)} %collective-permute-done.6.refs_0_.refs_4_), channel_id=1, source_target_pairs={{0,1},{1,0},{2,3},{3,2},{4,5},{5,4},{6,7},{7,6},{8,9},{9,8},{10,11... | collective-permute-start | bytes 614408 | tf_op jit(solution)/shard_map/ppermute | solution.py:388
  12.4 8.9 %collective-permute-start.13 = (bf16[400,256]{1,0:T(8,128)(2,1)S(1)}, bf16[400,256]{1,0:T(8,128)(2,1)S(1)}, u32[]{:S(2)}, u32[]{:S(2)}) collective-permute-start(bf16[400,256]{1,0:T(8,128)(2,1)S(1)} %collective-permute-done.6.refs_0_.refs_4_), channel_id=1, source_target_pairs={{0,1},{1,0},{2,4},{3,5},{4,6},{5,7},{6,2},{7,3},{8,9},{9,8},{10,12... | collective-permute-start | bytes 614408 | tf_op jit(solution)/shard_map/ppermute | solution.py:393
  16.9 1.4 %collective-permute-start.5 = (bf16[384,256]{1,0:T(8,128)(2,1)S(1)}, bf16[384,256]{1,0:T(8,128)(2,1)S(1)}, u32[]{:S(2)}, u32[]{:S(2)}) collective-permute-start(bf16[384,256]{1,0:T(8,128)(2,1)S(1)} %collective-permute-done.4.refs_0_.refs_6_), channel_id=1, source_target_pairs={{0,1},{1,0},{2,3},{3,2},{4,5},{5,4},{6,7},{7,6},{8,9},{9,8},{10,11... | collective-permute-start | bytes 589832 | tf_op jit(solution)/shard_map/ppermute | solution.py:388
  16.9 8.6 %collective-permute-start.8 = (bf16[384,256]{1,0:T(8,128)(2,1)S(1)}, bf16[384,256]{1,0:T(8,128)(2,1)S(1)}, u32[]{:S(2)}, u32[]{:S(2)}) collective-permute-start(bf16[384,256]{1,0:T(8,128)(2,1)S(1)} %collective-permute-done.4.refs_0_.refs_6_), channel_id=1, source_target_pairs={{0,1},{1,0},{2,3},{3,2},{4,6},{5,7},{6,4},{7,5},{8,9},{9,8},{10,11... | collective-permute-start | bytes 589832 | tf_op jit(solution)/shard_map/ppermute | solution.py:393
  21.3 11.5 %collective-permute-start.14 = (bf16[400,256]{1,0:T(8,128)(2,1)S(1)}, bf16[400,256]{1,0:T(8,128)(2,1)S(1)}, u32[]{:S(2)}, u32[]{:S(2)}) collective-permute-start(bf16[400,256]{1,0:T(8,128)(2,1)S(1)} %collective-permute-done.13.refs_0_.refs_6_), channel_id=1, source_target_pairs={{0,1},{1,0},{2,3},{3,2},{4,5},{5,4},{6,7},{7,6},{8,9},{9,8},{10,11... | collective-permute-start | bytes 614408 | tf_op jit(solution)/shard_map/ppermute | solution.py:388
  21.3 14.1 %collective-permute-start.15 = (bf16[400,256]{1,0:T(8,128)(2,1)S(1)}, bf16[400,256]{1,0:T(8,128)(2,1)S(1)}, u32[]{:S(2)}, u32[]{:S(2)}) collective-permute-start(bf16[400,256]{1,0:T(8,128)(2,1)S(1)} %collective-permute-done.13.refs_0_.refs_6_), channel_id=1, source_target_pairs={{0,1},{1,0},{2,3},{3,2},{4,6},{5,7},{6,4},{7,5},{8,9},{9,8},{10,11... | collective-permute-start | bytes 614408 | tf_op jit(solution)/shard_map/ppermute | solution.py:393
  22.0 13.4 %collective-permute-start.16 = (bf16[400,256]{1,0:T(8,128)(2,1)S(1)}, bf16[400,256]{1,0:T(8,128)(2,1)S(1)}, u32[]{:S(2)}, u32[]{:S(2)}) collective-permute-start(bf16[400,256]{1,0:T(8,128)(2,1)S(1)} %collective-permute-done.13.refs_0_.refs_6_), channel_id=1, source_target_pairs={{0,1},{1,0},{2,3},{3,2},{4,7},{5,6},{6,5},{7,4},{8,9},{9,8},{10,11... | collective-permute-start | bytes 614408 | tf_op jit(solution)/shard_map/ppermute | solution.py:393
  25.5 1.4 %collective-permute-start.9 = (bf16[384,256]{1,0:T(8,128)(2,1)S(1)}, bf16[384,256]{1,0:T(8,128)(2,1)S(1)}, u32[]{:S(2)}, u32[]{:S(2)}) collective-permute-start(bf16[384,256]{1,0:T(8,128)(2,1)S(1)} %collective-permute-done.8.refs_0_.refs_8_), channel_id=1, source_target_pairs={{0,1},{1,0},{2,3},{3,2},{4,5},{5,4},{6,7},{7,6},{8,9},{9,8},{10,11... | collective-permute-start | bytes 589832 | tf_op jit(solution)/shard_map/ppermute | solution.py:388
  29.7 8.7 %collective-permute-start.10 = (bf16[96,1024]{1,0:T(8,128)(2,1)S(1)}, bf16[96,1024]{1,0:T(8,128)(2,1)S(1)}, u32[]{:S(2)}, u32[]{:S(2)}) collective-permute-start(bf16[96,1024]{1,0:T(8,128)(2,1)S(1)} %get-tuple-element.74), channel_id=1, source_target_pairs={{0,24},{8,16},{16,8},{24,0},{1,25},{9,17},{17,9},{25,1},{2,26},{10... | collective-permute-start | bytes 589832 | tf_op jit(solution)/shard_map/ppermute | solution.py:426
  32.2 10.5 %collective-permute-start.11 = (bf16[96,1024]{1,0:T(8,128)(2,1)S(1)}, bf16[96,1024]{1,0:T(8,128)(2,1)S(1)}, u32[]{:S(2)}, u32[]{:S(2)}) collective-permute-start(bf16[96,1024]{1,0:T(8,128)(2,1)S(1)} %get-tuple-element.75), channel_id=1, source_target_pairs={{0,8},{8,0},{16,24},{24,16},{1,9},{9,1},{17,25},{25,17},{2,10},{10... | collective-permute-start | bytes 589832 | tf_op jit(solution)/shard_map/ppermute | solution.py:426
  32.8 10.0 %collective-permute-start.12 = (bf16[96,1024]{1,0:T(8,128)(2,1)S(1)}, bf16[96,1024]{1,0:T(8,128)(2,1)S(1)}, u32[]{:S(2)}, u32[]{:S(2)}) collective-permute-start(bf16[96,1024]{1,0:T(8,128)(2,1)S(1)} %get-tuple-element.76), channel_id=1, source_target_pairs={{0,16},{8,24},{16,0},{24,8},{1,17},{9,25},{17,1},{25,9},{2,18},{10... | collective-permute-start | bytes 589832 | tf_op jit(solution)/shard_map/ppermute | solution.py:426
  38.4 8.8 %collective-permute-start.17 = (bf16[96,1024]{1,0:T(8,128)(2,1)S(1)}, bf16[96,1024]{1,0:T(8,128)(2,1)S(1)}, u32[]{:S(2)}, u32[]{:S(2)}) collective-permute-start(bf16[96,1024]{1,0:T(8,128)(2,1)S(1)} %get-tuple-element.84), channel_id=1, source_target_pairs={{0,24},{8,16},{16,8},{24,0},{1,25},{9,17},{17,9},{25,1},{2,26},{10... | collective-permute-start | bytes 589832 | tf_op jit(solution)/shard_map/ppermute | solution.py:426
  40.9 9.7 %collective-permute-start.18 = (bf16[96,1024]{1,0:T(8,128)(2,1)S(1)}, bf16[96,1024]{1,0:T(8,128)(2,1)S(1)}, u32[]{:S(2)}, u32[]{:S(2)}) collective-permute-start(bf16[96,1024]{1,0:T(8,128)(2,1)S(1)} %get-tuple-element.86), channel_id=1, source_target_pairs={{0,8},{8,0},{16,24},{24,16},{1,9},{9,1},{17,25},{25,17},{2,10},{10... | collective-permute-start | bytes 589832 | tf_op jit(solution)/shard_map/ppermute | solution.py:426
  41.4 9.2 %collective-permute-start.19 = (bf16[96,1024]{1,0:T(8,128)(2,1)S(1)}, bf16[96,1024]{1,0:T(8,128)(2,1)S(1)}, u32[]{:S(2)}, u32[]{:S(2)}) collective-permute-start(bf16[96,1024]{1,0:T(8,128)(2,1)S(1)} %get-tuple-element.88), channel_id=1, source_target_pairs={{0,16},{8,24},{16,0},{24,8},{1,17},{9,25},{17,1},{25,9},{2,18},{10... | collective-permute-start | bytes 589832 | tf_op jit(solution)/shard_map/ppermute | solution.py:426
